TPU v7x, 32 devices: a whole 2x2x4 slice. The times are simulated.
32 devices in a mesh: seq: 16 (over z, y, x), head: 2 (over core).
Axes of the slice: x: 2, y: 2, z: 4, core: 2. Of those that a mesh axis runs over, the one named last changes fastest.
Arguments:
- queries: bfloat16 [12288, 1024], P('seq', 'head'), may hold values from -12 to 12
- keys: bfloat16 [12288, 1024], P('seq', 'head'), may hold values from -6 to 6
- values: bfloat16 [12288, 1024], P('seq', 'head'), may hold values from -6 to 6
- rates: float32 [12288, 2], P('seq', 'head'), may hold values from 0.02 to 1
- w_gate: bfloat16 [1024, 512], P('head'), may hold values from -0.25 to 0.25
- w_up: bfloat16 [1024, 512], P('head'), may hold values from -0.25 to 0.25
- w_down: bfloat16 [1024, 512], P('head'), may hold values from -0.25 to 0.25
- out_gain: float32 [1024], P('head'), may hold values from 0.1 to 1.9
Outputs:
- output: bfloat16 [12288, 1024], P('seq', 'head')
- next_gate: bfloat16 [1024, 512], P(('head', 'seq'))
- next_up: bfloat16 [1024, 512], P(('head', 'seq'))
- next_down: bfloat16 [1024, 512], P(('head', 'seq'))
All inputs are finite; a program needn't handle non-finite values.
Results may differ from a plain program's by a relative error of at most 0.0077.
Values may be sent and summed in bfloat16 or wider, within the bound.
No kernel may reach another device: no remote copies, remote signals or barrier semaphores. Data moves between devices by JAX's collectives and lax.ppermute only.
A program may use at most 64 MiB of HBM per device.

v0:
```python
import jax
import jax.numpy as jnp
from jax import lax
from jax.sharding import PartitionSpec as P

ATT_DIM = 128
WINDOW = 512


ETA_STEP = 0.5
EPSILON = 1e-06


def from_behind(x, axis, by):
    peers = lax.axis_size(axis)
    pairs = [(i, i + by) for i in range(peers) if 0 <= i + by < peers]
    return lax.ppermute(x, axis, pairs)


def silu_pair(gate_pre):
    sigmoid_val = jax.nn.sigmoid(gate_pre)
    return (gate_pre * sigmoid_val, sigmoid_val * (1.0 + gate_pre * (1.0 - sigmoid_val)))


def inner_rows(left_op, right_op):
    return lax.dot_general(
        left_op, right_op, (((0,), (0,)), ((), ())), preferred_element_type=jnp.float32
    )


def outer_cols(left_op, right_op):
    return lax.dot_general(
        left_op, right_op, (((1,), (1,)), ((), ())), preferred_element_type=jnp.float32
    )


def window_attend(query_block, key_window, value_window, query_pos, key_pos):
    allowed = (
        (key_pos[None, :] <= query_pos[:, None])
        & (query_pos[:, None] - key_pos[None, :] < WINDOW)
        & (key_pos[None, :] >= 0)
    )
    counts = jnp.minimum(query_pos + 1, WINDOW).astype(jnp.float32)
    pieces = []
    for head_pos in range(query_block.shape[1] // ATT_DIM):
        col_low = head_pos * ATT_DIM
        query_head = query_block[:, col_low : col_low + ATT_DIM]
        key_head = key_window[:, col_low : col_low + ATT_DIM]
        value_head = value_window[:, col_low : col_low + ATT_DIM]
        scores = outer_cols(query_head, key_head) * ATT_DIM ** (-0.5)
        weights = jnp.where(allowed, jnp.square(jnp.maximum(scores, 0.0)), 0.0).astype(jnp.bfloat16)
        pieces.append(jnp.dot(weights, value_head, preferred_element_type=jnp.float32))
    return jnp.concatenate(pieces, axis=1) / counts[:, None]


def local_grads(key_rows, value_rows, rate_col, gate_w, up_w, down_w):
    gate_pre = jnp.dot(key_rows, gate_w, preferred_element_type=jnp.float32)
    up_pre = jnp.dot(key_rows, up_w, preferred_element_type=jnp.float32)
    activated, derivative = silu_pair(gate_pre)
    hidden = (activated * up_pre).astype(jnp.bfloat16)
    target = (rate_col * value_rows.astype(jnp.float32)).astype(jnp.bfloat16)
    grad_down = inner_rows(hidden, target)
    backward = outer_cols(target, down_w)
    grad_gate = inner_rows(key_rows, (backward * up_pre * derivative).astype(jnp.bfloat16))
    grad_up = inner_rows(key_rows, (backward * activated).astype(jnp.bfloat16))
    return (grad_gate, grad_up, grad_down)


def step_weight(weight_part, gradient, square_sum, count_all, weight_full):
    full_float = weight_full.astype(jnp.float32)
    weight_rms = jnp.sqrt(jnp.mean(jnp.square(full_float)))
    grad_rms = jnp.sqrt(square_sum / count_all + EPSILON)
    return (weight_part.astype(jnp.float32) + ETA_STEP * weight_rms * gradient / grad_rms).astype(
        jnp.bfloat16
    )


def apply_fast(query_rows, gate_w, up_w, down_w):
    gate_pre = jnp.dot(query_rows, gate_w, preferred_element_type=jnp.float32)
    up_pre = jnp.dot(query_rows, up_w, preferred_element_type=jnp.float32)
    activated, derivative = silu_pair(gate_pre)
    hidden = (activated * up_pre).astype(jnp.bfloat16)
    return jnp.dot(hidden, down_w, preferred_element_type=jnp.float32)


def body(queries, keys, values, rates, w_gate, w_up, w_down, out_gain):
    tok_rows = queries.shape[0]
    seq_index = lax.axis_index("seq")
    seq_count = lax.axis_size("seq")
    reach_count = (WINDOW + tok_rows - 1) // tok_rows
    key_value = jnp.stack([keys, values])
    earlier = []
    tail_rows = WINDOW - (reach_count - 1) * tok_rows
    piece = key_value[:, tok_rows - tail_rows :]
    earlier.insert(0, from_behind(piece, "seq", 1))
    lead_rows = WINDOW
    window = jnp.concatenate(earlier + [key_value], axis=1)
    first_row = seq_index * tok_rows
    query_pos = first_row + jnp.arange(tok_rows, dtype=jnp.int32)
    key_pos = first_row - lead_rows + jnp.arange(lead_rows + tok_rows, dtype=jnp.int32)
    attended = window_attend(queries, window[0], window[1], query_pos, key_pos)
    gate_rows = w_gate.shape[0] // seq_count
    down_rows = w_down.shape[0] // seq_count
    grad_gate, grad_up, grad_down = local_grads(keys, values, rates, w_gate, w_up, w_down)
    total_gate, total_up, total_down = lax.psum((grad_gate, grad_up, grad_down), "seq")
    next_gate = step_weight(
        w_gate, total_gate, jnp.sum(jnp.square(total_gate)), w_gate.size, w_gate
    )
    next_up = step_weight(w_up, total_up, jnp.sum(jnp.square(total_up)), w_up.size, w_up)
    next_down = step_weight(
        w_down, total_down, jnp.sum(jnp.square(total_down)), w_down.size, w_down
    )
    part_gate = lax.dynamic_slice_in_dim(next_gate, seq_index * gate_rows, gate_rows, 0)
    part_up = lax.dynamic_slice_in_dim(next_up, seq_index * gate_rows, gate_rows, 0)
    part_down = lax.dynamic_slice_in_dim(next_down, seq_index * down_rows, down_rows, 0)
    applied = apply_fast(queries, next_gate, next_up, next_down)
    combined = attended + applied
    token_sums = lax.psum(jnp.sum(jnp.square(combined), axis=1), "head")
    full_width = combined.shape[1] * lax.axis_size("head")
    output = (
        combined * lax.rsqrt(token_sums[:, None] / full_width + EPSILON) * out_gain[None, :]
    ).astype(jnp.bfloat16)
    return (output, part_gate, part_up, part_down)


def solution(mesh):
    placed = (
        P("seq", "head"),
        P("seq", "head"),
        P("seq", "head"),
        P("seq", "head"),
        P("head", None),
        P("head", None),
        P("head", None),
        P("head"),
    )
    return jax.shard_map(
        body,
        mesh=mesh,
        in_specs=placed,
        out_specs=(
            P("seq", "head"),
            P(("head", "seq"), None),
            P(("head", "seq"), None),
            P(("head", "seq"), None),
        ),
        check_vma=False,
    )
```

profile of v0, /device:TPU:17, one launch (start us, length us, event | category | flops | bytes accessed | tf_op | source)
XLA Modules:
  0.0 205.0 jit_solution(8093586286909757668)
XLA Ops:
  7.2 2.4 %pad_maximum_fusion = bf16[2,512,512]{2,1,0:T(8,128)(2,1)} fusion(bf16[1,768,512]{2,1,0:T(8,128)(2,1)} %bitcast.73, bf16[1,768,512]{2,1,0:T(8,128)(2,1)} %bitcast.71), kind=kLoop, calls=%fused_computation.61 | loop fusion | flops 2097152 | bytes 2621440 | tf_op jit(solution)/shard_map/stack | solution.py:91
  9.6 3.2 %collective-permute-start = (bf16[2,512,512]{2,1,0:T(8,128)(2,1)}, bf16[2,512,512]{2,1,0:T(8,128)(2,1)}, u32[]{:S(2)}, u32[]{:S(2)}) collective-permute-start(bf16[2,512,512]{2,1,0:T(8,128)(2,1)} %pad_maximum_fusion), channel_id=1, source_target_pairs={{0,2},{2,4},{4,6},{6,8},{8,10},{10,12},{12,14},{14,16},{16,18},{18... | collective-permute-start | bytes 3145736 | tf_op jit(solution)/shard_map/ppermute | solution.py:17
  12.9 1.7 fusion.70
  14.6 1.7 fusion.71
  16.4 0.6 fusion.43
  17.0 0.8 copy-done.8
  17.8 3.4 %fusion.30 = f32[512,512]{1,0:T(8,128)} fusion(f32[768,512]{1,0:T(8,128)} %fusion.70, bf16[768,512]{1,0:T(8,128)(2,1)S(1)} %copy-done.1, f32[768]{0:T(1024)S(1)} %reduce, f32[768,512]{1,0:T(8,128)S(1)} %copy-done.8), kind=kOutput, calls=%fused_computation.65 | convolution fusion | flops 406192128 | bytes 4983808 | tf_op jit(solution)/shard_map/dot_general | solution.py:26
  21.2 2.0 convolution_bitcast_fusion.1
  23.3 1.7 convolution_bitcast_fusion
  25.2 0.9 fusion.28
  26.1 0.9 fusion.24
  26.9 1.3 copy.14
  29.6 0.9 fusion.26
  31.2 13.2 %collective-permute-done = bf16[2,512,512]{2,1,0:T(8,128)(2,1)} collective-permute-done((bf16[2,512,512]{2,1,0:T(8,128)(2,1)}, bf16[2,512,512]{2,1,0:T(8,128)(2,1)}, u32[]{:S(2)}, u32[]{:S(2)}) %collective-permute-start) | collective-permute-done | bytes 1048608 | tf_op jit(solution)/shard_map/ppermute | solution.py:17
  44.3 1.4 maximum_maximum_fusion
  45.7 1.3 slice_bitcast_fusion.1
  47.1 3.5 %fusion.23 = f32[768,128]{0,1:T(8,128)} fusion(bf16[1280,512]{1,0:T(8,128)(2,1)} %get-tuple-element.12, bf16[1280,512]{1,0:T(8,128)(2,1)S(1)} %get-tuple-element.11, bf16[768,512]{1,0:T(8,128)(2,1)} %param.8, s32[1280]{0:T(1024)S(1)} %iota_add_fusion, s32[768]{0:T(1024)S(1)} %get-tuple-element.18, pred[1280]{0:T(1024)(128)(4,1)S(1)} %broadcast_compare_fusion), kind=kOutput, calls=%fused_computation.46 | convolution fusion | flops 513146880 | bytes 1259520 | tf_op jit(solution)/shard_map/dot_general | solution.py:52
  50.6 3.5 %fusion.22 = f32[768,128]{0,1:T(8,128)} fusion(bf16[1280,512]{1,0:T(8,128)(2,1)} %get-tuple-element.12, bf16[1280,512]{1,0:T(8,128)(2,1)S(1)} %get-tuple-element.11, bf16[768,512]{1,0:T(8,128)(2,1)} %param.8, s32[1280]{0:T(1024)S(1)} %iota_add_fusion, s32[768]{0:T(1024)S(1)} %get-tuple-element.18, pred[1280]{0:T(1024)(128)(4,1)S(1)} %broadcast_compare_fusion), kind=kOutput, calls=%fused_computation.45 | convolution fusion | flops 513146880 | bytes 1259520 | tf_op jit(solution)/shard_map/dot_general | solution.py:52
  54.1 3.5 %fusion.21 = f32[768,128]{0,1:T(8,128)} fusion(bf16[1280,512]{1,0:T(8,128)(2,1)} %get-tuple-element.12, bf16[1280,512]{1,0:T(8,128)(2,1)S(1)} %get-tuple-element.11, bf16[768,512]{1,0:T(8,128)(2,1)} %param.8, s32[1280]{0:T(1024)S(1)} %iota_add_fusion, s32[768]{0:T(1024)S(1)} %get-tuple-element.18, pred[1280]{0:T(1024)(128)(4,1)S(1)} %broadcast_compare_fusion), kind=kOutput, calls=%fused_computation.44 | convolution fusion | flops 513146880 | bytes 1259520 | tf_op jit(solution)/shard_map/dot_general | solution.py:52
  57.6 3.5 %fusion.20 = f32[768,128]{0,1:T(8,128)} fusion(bf16[1280,512]{1,0:T(8,128)(2,1)} %get-tuple-element.12, bf16[1280,512]{1,0:T(8,128)(2,1)S(1)} %get-tuple-element.11, bf16[768,512]{1,0:T(8,128)(2,1)} %param.8, s32[1280]{0:T(1024)S(1)} %iota_add_fusion, s32[768]{0:T(1024)S(1)} %get-tuple-element.18, pred[1280]{0:T(1024)(128)(4,1)S(1)} %broadcast_compare_fusion), kind=kOutput, calls=%fused_computation.43 | convolution fusion | flops 513146880 | bytes 1259520 | tf_op jit(solution)/shard_map/dot_general | solution.py:52
  61.1 115.9 %all-reduce.3.cloned.1.call-done = (f32[512,512]{1,0:T(8,128)}, f32[512,512]{0,1:T(8,128)}, f32[512,512]{0,1:T(8,128)}) async-done(((f32[512,512]{1,0:T(8,128)}, f32[512,512]{0,1:T(8,128)}, f32[512,512]{0,1:T(8,128)}), (f32[512,512]{1,0:T(8,128)}, f32[512,512]{0,1:T(8,128)}, f32[512,512]{0,1:T(8,128)})) %all-reduce.3.cloned.1.call-update) | async-done | bytes 3145744 | tf_op jit(solution)/shard_map/psum | solution.py:105
  177.1 2.2 %multiply_reduce_fusion.1 = f32[]{:T(128)} fusion(f32[512,512]{1,0:T(8,128)} %get-tuple-element.8), kind=kLoop, calls=%fused_computation.62 | loop fusion | flops 524287 | bytes 1048580 | tf_op jit(solution)/shard_map/reduce_sum | solution.py:111
  179.9 0.9 multiply_reduce_fusion.3
  181.5 2.1 %multiply_reduce_fusion.2 = f32[]{:T(128)} fusion(f32[512,512]{0,1:T(8,128)} %get-tuple-element.10), kind=kLoop, calls=%fused_computation.63 | loop fusion | flops 524287 | bytes 1048580 | tf_op jit(solution)/shard_map/reduce_sum | solution.py:109
  184.3 1.8 fusion.25
  186.2 1.8 fusion.72
  188.4 0.6 constant_dynamic-slice_fusion
  189.7 3.0 %multiply_reduce_fusion = (f32[768]{0:T(1024)S(1)}, f32[768,512]{0,1:T(8,128)S(1)}) fusion(bf16[512,512]{1,0:T(8,128)(2,1)} %copy-done.12, f32[512,768]{0,1:T(8,128)S(1)} %copy-done.7, bf16[512,512]{0,1:T(8,128)(2,1)} %copy-done.10, bf16[768,512]{1,0:T(8,128)(2,1)} %param.8, f32[768]{0:T(1024)S(1)} %get-tuple-element.17, f32[768,128]{0,1:T(8,128)} %fusion.23, ...), kind=kOutput, calls=%fused_computation.34 | convolution fusion | flops 810417408 | bytes 6559744 | tf_op jit(solution)/shard_map/dot_general | solution.py:83
  192.7 2.8 %psum.31 = f32[768]{0:T(1024)S(1)} all-reduce(f32[768]{0:T(1024)S(1)} %get-tuple-element.13), channel_id=1, replica_groups=mesh['seq'=16,'head'=2] {'head'}, use_global_device_ids=true, to_apply=%region_10.11 | all-reduce | flops 768 | bytes 6144 | tf_op jit(solution)/shard_map/psum | solution.py:118
  195.6 1.2 copy.15
  196.8 0.7 copy.16
  197.5 0.7 copy.17
  (41 shorter events, 1.6 us)
Async XLA Ops:
  7.2 5.7 %copy-start = (bf16[768,512]{1,0:T(8,128)(2,1)S(1)}, bf16[768,512]{1,0:T(8,128)(2,1)}, u32[]{:S(2)}) copy-start(bf16[768,512]{1,0:T(8,128)(2,1)} %param.9) | copy-start | bytes 2359300
  7.2 5.7 %copy-start.6 = (bf16[512,512]{1,0:T(8,128)(2,1)S(1)}, bf16[512,512]{1,0:T(8,128)(2,1)}, u32[]{:S(2)}) copy-start(bf16[512,512]{1,0:T(8,128)(2,1)} %param.13) | copy-start | bytes 1572868
  7.2 169.9 %all-reduce.3.cloned.1.call-start = ((), (), s32[]{:S(2)}) async-start(), calls=%async_computation | async-start | bytes 6291456 | tf_op jit(solution)/shard_map/psum | solution.py:105
  9.6 5.0 %copy-start.5 = (bf16[512,512]{1,0:T(8,128)(2,1)S(1)}, bf16[512,512]{1,0:T(8,128)(2,1)}, u32[]{:S(2)}) copy-start(bf16[512,512]{1,0:T(8,128)(2,1)} %param.12) | copy-start | bytes 1572868
  9.6 34.7 %collective-permute-start = (bf16[2,512,512]{2,1,0:T(8,128)(2,1)}, bf16[2,512,512]{2,1,0:T(8,128)(2,1)}, u32[]{:S(2)}, u32[]{:S(2)}) collective-permute-start(bf16[2,512,512]{2,1,0:T(8,128)(2,1)} %pad_maximum_fusion), channel_id=1, source_target_pairs={{0,2},{2,4},{4,6},{6,8},{8,10},{10,12},{12,14},{14,16},{16,18},{18... | collective-permute-start | bytes 3145736 | tf_op jit(solution)/shard_map/ppermute | solution.py:17
  14.6 1.7 copy-start.13
  14.6 1.7 copy-start.1
  14.6 1.8 copy-start.2
  16.4 1.4 copy-start.8
  17.8 3.4 %copy-start.9 = (f32[768,512]{1,0:T(8,128)S(1)}, f32[768,512]{1,0:T(8,128)}, u32[]{:S(2)}) copy-start(f32[768,512]{1,0:T(8,128)} %fusion.70) | copy-start | bytes 4718596
  177.1 2.9 %copy-start.4 = (f32[512,512]{0,1:T(8,128)S(1)}, f32[512,512]{0,1:T(8,128)}, u32[]{:S(2)}) copy-start(f32[512,512]{0,1:T(8,128)} %get-tuple-element.9) | copy-start | bytes 3145732
  184.3 1.9 copy-start.11
  186.2 1.9 copy-start.10
  186.2 2.0 copy-start.3
  188.1 1.6 copy-start.7
  188.4 0.8 copy-start.12
  189.7 5.8 %copy-start.14 = (f32[512]{0:T(512)S(1)}, f32[512]{0:T(512)}, u32[]{:S(2)}) copy-start(f32[512]{0:T(512)} %param.15) | copy-start | bytes 6148
Sparse Core Ops, SparseCore 0:
  25.1 151.9 all-reduce.2
where the time goes:
time: 208 us; the launch traced here: 205 us
  waiting for transfers between devices  129 us (62%)
  matrix products  30 us (14%)
  between operations  18.4 us (9%)
  other arithmetic  13.8 us (7%)
  local copies, waits for them, and re-layouts  7.67 us (4%)
  starting transfers between devices  3.28 us (2%)
  blocking collectives  2.78 us (1%)
    psum x1, waiting for transfers between devices, body(): lax.psum((grad_gate, grad_up, grad_down), 'seq')  116 us
    dot_general x4, matrix products, window_attend(): jnp.dot(weights, value_head, preferred_element_type=jnp.float32)  14 us
    ppermute x1, waiting for transfers between devices, from_behind(): return lax.ppermute(x, axis, pairs)  13.2 us
    dot_general x3, matrix products, inner_rows(): lax.dot_general(left_op, right_op, (((0,), (0,)), ((), ())), preferred_el...  7.18 us
    unnamed x35, local copies, waits for them, and re-layouts  5.5 us
  transfers between devices with their start and end apart: 2, of which 2 were waited for; matrix products, arithmetic and copies ran while one was open for 16% of the time, Pallas kernels for 0%

commit v1 on v0

v1 whole, which is shorter than its diff:
```python
import functools

import jax
import jax.numpy as jnp
from jax import lax
from jax.experimental import pallas as pl
from jax.experimental.pallas import tpu as pltpu
from jax.sharding import PartitionSpec as P

ATT_DIM = 128
WINDOW = 512
BLOCK = 256
SUBROWS = 16
CHUNKS = 2


ETA_STEP = 0.5
EPSILON = 1e-06

F32 = jnp.float32
BF16 = jnp.bfloat16
VMEM_LIMIT = 50 * 1024 * 1024


def inner_rows(left_op, right_op):
    return lax.dot_general(
        left_op, right_op, (((0,), (0,)), ((), ())), preferred_element_type=F32
    )


def outer_cols(left_op, right_op):
    return lax.dot_general(
        left_op, right_op, (((1,), (1,)), ((), ())), preferred_element_type=F32
    )


def dot(left_op, right_op):
    return jnp.dot(left_op, right_op, preferred_element_type=F32)


def kernel_call(body, name, out_shape, flops, moved):
    return pl.pallas_call(
        body,
        out_shape=out_shape,
        name=name,
        compiler_params=pltpu.CompilerParams(vmem_limit_bytes=VMEM_LIMIT),
        cost_estimate=pl.CostEstimate(flops=flops, bytes_accessed=moved, transcendentals=0),
    )


def halving_masks(peers, rows):
    bits = []
    while peers % (2 << len(bits)) == 0 and peers > 1 << len(bits):
        bits.append(1 << len(bits))
    pairs = [(b, b) for b in bits]
    if len(bits) >= 3:
        pairs = [(bits[0], bits[1]), (bits[2], bits[2]), (bits[1], bits[0])]
        pairs += [(b, b) for b in bits[3:]]
    steps = []
    while pairs and rows % (2 * SUBROWS) == 0:
        steps.append(pairs.pop(0))
        rows //= 2
    return steps


def mask_here(masks):
    return jnp.where(lax.axis_index("head") % 2 == 0, masks[0], masks[1])


def bit_here(masks):
    return ((lax.axis_index("seq") & mask_here(masks)) != 0).astype(jnp.int32)


def swap(x, masks):
    peers, heads = lax.axis_size("seq"), lax.axis_size("head")
    pairs = [
        (s * heads + h, (s ^ masks[h % 2]) * heads + h)
        for s in range(peers)
        for h in range(heads)
    ]
    return lax.ppermute(x, ("seq", "head"), pairs)


def grads_kernel(k_ref, v_ref, rate_ref, gate_ref, up_ref, down_ref, out_ref):
    rows = k_ref.shape[0]
    key_rows = k_ref[...]
    gate_pre = dot(key_rows, gate_ref[...])
    up_pre = dot(key_rows, up_ref[...])
    sigmoid_val = jax.nn.sigmoid(gate_pre)
    activated = gate_pre * sigmoid_val
    hidden = (activated * up_pre).astype(BF16)
    rate_col = jnp.transpose(jnp.broadcast_to(rate_ref[...], (8, rows)))[:, :1]
    target = (rate_col * v_ref[...].astype(F32)).astype(BF16)
    out_ref[2] = inner_rows(hidden, target)
    backward = outer_cols(target, down_ref[...])
    out_ref[1] = inner_rows(key_rows, (backward * activated).astype(BF16))
    derivative = sigmoid_val * (1.0 + gate_pre * (1.0 - sigmoid_val))
    out_ref[0] = inner_rows(key_rows, (backward * up_pre * derivative).astype(BF16))


def attend_kernel(q_ref, k_ref, v_ref, prev_ref, gate_ref, up_ref, down_ref, out_ref, square_ref):
    rows = q_ref.shape[0]
    reach = WINDOW // BLOCK
    row_at = lax.broadcasted_iota(jnp.int32, (BLOCK, BLOCK), 0)
    col_at = lax.broadcasted_iota(jnp.int32, (BLOCK, BLOCK), 1)
    first = lax.axis_index("seq") * rows
    for block in range(rows // BLOCK):
        here = slice(block * BLOCK, (block + 1) * BLOCK)
        position = first + block * BLOCK + lax.broadcasted_iota(jnp.int32, (BLOCK, 1), 0)
        counts = jnp.minimum(position + 1, WINDOW).astype(F32)
        scale = 1.0 / (counts * ATT_DIM)
        for col in range(0, q_ref.shape[1], ATT_DIM):
            cols = slice(col, col + ATT_DIM)
            query = q_ref[here, cols]
            total = None
            for other in range(block - reach, block + 1):
                if other < 0:
                    there = slice((other + reach) * BLOCK, (other + reach + 1) * BLOCK)
                    key, value = prev_ref[0, there, cols], prev_ref[1, there, cols]
                else:
                    there = slice(other * BLOCK, (other + 1) * BLOCK)
                    key, value = k_ref[there, cols], v_ref[there, cols]
                score = jnp.maximum(outer_cols(query, key), 0.0)
                weight = score * score
                if other == block:
                    weight = jnp.where(col_at <= row_at, weight, 0.0)
                if other == block - reach:
                    weight = jnp.where(col_at > row_at, weight, 0.0)
                part = dot(weight.astype(BF16), value)
                total = part if total is None else total + part
            out_ref[here, cols] = total * scale
    for at, ref in enumerate((gate_ref, up_ref, down_ref)):
        whole = jnp.square(ref[...].astype(F32))
        square_ref[at] = jnp.sum(whole.reshape(-1, 8, whole.shape[1]), axis=0)


def apply_kernel(steps, part_rows, *refs):
    count = 2 * CHUNKS if steps else CHUNKS
    pieces, refs = refs[:count], refs[count:]
    q_ref, gate_ref, up_ref, down_ref, square_ref, attended_ref = refs[:6]
    combined_ref, sums_ref, next_gate_ref, next_up_ref, next_down_ref = refs[6:11]
    next_refs = refs[11:]
    bits = [bit_here(m) for m in steps]
    seq_index = lax.axis_index("seq")
    for at, (old_ref, new_ref) in enumerate(zip((gate_ref, up_ref, down_ref), next_refs)):
        size = old_ref.shape[0] * old_ref.shape[1]
        chunk_rows = old_ref.shape[0] // CHUNKS
        total = None
        for piece in pieces:
            part = jnp.square(piece[at].astype(F32))
            part = jnp.sum(part.reshape(-1, 8, part.shape[1]), axis=0)
            total = part if total is None else total + part
        grad_rms = jnp.sqrt(jnp.sum(total, keepdims=True) / size + EPSILON)
        weight_rms = jnp.sqrt(jnp.sum(square_ref[at], keepdims=True) / size)
        factor = ETA_STEP * weight_rms / grad_rms
        if not steps:
            for chunk, piece in enumerate(pieces):
                here = slice(chunk * chunk_rows, (chunk + 1) * chunk_rows)
                new_ref[here] = (old_ref[here].astype(F32) + factor * piece[at].astype(F32)).astype(BF16)
            continue
        unit = chunk_rows >> len(steps)
        for chunk in range(CHUNKS):
            for arrived in range(2):
                piece = pieces[2 * chunk + arrived]
                for block in range(piece.shape[1] // unit):
                    start = chunk * chunk_rows
                    for p, bit in enumerate(bits):
                        came = arrived if p == 0 else (block >> (len(steps) - 1 - p)) & 1
                        start = start + (bit ^ came) * (chunk_rows >> (p + 1))
                    there = pl.ds(pl.multiple_of(start, unit), unit)
                    grad = piece[at, block * unit : (block + 1) * unit].astype(F32)
                    new_ref[there] = (old_ref[there].astype(F32) + factor * grad).astype(BF16)
    for new_ref, part_ref in zip(next_refs, (next_gate_ref, next_up_ref, next_down_ref)):
        kept = part_ref.shape[0]
        start = (seq_index * part_rows) // kept * kept
        part_ref[...] = new_ref[pl.ds(pl.multiple_of(start, kept), kept)]
    ones = jnp.ones((8, attended_ref.shape[1]), BF16)
    for block in range(q_ref.shape[0] // BLOCK):
        here = slice(block * BLOCK, (block + 1) * BLOCK)
        query = q_ref[here]
        gate_pre = dot(query, next_refs[0][...])
        up_pre = dot(query, next_refs[1][...])
        hidden = (gate_pre * jax.nn.sigmoid(gate_pre) * up_pre).astype(BF16)
        combined = attended_ref[here] + dot(hidden, next_refs[2][...])
        combined_ref[here] = combined
        squares = combined * combined
        high = squares.astype(BF16)
        low = (squares - high.astype(F32)).astype(BF16)
        sums_ref[:, here] = outer_cols(ones, high) + outer_cols(ones, low)


def norm_kernel(width, combined_ref, sums_ref, more_ref, gain_ref, out_ref):
    sums = sums_ref[...] if more_ref is None else sums_ref[...] + more_ref[...]
    scale = jnp.transpose(lax.rsqrt(sums / width + EPSILON))[:, :1]
    out_ref[...] = (combined_ref[...] * scale * gain_ref[...]).astype(BF16)


def body(queries, keys, values, rates, w_gate, w_up, w_down, out_gain):
    tok_rows, fw_dim = queries.shape
    seq_count, head_count = lax.axis_size("seq"), lax.axis_size("head")
    w_rows, w_cols = w_gate.shape
    weights = (w_gate, w_up, w_down)

    tail = jnp.stack([keys, values])[:, tok_rows - WINDOW :]
    prev = lax.ppermute(tail, "seq", [(i, i + 1) for i in range(seq_count - 1)])

    grads = kernel_call(
        grads_kernel,
        "gradients",
        jax.ShapeDtypeStruct((3, w_rows, w_cols), F32),
        12 * tok_rows * fw_dim * w_cols,
        8 * tok_rows * fw_dim,
    )(keys, values, rates.reshape(1, tok_rows), *weights)

    chunk_rows = w_rows // CHUNKS
    steps = halving_masks(seq_count, chunk_rows)
    chunks = [grads[:, c * chunk_rows : (c + 1) * chunk_rows] for c in range(CHUNKS)]
    for masks in steps:
        bit = bit_here(masks)
        halves = []
        for g in chunks:
            half = g.shape[1] // 2
            kept = lax.dynamic_slice_in_dim(g, bit * half, half, 1)
            sent = lax.dynamic_slice_in_dim(g, (1 - bit) * half, half, 1).astype(BF16)
            halves.append(kept + swap(sent, masks).astype(F32))
        chunks = halves
    if 1 << len(steps) < seq_count:
        used = 0
        for masks in steps:
            used |= masks[0]
        groups = {}
        for s in range(seq_count):
            groups.setdefault(s & used, []).append(s)
        chunks = [lax.psum(g, "seq", axis_index_groups=list(groups.values())) for g in chunks]
    chunks = [g.astype(BF16) for g in chunks]
    for masks in steps[:0:-1]:
        chunks = [jnp.concatenate([g, swap(g, masks)], axis=1) for g in chunks]
    pieces = []
    for g in chunks:
        pieces.append(g)
        if steps:
            pieces.append(swap(g, steps[0]))

    attended, squares = kernel_call(
        attend_kernel,
        "window_attention",
        (
            jax.ShapeDtypeStruct((tok_rows, fw_dim), F32),
            jax.ShapeDtypeStruct((3, 8, w_cols), F32),
        ),
        4 * tok_rows * (WINDOW + BLOCK) * fw_dim,
        8 * tok_rows * fw_dim,
    )(queries, keys, values, prev, *weights)

    part_rows = w_rows // seq_count
    kept_rows = max(part_rows, SUBROWS)
    part_shape = jax.ShapeDtypeStruct((kept_rows, w_cols), BF16)
    combined, sums, *parts = pl.pallas_call(
        functools.partial(apply_kernel, steps, part_rows),
        out_shape=(
            jax.ShapeDtypeStruct((tok_rows, fw_dim), F32),
            jax.ShapeDtypeStruct((8, tok_rows), F32),
            part_shape,
            part_shape,
            part_shape,
        ),
        name="apply",
        scratch_shapes=[pltpu.VMEM((w_rows, w_cols), BF16)] * 3,
        compiler_params=pltpu.CompilerParams(vmem_limit_bytes=VMEM_LIMIT),
        cost_estimate=pl.CostEstimate(
            flops=6 * tok_rows * fw_dim * w_cols,
            bytes_accessed=12 * tok_rows * fw_dim,
            transcendentals=0,
        ),
    )(*pieces, queries, *weights, squares, attended)
    if part_rows < kept_rows:
        start = (lax.axis_index("seq") * part_rows) % kept_rows
        parts = [lax.dynamic_slice_in_dim(p, start, part_rows, 0) for p in parts]

    width = fw_dim * head_count
    if head_count == 2:
        more = [lax.ppermute(sums, "head", [(0, 1), (1, 0)])]
        norm = functools.partial(norm_kernel, width)
    else:
        sums, more = lax.psum(sums, "head"), []

        def norm(combined_ref, sums_ref, gain_ref, out_ref):
            norm_kernel(width, combined_ref, sums_ref, None, gain_ref, out_ref)

    output = kernel_call(
        norm,
        "norm",
        jax.ShapeDtypeStruct((tok_rows, fw_dim), BF16),
        4 * tok_rows * fw_dim,
        6 * tok_rows * fw_dim,
    )(combined, sums, *more, out_gain.reshape(1, fw_dim))
    return (output, *parts)


def solution(mesh):
    placed = (
        P("seq", "head"),
        P("seq", "head"),
        P("seq", "head"),
        P("seq", "head"),
        P("head", None),
        P("head", None),
        P("head", None),
        P("head"),
    )
    return jax.shard_map(
        body,
        mesh=mesh,
        in_specs=placed,
        out_specs=(
            P("seq", "head"),
            P(("head", "seq"), None),
            P(("head", "seq"), None),
            P(("head", "seq"), None),
        ),
        check_vma=False,
    )
```

time: 208 us -> 104 us (0.50)
  waiting for transfers between devices: 129 us -> 42.1 us
  matrix products: 30 us -> 0 us
  starting transfers between devices: 3.28 us -> 23.8 us
  Pallas kernels: 0 us -> 18.9 us
  between operations: 18.4 us -> 0.95 us
  other arithmetic: 13.8 us -> 2.81 us
  local copies, waits for them, and re-layouts: 7.67 us -> 14 us
  blocking collectives: 2.78 us -> 0 us
    psum x1 -> x0, waiting for transfers between devices: 116 us -> none  [body(): lax.psum((grad_gate, grad_up, grad_down), 'seq')]
    dot_general x12 -> x0, matrix products: 30 us -> none  [the longest x4 14 us: window_attend(): jnp.dot(weights, value_head, preferred_element_type=jnp.float32)]
    ppermute x1 -> x18, waiting for transfers between devices: 13.2 us -> 42.1 us  [the longest x16 41.2 us: swap(): return lax.ppermute(x, ('seq', 'head'), pairs)]
    ppermute x1 -> x18, starting transfers between devices: 3.24 us -> 23.8 us  [the longest x16 13.3 us: swap(): return lax.ppermute(x, ('seq', 'head'), pairs)]
    pallas_call x0 -> x4, Pallas kernels: none -> 18.9 us  [the longest x1 7.4 us: body(): kernel_call(attend_kernel, 'window_attention', (jax.ShapeDtypeStruct((tok...]
    reduce_sum x6 -> x0, other arithmetic: 7.76 us -> none  [the longest x3 2.61 us: step_weight(): weight_rms = jnp.sqrt(jnp.mean(jnp.square(full_float)))]
    slice x0 -> x1, local copies, waits for them, and re-layouts: none -> 3.51 us  [body(): grads[:, c * chunk_rows:(c + 1) * chunk_rows]]
    convert_element_type x0 -> x8, local copies, waits for them, and re-layouts: none -> 2.99 us  [body(): sent = lax.dynamic_slice_in_dim(g, (1 - bit) * half, half, 1).astype(BF16)]
  transfers between devices with their start and end apart: 2 -> 18, of which waited for: 2 -> 15; matrix products, arithmetic and copies ran while one was open for 16% -> 4% of each run, Pallas kernels for 0% -> 7%
where the time goes in v1:
time: 104 us; the launch traced here: 103 us
  waiting for transfers between devices  42.1 us (40%)
  starting transfers between devices  23.8 us (23%)
  Pallas kernels  18.9 us (18%)
  local copies, waits for them, and re-layouts  14 us (13%)
  other arithmetic  2.81 us (3%)
    ppermute x16, waiting for transfers between devices, swap(): return lax.ppermute(x, ('seq', 'head'), pairs)  41.2 us
    ppermute x16, starting transfers between devices, swap(): return lax.ppermute(x, ('seq', 'head'), pairs)  13.3 us
    unnamed x28, local copies, waits for them, and re-layouts  7.51 us
    pallas_call x1, Pallas kernels, body(): kernel_call(attend_kernel, 'window_attention', (jax.ShapeDtypeStruct((tok...  7.4 us
    ppermute x1, starting transfers between devices, body(): more = [lax.ppermute(sums, 'head', [(0, 1), (1, 0)])]  7.21 us
    pallas_call x1, Pallas kernels, body(): pl.pallas_call(functools.partial(apply_kernel, steps, part_rows), out_sha...  5.42 us
    pallas_call x1, Pallas kernels, body(): kernel_call(grads_kernel, 'gradients', jax.ShapeDtypeStruct((3, w_rows, w...  4.84 us
    slice x1, local copies, waits for them, and re-layouts, body(): grads[:, c * chunk_rows:(c + 1) * chunk_rows]  3.51 us
  transfers between devices with their start and end apart: 18, of which 15 were waited for; matrix products, arithmetic and copies ran while one was open for 4% of the time, Pallas kernels for 7%

profile of v1, /device:TPU:17, one launch (start us, length us, event | category | flops | bytes accessed | tf_op | source)
XLA Modules:
  0.0 102.5 jit_solution(14112919107000233268)
XLA Ops:
  0.7 1.1 %copy-done = bf16[768,512]{1,0:T(8,128)(2,1)S(1)} copy-done((bf16[768,512]{1,0:T(8,128)(2,1)S(1)}, bf16[768,512]{1,0:T(8,128)(2,1)}, u32[]{:S(2)}) %copy-start) | copy-done | bytes 786456
  1.8 1.1 %copy-done.2 = bf16[768,512]{1,0:T(8,128)(2,1)S(1)} copy-done((bf16[768,512]{1,0:T(8,128)(2,1)S(1)}, bf16[768,512]{1,0:T(8,128)(2,1)}, u32[]{:S(2)}) %copy-start.2) | copy-done | bytes 786456
  2.9 1.0 %copy-done.5 = bf16[512,512]{1,0:T(8,128)(2,1)S(1)} copy-done((bf16[512,512]{1,0:T(8,128)(2,1)S(1)}, bf16[512,512]{1,0:T(8,128)(2,1)}, u32[]{:S(2)}) %copy-start.5) | copy-done | bytes 524312
  4.0 1.0 %copy-done.7 = bf16[512,512]{1,0:T(8,128)(2,1)S(1)} copy-done((bf16[512,512]{1,0:T(8,128)(2,1)S(1)}, bf16[512,512]{1,0:T(8,128)(2,1)}, u32[]{:S(2)}) %copy-start.7) | copy-done | bytes 524312
  5.0 1.0 %copy-done.9 = bf16[512,512]{1,0:T(8,128)(2,1)S(1)} copy-done((bf16[512,512]{1,0:T(8,128)(2,1)S(1)}, bf16[512,512]{1,0:T(8,128)(2,1)}, u32[]{:S(2)}) %copy-start.9) | copy-done | bytes 524312
  6.7 4.8 %gradients.1 = f32[3,512,512]{2,1,0:T(8,128)} custom-call(bf16[768,512]{1,0:T(8,128)(2,1)S(1)} %copy-done, bf16[768,512]{1,0:T(8,128)(2,1)S(1)} %copy-done.2, f32[1,768]{1,0:T(1,128)S(1)} %bitcast.7, bf16[512,512]{1,0:T(8,128)(2,1)S(1)} %copy-done.5, bf16[512,512]{1,0:T(8,128)(2,1)S(1)} %copy-done.7, bf16[512,512]{1,0:T(8,128)(2,1)S(1)} %copy-done.9), custom_call_target="tpu_custom_call" | custom-call | flops 2415919104 | bytes 3145728 | tf_op jit(solution)/shard_map/gradients/pallas_call | solution.py:207
  11.6 3.5 %fusion = (f32[3,256,512]{2,1,0:T(8,128)S(1)}, f32[3,256,512]{2,1,0:T(8,128)}) fusion(f32[3,512,512]{2,1,0:T(8,128)} %gradients.1), kind=kLoop, calls=%fused_computation.23 | loop fusion | bytes 6291456 | tf_op jit(solution)/shard_map/slice | solution.py:217
  15.1 2.0 %dynamic-slice_convert_fusion.1 = bf16[3,128,512]{2,1,0:T(8,128)(2,1)} fusion(f32[3,256,512]{2,1,0:T(8,128)} %get-tuple-element.19, s32[]{:T(128)S(6)} %select_n.48), kind=kLoop, calls=%fused_computation.4 | loop fusion | bytes 786436 | tf_op jit(solution)/shard_map/convert_element_type | solution.py:224
  17.1 1.2 %collective-permute-start = (bf16[3,128,512]{2,1,0:T(8,128)(2,1)}, bf16[3,128,512]{2,1,0:T(8,128)(2,1)}, u32[]{:S(2)}, u32[]{:S(2)}) collective-permute-start(bf16[3,128,512]{2,1,0:T(8,128)(2,1)} %dynamic-slice_convert_fusion.1), channel_id=1, source_target_pairs={{0,2},{1,5},{2,0},{3,7},{4,6},{5,1},{6,4},{7,3},{8,10},{9,13},{10,... | collective-permute-start | bytes 1179656 | tf_op jit(solution)/shard_map/ppermute | solution.py:81
  19.4 1.1 %pad_maximum_fusion = bf16[2,512,512]{2,1,0:T(8,128)(2,1)} fusion(bf16[1,768,512]{2,1,0:T(8,128)(2,1)S(1)} %bitcast.5, bf16[1,768,512]{2,1,0:T(8,128)(2,1)S(1)} %bitcast.4), kind=kLoop, calls=%fused_computation | loop fusion | flops 2097152 | bytes 2621440 | tf_op jit(solution)/shard_map/stack | solution.py:204
  20.4 3.3 %collective-permute-start.16 = (bf16[2,512,512]{2,1,0:T(8,128)(2,1)}, bf16[2,512,512]{2,1,0:T(8,128)(2,1)}, u32[]{:S(2)}, u32[]{:S(2)}) collective-permute-start(bf16[2,512,512]{2,1,0:T(8,128)(2,1)} %pad_maximum_fusion), channel_id=1, source_target_pairs={{0,2},{2,4},{4,6},{6,8},{8,10},{10,12},{12,14},{14,16},{16,18},{18... | collective-permute-start | bytes 3145736 | tf_op jit(solution)/shard_map/ppermute | solution.py:205
  24.4 1.4 %convert_add_fusion.1 = f32[3,128,512]{2,1,0:T(8,128)S(1)} fusion(bf16[3,128,512]{2,1,0:T(8,128)(2,1)} %collective-permute-done, f32[3,256,512]{2,1,0:T(8,128)} %get-tuple-element.19, s32[]{:T(128)S(6)} %mul.32), kind=kLoop, calls=%fused_computation.3 | loop fusion | flops 393216 | bytes 1966084 | tf_op jit(solution)/shard_map/add | solution.py:225
  25.8 1.4 %collective-permute-start.1 = (bf16[3,64,512]{2,1,0:T(8,128)(2,1)S(1)}, bf16[3,64,512]{2,1,0:T(8,128)(2,1)S(1)}, u32[]{:S(2)}, u32[]{:S(2)}) collective-permute-start(bf16[3,64,512]{2,1,0:T(8,128)(2,1)S(1)} %dynamic-slice_convert_fusion.3), channel_id=1, source_target_pairs={{0,8},{1,9},{2,10},{3,11},{4,12},{5,13},{6,14},{7,15},{8,0},{9,1},... | collective-permute-start | bytes 589832 | tf_op jit(solution)/shard_map/ppermute | solution.py:81
  27.1 23.5 %collective-permute-done.8 = bf16[3,128,512]{2,1,0:T(8,128)(2,1)S(1)} collective-permute-done((bf16[3,128,512]{2,1,0:T(8,128)(2,1)}, bf16[3,128,512]{2,1,0:T(8,128)(2,1)S(1)}, u32[]{:S(2)}, u32[]{:S(2)}) %collective-permute-start.8) | collective-permute-done | bytes 393248 | tf_op jit(solution)/shard_map/ppermute | solution.py:81
  50.8 1.4 %collective-permute-start.9 = (bf16[3,64,512]{2,1,0:T(8,128)(2,1)S(1)}, bf16[3,64,512]{2,1,0:T(8,128)(2,1)S(1)}, u32[]{:S(2)}, u32[]{:S(2)}) collective-permute-start(bf16[3,64,512]{2,1,0:T(8,128)(2,1)S(1)} %dynamic-slice_convert_fusion.2), channel_id=1, source_target_pairs={{0,8},{1,9},{2,10},{3,11},{4,12},{5,13},{6,14},{7,15},{8,0},{9,1},... | collective-permute-start | bytes 589832 | tf_op jit(solution)/shard_map/ppermute | solution.py:81
  52.4 3.0 %collective-permute-done.9 = bf16[3,64,512]{2,1,0:T(8,128)(2,1)S(1)} collective-permute-done((bf16[3,64,512]{2,1,0:T(8,128)(2,1)S(1)}, bf16[3,64,512]{2,1,0:T(8,128)(2,1)S(1)}, u32[]{:S(2)}, u32[]{:S(2)}) %collective-permute-start.9) | collective-permute-done | bytes 196640 | tf_op jit(solution)/shard_map/ppermute | solution.py:81
  56.0 3.0 %collective-permute-done.10 = bf16[3,32,512]{2,1,0:T(8,128)(2,1)S(1)} collective-permute-done((bf16[3,32,512]{2,1,0:T(8,128)(2,1)S(1)}, bf16[3,32,512]{2,1,0:T(8,128)(2,1)S(1)}, u32[]{:S(2)}, u32[]{:S(2)}) %collective-permute-start.10) | collective-permute-done | bytes 98336 | tf_op jit(solution)/shard_map/ppermute | solution.py:81
  59.9 1.7 %collective-permute-start.4 = (bf16[3,16,512]{2,1,0:T(8,128)(2,1)S(1)}, bf16[3,16,512]{2,1,0:T(8,128)(2,1)S(1)}, u32[]{:S(2)}, u32[]{:S(2)}) collective-permute-start(bf16[3,16,512]{2,1,0:T(8,128)(2,1)S(1)} %add_convert_fusion.1), channel_id=1, source_target_pairs={{0,16},{1,17},{2,18},{3,19},{4,20},{5,21},{6,22},{7,23},{8,24},{9,... | collective-permute-start | bytes 147464 | tf_op jit(solution)/shard_map/ppermute | solution.py:81
  61.6 1.4 %collective-permute-done.11 = bf16[3,16,512]{2,1,0:T(8,128)(2,1)S(1)} collective-permute-done((bf16[3,16,512]{2,1,0:T(8,128)(2,1)S(1)}, bf16[3,16,512]{2,1,0:T(8,128)(2,1)S(1)}, u32[]{:S(2)}, u32[]{:S(2)}) %collective-permute-start.11) | collective-permute-done | bytes 49184 | tf_op jit(solution)/shard_map/ppermute | solution.py:81
  63.9 1.2 %collective-permute-start.5 = (bf16[3,32,512]{2,1,0:T(8,128)(2,1)S(1)}, bf16[3,32,512]{2,1,0:T(8,128)(2,1)S(1)}, u32[]{:S(2)}, u32[]{:S(2)}) collective-permute-start(bf16[3,32,512]{2,1,0:T(8,128)(2,1)S(1)} %pad_maximum_fusion.5), channel_id=1, source_target_pairs={{0,4},{1,3},{2,6},{3,1},{4,0},{5,7},{6,2},{7,5},{8,12},{9,11},{10,... | collective-permute-start | bytes 294920 | tf_op jit(solution)/shard_map/ppermute | solution.py:81
  65.1 2.4 %collective-permute-done.12 = bf16[3,16,512]{2,1,0:T(8,128)(2,1)S(1)} collective-permute-done((bf16[3,16,512]{2,1,0:T(8,128)(2,1)S(1)}, bf16[3,16,512]{2,1,0:T(8,128)(2,1)S(1)}, u32[]{:S(2)}, u32[]{:S(2)}) %collective-permute-start.12) | collective-permute-done | bytes 49184 | tf_op jit(solution)/shard_map/ppermute | solution.py:81
  67.7 3.0 %collective-permute-start.6 = (bf16[3,64,512]{2,1,0:T(8,128)(2,1)S(1)}, bf16[3,64,512]{2,1,0:T(8,128)(2,1)S(1)}, u32[]{:S(2)}, u32[]{:S(2)}) collective-permute-start(bf16[3,64,512]{2,1,0:T(8,128)(2,1)S(1)} %pad_maximum_fusion.3), channel_id=1, source_target_pairs={{0,8},{1,9},{2,10},{3,11},{4,12},{5,13},{6,14},{7,15},{8,0},{9,1},... | collective-permute-start | bytes 589832 | tf_op jit(solution)/shard_map/ppermute | solution.py:81
  71.1 2.5 %collective-permute-start.14 = (bf16[3,64,512]{2,1,0:T(8,128)(2,1)S(1)}, bf16[3,64,512]{2,1,0:T(8,128)(2,1)S(1)}, u32[]{:S(2)}, u32[]{:S(2)}) collective-permute-start(bf16[3,64,512]{2,1,0:T(8,128)(2,1)S(1)} %pad_maximum_fusion.4), channel_id=1, source_target_pairs={{0,8},{1,9},{2,10},{3,11},{4,12},{5,13},{6,14},{7,15},{8,0},{9,1},... | collective-permute-start | bytes 589832 | tf_op jit(solution)/shard_map/ppermute | solution.py:81
  73.6 1.0 %collective-permute-done.6 = bf16[3,64,512]{2,1,0:T(8,128)(2,1)S(1)} collective-permute-done((bf16[3,64,512]{2,1,0:T(8,128)(2,1)S(1)}, bf16[3,64,512]{2,1,0:T(8,128)(2,1)S(1)}, u32[]{:S(2)}, u32[]{:S(2)}) %collective-permute-start.6) | collective-permute-done | bytes 196640 | tf_op jit(solution)/shard_map/ppermute | solution.py:81
  74.7 2.2 %collective-permute-done.14 = bf16[3,64,512]{2,1,0:T(8,128)(2,1)S(1)} collective-permute-done((bf16[3,64,512]{2,1,0:T(8,128)(2,1)S(1)}, bf16[3,64,512]{2,1,0:T(8,128)(2,1)S(1)}, u32[]{:S(2)}, u32[]{:S(2)}) %collective-permute-start.14) | collective-permute-done | bytes 196640 | tf_op jit(solution)/shard_map/ppermute | solution.py:81
  77.1 7.4 %window_attention.1 = (f32[768,512]{1,0:T(8,128)}, f32[3,8,512]{2,1,0:T(8,128)S(1)}) custom-call(bf16[768,512]{1,0:T(8,128)(2,1)S(1)} %copy-done.4, bf16[768,512]{1,0:T(8,128)(2,1)S(1)} %copy-done.1, bf16[768,512]{1,0:T(8,128)(2,1)S(1)} %copy-done.3, bf16[2,512,512]{2,1,0:T(8,128)(2,1)} %collective-permute-done.16.prev_ref, bf16[512,512]{1,0:T(8,128)(2,1)S(1)} %copy-done.6, ...), custom_call_target="tpu_custom_call" | custom-call | flops 1207959552 | bytes 3145728 | tf_op jit(solution)/shard_map/window_attention/pallas_call | solution.py:244
  84.5 1.9 %collective-permute-done.15.refs_3_ = bf16[3,128,512]{2,1,0:T(8,128)(2,1)S(1)} collective-permute-done((bf16[3,128,512]{2,1,0:T(8,128)(2,1)S(1)}, bf16[3,128,512]{2,1,0:T(8,128)(2,1)S(1)}, u32[]{:S(2)}, u32[]{:S(2)}) %collective-permute-start.15) | collective-permute-done | bytes 393248 | tf_op jit(solution)/shard_map/ppermute | solution.py:81
  86.4 5.4 %apply.1 = (f32[768,512]{1,0:T(8,128)}, f32[8,768]{1,0:T(8,128)S(1)}, bf16[32,512]{1,0:T(8,128)(2,1)}, bf16[32,512]{1,0:T(8,128)(2,1)}, bf16[32,512]{1,0:T(8,128)(2,1)}) custom-call(bf16[3,128,512]{2,1,0:T(8,128)(2,1)S(1)} %pad_maximum_fusion.1.refs_0_, bf16[3,128,512]{2,1,0:T(8,128)(2,1)S(1)} %collective-permute-done.7.refs_1_, ...), custom_call_target="tpu_custom_call" | custom-call | flops 1207959552 | bytes 4718592 | tf_op jit(solution)/shard_map/apply/pallas_call | solution.py:258
  91.8 7.2 %collective-permute-start.17 = (f32[8,768]{1,0:T(8,128)S(1)}, f32[8,768]{1,0:T(8,128)S(1)}, u32[]{:S(2)}, u32[]{:S(2)}) collective-permute-start(f32[8,768]{1,0:T(8,128)S(1)} %get-tuple-element.14.sums_ref), channel_id=1, source_target_pairs={{0,1},{1,0},{2,3},{3,2},{4,5},{5,4},{6,7},{7,6},{8,9},{9,8},{10,11... | collective-permute-start | bytes 73736 | tf_op jit(solution)/shard_map/ppermute | solution.py:282
  99.0 0.8 collective-permute-done.17.more_ref
  99.9 1.4 %copy-done.11 = f32[768,512]{1,0:T(8,128)S(1)} copy-done((f32[768,512]{1,0:T(8,128)S(1)}, f32[768,512]{1,0:T(8,128)}, u32[]{:S(2)}) %copy-start.11) | copy-done | bytes 1572888
  101.3 1.2 %norm.1 = bf16[768,512]{1,0:T(8,128)(2,1)} custom-call(f32[768,512]{1,0:T(8,128)S(1)} %copy-done.11, f32[8,768]{1,0:T(8,128)S(1)} %get-tuple-element.14.sums_ref, f32[8,768]{1,0:T(8,128)S(1)} %collective-permute-done.17.more_ref, f32[1,512]{1,0:T(1,128)S(1)} %bitcast.6), custom_call_target="tpu_custom_call" | custom-call | flops 1572864 | bytes 2359296 | tf_op jit(solution)/shard_map/norm/pallas_call | solution.py:290
  (60 shorter events, 5.6 us)
Async XLA Ops:
  0.6 1.1 %copy-start = (bf16[768,512]{1,0:T(8,128)(2,1)S(1)}, bf16[768,512]{1,0:T(8,128)(2,1)}, u32[]{:S(2)}) copy-start(bf16[768,512]{1,0:T(8,128)(2,1)} %k_ref.3) | copy-start | bytes 2359300
  1.8 1.1 %copy-start.2 = (bf16[768,512]{1,0:T(8,128)(2,1)S(1)}, bf16[768,512]{1,0:T(8,128)(2,1)}, u32[]{:S(2)}) copy-start(bf16[768,512]{1,0:T(8,128)(2,1)} %v_ref.3) | copy-start | bytes 2359300
  2.9 1.0 %copy-start.5 = (bf16[512,512]{1,0:T(8,128)(2,1)S(1)}, bf16[512,512]{1,0:T(8,128)(2,1)}, u32[]{:S(2)}) copy-start(bf16[512,512]{1,0:T(8,128)(2,1)} %refs_5_.1) | copy-start | bytes 1572868
  4.0 1.0 %copy-start.7 = (bf16[512,512]{1,0:T(8,128)(2,1)S(1)}, bf16[512,512]{1,0:T(8,128)(2,1)}, u32[]{:S(2)}) copy-start(bf16[512,512]{1,0:T(8,128)(2,1)} %refs_6_.1) | copy-start | bytes 1572868
  5.0 1.0 %copy-start.9 = (bf16[512,512]{1,0:T(8,128)(2,1)S(1)}, bf16[512,512]{1,0:T(8,128)(2,1)}, u32[]{:S(2)}) copy-start(bf16[512,512]{1,0:T(8,128)(2,1)} %refs_7_.1) | copy-start | bytes 1572868
  6.0 0.7 copy-start.13
  15.1 4.3 %copy-start.1 = (bf16[768,512]{1,0:T(8,128)(2,1)S(1)}, bf16[768,512]{1,0:T(8,128)(2,1)}, u32[]{:S(2)}) copy-start(bf16[768,512]{1,0:T(8,128)(2,1)} %k_ref.3) | copy-start | bytes 2359300
  15.1 4.3 %copy-start.3 = (bf16[768,512]{1,0:T(8,128)(2,1)S(1)}, bf16[768,512]{1,0:T(8,128)(2,1)}, u32[]{:S(2)}) copy-start(bf16[768,512]{1,0:T(8,128)(2,1)} %v_ref.3) | copy-start | bytes 2359300
  17.1 7.2 %collective-permute-start = (bf16[3,128,512]{2,1,0:T(8,128)(2,1)}, bf16[3,128,512]{2,1,0:T(8,128)(2,1)}, u32[]{:S(2)}, u32[]{:S(2)}) collective-permute-start(bf16[3,128,512]{2,1,0:T(8,128)(2,1)} %dynamic-slice_convert_fusion.1), channel_id=1, source_target_pairs={{0,2},{1,5},{2,0},{3,7},{4,6},{5,1},{6,4},{7,3},{8,10},{9,13},{10,... | collective-permute-start | bytes 1179656 | tf_op jit(solution)/shard_map/ppermute | solution.py:81
  19.1 31.5 %collective-permute-start.8 = (bf16[3,128,512]{2,1,0:T(8,128)(2,1)}, bf16[3,128,512]{2,1,0:T(8,128)(2,1)S(1)}, u32[]{:S(2)}, u32[]{:S(2)}) collective-permute-start(bf16[3,128,512]{2,1,0:T(8,128)(2,1)} %dynamic-slice_convert_fusion), channel_id=1, source_target_pairs={{0,2},{1,5},{2,0},{3,7},{4,6},{5,1},{6,4},{7,3},{8,10},{9,13},{10,... | collective-permute-start | bytes 1179656 | tf_op jit(solution)/shard_map/ppermute | solution.py:81
  20.4 56.6 %collective-permute-start.16 = (bf16[2,512,512]{2,1,0:T(8,128)(2,1)}, bf16[2,512,512]{2,1,0:T(8,128)(2,1)}, u32[]{:S(2)}, u32[]{:S(2)}) collective-permute-start(bf16[2,512,512]{2,1,0:T(8,128)(2,1)} %pad_maximum_fusion), channel_id=1, source_target_pairs={{0,2},{2,4},{4,6},{6,8},{8,10},{10,12},{12,14},{14,16},{16,18},{18... | collective-permute-start | bytes 3145736 | tf_op jit(solution)/shard_map/ppermute | solution.py:205
  25.8 26.5 %collective-permute-start.1 = (bf16[3,64,512]{2,1,0:T(8,128)(2,1)S(1)}, bf16[3,64,512]{2,1,0:T(8,128)(2,1)S(1)}, u32[]{:S(2)}, u32[]{:S(2)}) collective-permute-start(bf16[3,64,512]{2,1,0:T(8,128)(2,1)S(1)} %dynamic-slice_convert_fusion.3), channel_id=1, source_target_pairs={{0,8},{1,9},{2,10},{3,11},{4,12},{5,13},{6,14},{7,15},{8,0},{9,1},... | collective-permute-start | bytes 589832 | tf_op jit(solution)/shard_map/ppermute | solution.py:81
  50.8 4.6 %collective-permute-start.9 = (bf16[3,64,512]{2,1,0:T(8,128)(2,1)S(1)}, bf16[3,64,512]{2,1,0:T(8,128)(2,1)S(1)}, u32[]{:S(2)}, u32[]{:S(2)}) collective-permute-start(bf16[3,64,512]{2,1,0:T(8,128)(2,1)S(1)} %dynamic-slice_convert_fusion.2), channel_id=1, source_target_pairs={{0,8},{1,9},{2,10},{3,11},{4,12},{5,13},{6,14},{7,15},{8,0},{9,1},... | collective-permute-start | bytes 589832 | tf_op jit(solution)/shard_map/ppermute | solution.py:81
  52.3 3.5 %collective-permute-start.2 = (bf16[3,32,512]{2,1,0:T(8,128)(2,1)S(1)}, bf16[3,32,512]{2,1,0:T(8,128)(2,1)S(1)}, u32[]{:S(2)}, u32[]{:S(2)}) collective-permute-start(bf16[3,32,512]{2,1,0:T(8,128)(2,1)S(1)} %dynamic-slice_convert_fusion.5), channel_id=1, source_target_pairs={{0,4},{1,3},{2,6},{3,1},{4,0},{5,7},{6,2},{7,5},{8,12},{9,11},{10,... | collective-permute-start | bytes 294920 | tf_op jit(solution)/shard_map/ppermute | solution.py:81
  55.5 3.5 %collective-permute-start.10 = (bf16[3,32,512]{2,1,0:T(8,128)(2,1)S(1)}, bf16[3,32,512]{2,1,0:T(8,128)(2,1)S(1)}, u32[]{:S(2)}, u32[]{:S(2)}) collective-permute-start(bf16[3,32,512]{2,1,0:T(8,128)(2,1)S(1)} %dynamic-slice_convert_fusion.4), channel_id=1, source_target_pairs={{0,4},{1,3},{2,6},{3,1},{4,0},{5,7},{6,2},{7,5},{8,12},{9,11},{10,... | collective-permute-start | bytes 294920 | tf_op jit(solution)/shard_map/ppermute | solution.py:81
  55.9 4.0 %collective-permute-start.3 = (bf16[3,16,512]{2,1,0:T(8,128)(2,1)S(1)}, bf16[3,16,512]{2,1,0:T(8,128)(2,1)S(1)}, u32[]{:S(2)}, u32[]{:S(2)}) collective-permute-start(bf16[3,16,512]{2,1,0:T(8,128)(2,1)S(1)} %dynamic-slice_convert_fusion.7), channel_id=1, source_target_pairs={{0,16},{1,17},{2,18},{3,19},{4,20},{5,21},{6,22},{7,23},{8,24},{9,... | collective-permute-start | bytes 147464 | tf_op jit(solution)/shard_map/ppermute | solution.py:81
  59.1 18.0 %copy-start.4 = (bf16[768,512]{1,0:T(8,128)(2,1)S(1)}, bf16[768,512]{1,0:T(8,128)(2,1)}, u32[]{:S(2)}) copy-start(bf16[768,512]{1,0:T(8,128)(2,1)} %refs_4_.1) | copy-start | bytes 2359300
  59.1 18.0 %copy-start.6 = (bf16[512,512]{1,0:T(8,128)(2,1)S(1)}, bf16[512,512]{1,0:T(8,128)(2,1)}, u32[]{:S(2)}) copy-start(bf16[512,512]{1,0:T(8,128)(2,1)} %refs_5_.1) | copy-start | bytes 1572868
  59.1 18.0 %copy-start.8 = (bf16[512,512]{1,0:T(8,128)(2,1)S(1)}, bf16[512,512]{1,0:T(8,128)(2,1)}, u32[]{:S(2)}) copy-start(bf16[512,512]{1,0:T(8,128)(2,1)} %refs_6_.1) | copy-start | bytes 1572868
  59.1 18.0 %copy-start.10 = (bf16[512,512]{1,0:T(8,128)(2,1)S(1)}, bf16[512,512]{1,0:T(8,128)(2,1)}, u32[]{:S(2)}) copy-start(bf16[512,512]{1,0:T(8,128)(2,1)} %refs_7_.1) | copy-start | bytes 1572868
  59.1 3.9 %collective-permute-start.11 = (bf16[3,16,512]{2,1,0:T(8,128)(2,1)S(1)}, bf16[3,16,512]{2,1,0:T(8,128)(2,1)S(1)}, u32[]{:S(2)}, u32[]{:S(2)}) collective-permute-start(bf16[3,16,512]{2,1,0:T(8,128)(2,1)S(1)} %dynamic-slice_convert_fusion.6), channel_id=1, source_target_pairs={{0,16},{1,17},{2,18},{3,19},{4,20},{5,21},{6,22},{7,23},{8,24},{9,... | collective-permute-start | bytes 147464 | tf_op jit(solution)/shard_map/ppermute | solution.py:81
  59.9 3.9 %collective-permute-start.4 = (bf16[3,16,512]{2,1,0:T(8,128)(2,1)S(1)}, bf16[3,16,512]{2,1,0:T(8,128)(2,1)S(1)}, u32[]{:S(2)}, u32[]{:S(2)}) collective-permute-start(bf16[3,16,512]{2,1,0:T(8,128)(2,1)S(1)} %add_convert_fusion.1), channel_id=1, source_target_pairs={{0,16},{1,17},{2,18},{3,19},{4,20},{5,21},{6,22},{7,23},{8,24},{9,... | collective-permute-start | bytes 147464 | tf_op jit(solution)/shard_map/ppermute | solution.py:81
  63.1 4.5 %collective-permute-start.12 = (bf16[3,16,512]{2,1,0:T(8,128)(2,1)S(1)}, bf16[3,16,512]{2,1,0:T(8,128)(2,1)S(1)}, u32[]{:S(2)}, u32[]{:S(2)}) collective-permute-start(bf16[3,16,512]{2,1,0:T(8,128)(2,1)S(1)} %add_convert_fusion), channel_id=1, source_target_pairs={{0,16},{1,17},{2,18},{3,19},{4,20},{5,21},{6,22},{7,23},{8,24},{9,... | collective-permute-start | bytes 147464 | tf_op jit(solution)/shard_map/ppermute | solution.py:81
  63.9 3.8 %collective-permute-start.5 = (bf16[3,32,512]{2,1,0:T(8,128)(2,1)S(1)}, bf16[3,32,512]{2,1,0:T(8,128)(2,1)S(1)}, u32[]{:S(2)}, u32[]{:S(2)}) collective-permute-start(bf16[3,32,512]{2,1,0:T(8,128)(2,1)S(1)} %pad_maximum_fusion.5), channel_id=1, source_target_pairs={{0,4},{1,3},{2,6},{3,1},{4,0},{5,7},{6,2},{7,5},{8,12},{9,11},{10,... | collective-permute-start | bytes 294920 | tf_op jit(solution)/shard_map/ppermute | solution.py:81
  67.5 3.5 %collective-permute-start.13 = (bf16[3,32,512]{2,1,0:T(8,128)(2,1)S(1)}, bf16[3,32,512]{2,1,0:T(8,128)(2,1)S(1)}, u32[]{:S(2)}, u32[]{:S(2)}) collective-permute-start(bf16[3,32,512]{2,1,0:T(8,128)(2,1)S(1)} %pad_maximum_fusion.6), channel_id=1, source_target_pairs={{0,4},{1,3},{2,6},{3,1},{4,0},{5,7},{6,2},{7,5},{8,12},{9,11},{10,... | collective-permute-start | bytes 294920 | tf_op jit(solution)/shard_map/ppermute | solution.py:81
  67.7 6.9 %collective-permute-start.6 = (bf16[3,64,512]{2,1,0:T(8,128)(2,1)S(1)}, bf16[3,64,512]{2,1,0:T(8,128)(2,1)S(1)}, u32[]{:S(2)}, u32[]{:S(2)}) collective-permute-start(bf16[3,64,512]{2,1,0:T(8,128)(2,1)S(1)} %pad_maximum_fusion.3), channel_id=1, source_target_pairs={{0,8},{1,9},{2,10},{3,11},{4,12},{5,13},{6,14},{7,15},{8,0},{9,1},... | collective-permute-start | bytes 589832 | tf_op jit(solution)/shard_map/ppermute | solution.py:81
  71.1 5.8 %collective-permute-start.14 = (bf16[3,64,512]{2,1,0:T(8,128)(2,1)S(1)}, bf16[3,64,512]{2,1,0:T(8,128)(2,1)S(1)}, u32[]{:S(2)}, u32[]{:S(2)}) collective-permute-start(bf16[3,64,512]{2,1,0:T(8,128)(2,1)S(1)} %pad_maximum_fusion.4), channel_id=1, source_target_pairs={{0,8},{1,9},{2,10},{3,11},{4,12},{5,13},{6,14},{7,15},{8,0},{9,1},... | collective-permute-start | bytes 589832 | tf_op jit(solution)/shard_map/ppermute | solution.py:81
  74.6 9.9 %collective-permute-start.7 = (bf16[3,128,512]{2,1,0:T(8,128)(2,1)S(1)}, bf16[3,128,512]{2,1,0:T(8,128)(2,1)S(1)}, u32[]{:S(2)}, u32[]{:S(2)}) collective-permute-start(bf16[3,128,512]{2,1,0:T(8,128)(2,1)S(1)} %pad_maximum_fusion.1.refs_0_), channel_id=1, source_target_pairs={{0,2},{1,5},{2,0},{3,7},{4,6},{5,1},{6,4},{7,3},{8,10},{9,13},{10,... | collective-permute-start | bytes 1179656 | tf_op jit(solution)/shard_map/ppermute | solution.py:81
  77.0 9.4 %collective-permute-start.15 = (bf16[3,128,512]{2,1,0:T(8,128)(2,1)S(1)}, bf16[3,128,512]{2,1,0:T(8,128)(2,1)S(1)}, u32[]{:S(2)}, u32[]{:S(2)}) collective-permute-start(bf16[3,128,512]{2,1,0:T(8,128)(2,1)S(1)} %pad_maximum_fusion.2.refs_2_), channel_id=1, source_target_pairs={{0,2},{1,5},{2,0},{3,7},{4,6},{5,1},{6,4},{7,3},{8,10},{9,13},{10,... | collective-permute-start | bytes 1179656 | tf_op jit(solution)/shard_map/ppermute | solution.py:81
  86.4 13.5 %copy-start.12 = (f32[512]{0:T(512)S(1)}, f32[512]{0:T(512)}, u32[]{:S(2)}) copy-start(f32[512]{0:T(512)} %param.15) | copy-start | bytes 6148
  91.8 8.1 %collective-permute-start.17 = (f32[8,768]{1,0:T(8,128)S(1)}, f32[8,768]{1,0:T(8,128)S(1)}, u32[]{:S(2)}, u32[]{:S(2)}) collective-permute-start(f32[8,768]{1,0:T(8,128)S(1)} %get-tuple-element.14.sums_ref), channel_id=1, source_target_pairs={{0,1},{1,0},{2,3},{3,2},{4,5},{5,4},{6,7},{7,6},{8,9},{9,8},{10,11... | collective-permute-start | bytes 73736 | tf_op jit(solution)/shard_map/ppermute | solution.py:282
  99.9 1.4 %copy-start.11 = (f32[768,512]{1,0:T(8,128)S(1)}, f32[768,512]{1,0:T(8,128)}, u32[]{:S(2)}) copy-start(f32[768,512]{1,0:T(8,128)} %get-tuple-element.13.combined_ref) | copy-start | bytes 4718596

commit v2 on v1

--- a/solution.py
+++ b/solution.py
@@ -19,7 +19,8 @@
 
 F32 = jnp.float32
 BF16 = jnp.bfloat16
-VMEM_LIMIT = 50 * 1024 * 1024
+VMEM_LIMIT = 40 * 1024 * 1024
+VMEM_WHOLE = 62 * 1024 * 1024
 
 
 def inner_rows(left_op, right_op):
@@ -48,19 +49,10 @@
     )
 
 
-def halving_masks(peers, rows):
-    bits = []
-    while peers % (2 << len(bits)) == 0 and peers > 1 << len(bits):
-        bits.append(1 << len(bits))
-    pairs = [(b, b) for b in bits]
-    if len(bits) >= 3:
-        pairs = [(bits[0], bits[1]), (bits[2], bits[2]), (bits[1], bits[0])]
-        pairs += [(b, b) for b in bits[3:]]
-    steps = []
-    while pairs and rows % (2 * SUBROWS) == 0:
-        steps.append(pairs.pop(0))
-        rows //= 2
-    return steps
+def exchange_masks(peers):
+    bits = [1 << at for at in range(peers.bit_length() - 1)]
+    halving = [(bits[1], bits[2]), (bits[2], bits[1]), (bits[0], bits[0])]
+    return halving, [(b, b) for b in bits[3:]]
 
 
 def mask_here(masks):
@@ -81,24 +73,127 @@
     return lax.ppermute(x, ("seq", "head"), pairs)
 
 
-def grads_kernel(k_ref, v_ref, rate_ref, gate_ref, up_ref, down_ref, out_ref):
+def tails_kernel(v_hbm, k_hbm, v_out, k_out, v_ref, k_ref, sems):
+    rows = v_ref.shape[0]
+    moves = []
+    for source, held, target in ((v_hbm, v_ref, v_out), (k_hbm, k_ref, k_out)):
+        for start in range(0, rows, BLOCK // 2):
+            here = pl.ds(start, BLOCK // 2)
+            there = pl.ds(source.shape[0] - rows + start, BLOCK // 2)
+            moves.append((source.at[there], held.at[here], target.at[here]))
+    first = [pltpu.make_async_copy(a, b, sems.at[0, i]) for i, (a, b, _) in enumerate(moves)]
+    second = [pltpu.make_async_copy(b, c, sems.at[1, i]) for i, (_, b, c) in enumerate(moves)]
+    for copy in first:
+        copy.start()
+    for copy, after in zip(first, second):
+        copy.wait()
+        after.start()
+    for after in second:
+        after.wait()
+
+
+def shift_tail(x):
+    return lax.ppermute(x, "seq", [(i, i + 1) for i in range(lax.axis_size("seq") - 1)])
+
+
+def pass_odd(x):
+    return lax.ppermute(x, "seq", [(i, i ^ 2) for i in range(1, lax.axis_size("seq"), 2)])
+
+
+def shift_passed(x, passed):
+    peers = lax.axis_size("seq")
+    odd = lax.axis_index("seq") % 2 == 1
+    pairs = [(i, i + 1) for i in range(0, peers, 2)]
+    pairs += [(i, (i ^ 2) + 1) for i in range(1, peers, 2) if (i ^ 2) + 1 < peers]
+    return lax.ppermute(jnp.where(odd, passed, x), "seq", pairs)
+
+
+def grads_kernel(step, *refs):
+    k_hbm, v_hbm, gate_hbm, up_hbm, down_hbm, rate_ref = refs[:6]
+    sent_refs, kept_refs = refs[6 : 6 + CHUNKS], refs[6 + CHUNKS : 6 + 2 * CHUNKS]
+    k_ref, v_ref, gate_ref, up_ref, down_ref, order_ref, hidden_ref, sems = refs[6 + 2 * CHUNKS :]
+    copies = [
+        pltpu.make_async_copy(source, target, sems.at[at])
+        for at, (source, target) in enumerate(
+            (
+                (k_hbm, k_ref),
+                (gate_hbm, gate_ref),
+                (up_hbm, up_ref),
+                (v_hbm, v_ref),
+                (down_hbm, down_ref),
+            )
+        )
+    ]
+    for copy in copies:
+        copy.start()
     rows = k_ref.shape[0]
+    half = sent_refs[0].shape[1]
+    bit = bit_here(step)
+    places = []
+    for chunk in range(CHUNKS):
+        for which in (1 - bit, bit):
+            start = pl.multiple_of((2 * chunk + which) * half, half)
+            places.append(pl.ds(start, half))
+    copies[0].wait()
     key_rows = k_ref[...]
+    for at, place in enumerate(places):
+        order_ref[:, at * half : (at + 1) * half] = k_ref[:, place]
+    copies[1].wait()
     gate_pre = dot(key_rows, gate_ref[...])
+    copies[2].wait()
     up_pre = dot(key_rows, up_ref[...])
     sigmoid_val = jax.nn.sigmoid(gate_pre)
     activated = gate_pre * sigmoid_val
-    hidden = (activated * up_pre).astype(BF16)
+    hidden_ref[...] = (activated * up_pre).astype(BF16)
+    copies[3].wait()
     rate_col = jnp.transpose(jnp.broadcast_to(rate_ref[...], (8, rows)))[:, :1]
     target = (rate_col * v_ref[...].astype(F32)).astype(BF16)
-    out_ref[2] = inner_rows(hidden, target)
+    copies[4].wait()
     backward = outer_cols(target, down_ref[...])
-    out_ref[1] = inner_rows(key_rows, (backward * activated).astype(BF16))
     derivative = sigmoid_val * (1.0 + gate_pre * (1.0 - sigmoid_val))
-    out_ref[0] = inner_rows(key_rows, (backward * up_pre * derivative).astype(BF16))
-
-
-def attend_kernel(q_ref, k_ref, v_ref, prev_ref, gate_ref, up_ref, down_ref, out_ref, square_ref):
+    d_gate = (backward * up_pre * derivative).astype(BF16)
+    d_up = (backward * activated).astype(BF16)
+
+    def put(matrix, product):
+        for chunk in range(CHUNKS):
+            start = 2 * chunk * half
+            sent_refs[chunk][matrix] = product[start : start + half].astype(BF16)
+            kept_refs[chunk][matrix] = product[start + half : start + 2 * half]
+
+    ordered = order_ref[...]
+    put(0, inner_rows(ordered, d_gate))
+    put(1, inner_rows(ordered, d_up))
+    for at, place in enumerate(places):
+        order_ref[:, at * half : (at + 1) * half] = hidden_ref[:, place]
+    put(2, inner_rows(order_ref[...], target))
+
+
+def fold_kernel(step, *refs):
+    sent_ref, next_ref = refs[-2:]
+    kept_refs, came_refs = refs[: len(refs) // 2 - 1], refs[len(refs) // 2 - 1 : -2]
+    half = sent_ref.shape[1] // len(kept_refs)
+    bit = bit_here(step)
+    for at, (kept_ref, came_ref) in enumerate(zip(kept_refs, came_refs)):
+        there = slice(at * half, (at + 1) * half)
+        for which, ref in ((1 - bit, sent_ref), (bit, next_ref)):
+            rows = pl.ds(pl.multiple_of(which * half, half), half)
+            ref[:, there] = (kept_ref[:, rows] + came_ref[:, rows].astype(F32)).astype(ref.dtype)
+
+
+def fold(step, kept, came):
+    rows = sum(k.shape[1] // 2 for k in kept)
+    shape = (kept[0].shape[0], rows, kept[0].shape[2])
+    size = shape[0] * shape[1] * shape[2]
+    return kernel_call(
+        functools.partial(fold_kernel, step),
+        "fold",
+        (jax.ShapeDtypeStruct(shape, BF16), jax.ShapeDtypeStruct(shape, F32)),
+        2 * size,
+        18 * size,
+    )(*kept, *came)
+
+
+def attend_kernel(q_ref, k_ref, v_ref, prev_k_ref, prev_v_ref, gate_ref, up_ref, down_ref, out_ref, square_ref):
     rows = q_ref.shape[0]
     reach = WINDOW // BLOCK
     row_at = lax.broadcasted_iota(jnp.int32, (BLOCK, BLOCK), 0)
@@ -116,7 +211,7 @@
             for other in range(block - reach, block + 1):
                 if other < 0:
                     there = slice((other + reach) * BLOCK, (other + reach + 1) * BLOCK)
-                    key, value = prev_ref[0, there, cols], prev_ref[1, there, cols]
+                    key, value = prev_k_ref[there, cols], prev_v_ref[there, cols]
                 else:
                     there = slice(other * BLOCK, (other + 1) * BLOCK)
                     key, value = k_ref[there, cols], v_ref[there, cols]
@@ -135,7 +230,7 @@
 
 
 def apply_kernel(steps, part_rows, *refs):
-    count = 2 * CHUNKS if steps else CHUNKS
+    count = 2 * CHUNKS
     pieces, refs = refs[:count], refs[count:]
     q_ref, gate_ref, up_ref, down_ref, square_ref, attended_ref = refs[:6]
     combined_ref, sums_ref, next_gate_ref, next_up_ref, next_down_ref = refs[6:11]
@@ -153,11 +248,6 @@
         grad_rms = jnp.sqrt(jnp.sum(total, keepdims=True) / size + EPSILON)
         weight_rms = jnp.sqrt(jnp.sum(square_ref[at], keepdims=True) / size)
         factor = ETA_STEP * weight_rms / grad_rms
-        if not steps:
-            for chunk, piece in enumerate(pieces):
-                here = slice(chunk * chunk_rows, (chunk + 1) * chunk_rows)
-                new_ref[here] = (old_ref[here].astype(F32) + factor * piece[at].astype(F32)).astype(BF16)
-            continue
         unit = chunk_rows >> len(steps)
         for chunk in range(CHUNKS):
             for arrived in range(2):
@@ -201,45 +291,70 @@
     w_rows, w_cols = w_gate.shape
     weights = (w_gate, w_up, w_down)
 
-    tail = jnp.stack([keys, values])[:, tok_rows - WINDOW :]
-    prev = lax.ppermute(tail, "seq", [(i, i + 1) for i in range(seq_count - 1)])
-
-    grads = kernel_call(
-        grads_kernel,
-        "gradients",
-        jax.ShapeDtypeStruct((3, w_rows, w_cols), F32),
-        12 * tok_rows * fw_dim * w_cols,
-        8 * tok_rows * fw_dim,
-    )(keys, values, rates.reshape(1, tok_rows), *weights)
+    hbm = pl.BlockSpec(memory_space=pltpu.HBM)
+    tail_shape = jax.ShapeDtypeStruct((WINDOW, fw_dim), BF16)
+    value_tail, key_tail = pl.pallas_call(
+        tails_kernel,
+        out_shape=(tail_shape, tail_shape),
+        in_specs=[hbm, hbm],
+        out_specs=(hbm, hbm),
+        name="tails",
+        scratch_shapes=[
+            pltpu.VMEM((WINDOW, fw_dim), BF16),
+            pltpu.VMEM((WINDOW, fw_dim), BF16),
+            pltpu.SemaphoreType.DMA((2, 4 * WINDOW // BLOCK)),
+        ],
+        compiler_params=pltpu.CompilerParams(vmem_limit_bytes=VMEM_WHOLE),
+    )(values, keys)
+    prev_keys, passed = shift_tail(key_tail), pass_odd(value_tail)
 
     chunk_rows = w_rows // CHUNKS
-    steps = halving_masks(seq_count, chunk_rows)
-    chunks = [grads[:, c * chunk_rows : (c + 1) * chunk_rows] for c in range(CHUNKS)]
-    for masks in steps:
-        bit = bit_here(masks)
-        halves = []
-        for g in chunks:
-            half = g.shape[1] // 2
-            kept = lax.dynamic_slice_in_dim(g, bit * half, half, 1)
-            sent = lax.dynamic_slice_in_dim(g, (1 - bit) * half, half, 1).astype(BF16)
-            halves.append(kept + swap(sent, masks).astype(F32))
-        chunks = halves
-    if 1 << len(steps) < seq_count:
-        used = 0
-        for masks in steps:
-            used |= masks[0]
-        groups = {}
-        for s in range(seq_count):
-            groups.setdefault(s & used, []).append(s)
-        chunks = [lax.psum(g, "seq", axis_index_groups=list(groups.values())) for g in chunks]
-    chunks = [g.astype(BF16) for g in chunks]
-    for masks in steps[:0:-1]:
-        chunks = [jnp.concatenate([g, swap(g, masks)], axis=1) for g in chunks]
+    steps, others = exchange_masks(seq_count)
+    half = chunk_rows // 2
+    parts = pl.pallas_call(
+        functools.partial(grads_kernel, steps[0]),
+        out_shape=[jax.ShapeDtypeStruct((3, half, w_cols), BF16)] * CHUNKS
+        + [jax.ShapeDtypeStruct((3, half, w_cols), F32)] * CHUNKS,
+        in_specs=[hbm] * 5 + [pl.BlockSpec(memory_space=pltpu.VMEM)],
+        name="gradients",
+        scratch_shapes=[
+            pltpu.VMEM(keys.shape, BF16),
+            pltpu.VMEM(values.shape, BF16),
+            pltpu.VMEM(w_gate.shape, BF16),
+            pltpu.VMEM(w_up.shape, BF16),
+            pltpu.VMEM(w_down.shape, BF16),
+            pltpu.VMEM(keys.shape, BF16),
+            pltpu.VMEM((tok_rows, w_cols), BF16),
+            pltpu.SemaphoreType.DMA((5,)),
+        ],
+        compiler_params=pltpu.CompilerParams(vmem_limit_bytes=VMEM_WHOLE),
+        cost_estimate=pl.CostEstimate(
+            flops=12 * tok_rows * fw_dim * w_cols,
+            bytes_accessed=16 * tok_rows * fw_dim,
+            transcendentals=0,
+        ),
+    )(keys, values, *weights, rates.reshape(1, tok_rows))
+    sent, kept = parts[:CHUNKS], parts[CHUNKS:]
+    came = [swap(x, steps[0]) for x in sent]
+    came[0], prev_keys, passed = lax.optimization_barrier((came[0], prev_keys, passed))
+    prev_values = shift_passed(value_tail, passed)
+    folded = [fold(steps[1], [k], [c]) for k, c in zip(kept, came)]
+    came = [swap(x, steps[1]) for x, _ in folded]
+    sent, kept = fold(steps[2], [k for _, k in folded], came)
+    came, prev_values = lax.optimization_barrier((swap(sent, steps[2]), prev_values))
+    total = kept + came.astype(F32)
+    for masks in others:
+        total = total.astype(BF16)
+        total = total.astype(F32) + swap(total, masks).astype(F32)
+    total = total.astype(BF16)
+    more = swap(total, steps[2])
+    rows = total.shape[1] // CHUNKS
     pieces = []
-    for g in chunks:
-        pieces.append(g)
-        if steps:
-            pieces.append(swap(g, steps[0]))
+    for c in range(CHUNKS):
+        here = slice(c * rows, (c + 1) * rows)
+        piece = jnp.concatenate([total[:, here], more[:, here]], axis=1)
+        piece = jnp.concatenate([piece, swap(piece, steps[1])], axis=1)
+        pieces += [piece, swap(piece, steps[0])]
 
     attended, squares = kernel_call(
         attend_kernel,
@@ -250,7 +365,7 @@
         ),
         4 * tok_rows * (WINDOW + BLOCK) * fw_dim,
         8 * tok_rows * fw_dim,
-    )(queries, keys, values, prev, *weights)
+    )(queries, keys, values, prev_keys, prev_values, *weights)
 
     part_rows = w_rows // seq_count
     kept_rows = max(part_rows, SUBROWS)

time: 104 us -> 89.9 us (0.86)
  the two profiles are of different devices: /device:TPU:17 before, /device:TPU:0 now
where the time goes in v2:
time: 89.9 us; the launch traced here: 89.7 us
  waiting for transfers between devices  38.7 us (43%)
  starting transfers between devices  30.4 us (34%)
  Pallas kernels  19.4 us (22%)
    ppermute x11, waiting for transfers between devices, swap(): return lax.ppermute(x, ('seq', 'head'), pairs)  37.5 us
    ppermute x11, starting transfers between devices, swap(): return lax.ppermute(x, ('seq', 'head'), pairs)  16.6 us
    ppermute x1, starting transfers between devices, shift_passed(): return lax.ppermute(jnp.where(odd, passed, x), 'seq', pairs)  7.42 us
    pallas_call x1, Pallas kernels, body(): pl.pallas_call(functools.partial(grads_kernel, steps[0]), out_shape=[jax....  7.32 us
    pallas_call x1, Pallas kernels, body(): kernel_call(attend_kernel, 'window_attention', (jax.ShapeDtypeStruct((tok...  5 us
    ppermute x1, starting transfers between devices, shift_tail(): lax.ppermute(x, 'seq', [(i, i + 1) for i in range(lax.axis_size('seq') -...  4.87 us
    pallas_call x1, Pallas kernels, body(): pl.pallas_call(functools.partial(apply_kernel, steps, part_rows), out_sha...  3.49 us
    pallas_call x1, Pallas kernels, body(): pl.pallas_call(tails_kernel, out_shape=(tail_shape, tail_shape), in_specs...  2.13 us
  transfers between devices with their start and end apart: 15, of which 10 were waited for; matrix products, arithmetic and copies ran while one was open for 0% of the time, Pallas kernels for 14%

profile of v2, /device:TPU:0, one launch (start us, length us, event | category | flops | bytes accessed | tf_op | source)
XLA Modules:
  0.0 89.7 jit_solution(15721069945621146380)
XLA Ops:
  0.6 2.1 %tails.1 = (bf16[512,512]{1,0:T(8,128)(2,1)}, bf16[512,512]{1,0:T(8,128)(2,1)}) custom-call(bf16[768,512]{1,0:T(8,128)(2,1)} %v_ref.1, bf16[768,512]{1,0:T(8,128)(2,1)} %k_ref.1), custom_call_target="tpu_custom_call" | custom-call | tf_op jit(solution)/shard_map/tails/pallas_call | solution.py:296
  2.8 4.9 %collective-permute-start.1 = (bf16[512,512]{1,0:T(8,128)(2,1)}, bf16[512,512]{1,0:T(8,128)(2,1)S(1)}, u32[]{:S(2)}, u32[]{:S(2)}) collective-permute-start(bf16[512,512]{1,0:T(8,128)(2,1)} %get-tuple-element.30), channel_id=1, source_target_pairs={{0,2},{2,4},{4,6},{6,8},{8,10},{10,12},{12,14},{14,16},{16,18},{18... | collective-permute-start | bytes 1572872 | tf_op jit(solution)/shard_map/ppermute | solution.py:96
  7.6 1.5 %collective-permute-start.2 = (bf16[512,512]{1,0:T(8,128)(2,1)}, bf16[512,512]{1,0:T(8,128)(2,1)}, u32[]{:S(2)}, u32[]{:S(2)}) collective-permute-start(bf16[512,512]{1,0:T(8,128)(2,1)} %get-tuple-element.31), channel_id=1, source_target_pairs={{2,6},{6,2},{10,14},{14,10},{18,22},{22,18},{26,30},{30,26},{3,7},... | collective-permute-start | bytes 1572872 | tf_op jit(solution)/shard_map/ppermute | solution.py:100
  9.1 7.3 %gradients.1 = (bf16[3,128,512]{2,1,0:T(8,128)(2,1)}, bf16[3,128,512]{2,1,0:T(8,128)(2,1)}, f32[3,128,512]{2,1,0:T(8,128)}, f32[3,128,512]{2,1,0:T(8,128)}) custom-call(bf16[768,512]{1,0:T(8,128)(2,1)} %k_ref.1, bf16[768,512]{1,0:T(8,128)(2,1)} %v_ref.1, bf16[512,512]{1,0:T(8,128)(2,1)} %refs_5_.1, bf16[512,512]{1,0:T(8,128)(2,1)} %refs_6_.1, ...), custom_call_target="tpu_custom_call" | custom-call | flops 2415919104 | bytes 6291456 | tf_op jit(solution)/shard_map/gradients/pallas_call | solution.py:314
  16.5 1.6 %collective-permute-start = (bf16[3,128,512]{2,1,0:T(8,128)(2,1)}, bf16[3,128,512]{2,1,0:T(8,128)(2,1)S(1)}, u32[]{:S(2)}, u32[]{:S(2)}) collective-permute-start(bf16[3,128,512]{2,1,0:T(8,128)(2,1)} %get-tuple-element.29), channel_id=1, source_target_pairs={{0,4},{1,9},{2,6},{3,11},{4,0},{5,13},{6,2},{7,15},{8,12},{9,1},{1... | collective-permute-start | bytes 1179656 | tf_op jit(solution)/shard_map/ppermute | solution.py:73
  18.0 0.5 collective-permute-start.3
  18.6 6.0 %collective-permute-done.refs_1_ = bf16[3,128,512]{2,1,0:T(8,128)(2,1)S(1)} collective-permute-done((bf16[3,128,512]{2,1,0:T(8,128)(2,1)}, bf16[3,128,512]{2,1,0:T(8,128)(2,1)S(1)}, u32[]{:S(2)}, u32[]{:S(2)}) %collective-permute-start) | collective-permute-done | bytes 393248 | tf_op jit(solution)/shard_map/ppermute | solution.py:73
  24.6 0.1 broadcast_select_fusion
  24.6 7.4 %collective-permute-start.7 = (bf16[512,512]{1,0:T(8,128)(2,1)S(1)}, bf16[512,512]{1,0:T(8,128)(2,1)S(1)}, u32[]{:S(2)}, u32[]{:S(2)}) collective-permute-start(bf16[512,512]{1,0:T(8,128)(2,1)S(1)} %broadcast_select_fusion), channel_id=1, source_target_pairs={{0,2},{4,6},{8,10},{12,14},{16,18},{20,22},{24,26},{28,30},{2,8},{... | collective-permute-start | bytes 1572872 | tf_op jit(solution)/shard_map/ppermute | solution.py:108
  32.1 0.1 fold.4
  32.2 1.6 %collective-permute-start.5 = (bf16[3,64,512]{2,1,0:T(8,128)(2,1)S(1)}, bf16[3,64,512]{2,1,0:T(8,128)(2,1)S(1)}, u32[]{:S(2)}, u32[]{:S(2)}) collective-permute-start(bf16[3,64,512]{2,1,0:T(8,128)(2,1)S(1)} %get-tuple-element.38), channel_id=1, source_target_pairs={{0,8},{1,5},{2,10},{3,7},{4,12},{5,1},{6,14},{7,3},{8,0},{9,13},{1... | collective-permute-start | bytes 589832 | tf_op jit(solution)/shard_map/ppermute | solution.py:73
  33.8 0.1 fold.3
  33.9 0.5 collective-permute-start.4
  34.4 3.5 %collective-permute-done.5.refs_3_ = bf16[3,64,512]{2,1,0:T(8,128)(2,1)S(1)} collective-permute-done((bf16[3,64,512]{2,1,0:T(8,128)(2,1)S(1)}, bf16[3,64,512]{2,1,0:T(8,128)(2,1)S(1)}, u32[]{:S(2)}, u32[]{:S(2)}) %collective-permute-start.5) | collective-permute-done | bytes 196640 | tf_op jit(solution)/shard_map/ppermute | solution.py:73
  37.9 2.1 %collective-permute-done.4.refs_2_ = bf16[3,64,512]{2,1,0:T(8,128)(2,1)S(1)} collective-permute-done((bf16[3,64,512]{2,1,0:T(8,128)(2,1)S(1)}, bf16[3,64,512]{2,1,0:T(8,128)(2,1)S(1)}, u32[]{:S(2)}, u32[]{:S(2)}) %collective-permute-start.4) | collective-permute-done | bytes 196640 | tf_op jit(solution)/shard_map/ppermute | solution.py:73
  40.1 5.3 %collective-permute-start.6 = (bf16[3,64,512]{2,1,0:T(8,128)(2,1)S(1)}, bf16[3,64,512]{2,1,0:T(8,128)(2,1)S(1)}, u32[]{:S(2)}, u32[]{:S(2)}) collective-permute-start(bf16[3,64,512]{2,1,0:T(8,128)(2,1)S(1)} %get-tuple-element.40), channel_id=1, source_target_pairs={{0,2},{1,3},{2,0},{3,1},{4,6},{5,7},{6,4},{7,5},{8,10},{9,11},{10,... | collective-permute-start | bytes 589832 | tf_op jit(solution)/shard_map/ppermute | solution.py:73
  45.4 3.6 %collective-permute-done.6 = bf16[3,64,512]{2,1,0:T(8,128)(2,1)S(1)} collective-permute-done((bf16[3,64,512]{2,1,0:T(8,128)(2,1)S(1)}, bf16[3,64,512]{2,1,0:T(8,128)(2,1)S(1)}, u32[]{:S(2)}, u32[]{:S(2)}) %collective-permute-start.6) | collective-permute-done | bytes 196640 | tf_op jit(solution)/shard_map/ppermute | solution.py:73
  49.1 2.7 %collective-permute-start.8 = (bf16[3,64,512]{2,1,0:T(8,128)(2,1)S(1)}, bf16[3,64,512]{2,1,0:T(8,128)(2,1)S(1)}, u32[]{:S(2)}, u32[]{:S(2)}) collective-permute-start(bf16[3,64,512]{2,1,0:T(8,128)(2,1)S(1)} %add_convert_fusion.1), channel_id=1, source_target_pairs={{0,16},{1,17},{2,18},{3,19},{4,20},{5,21},{6,22},{7,23},{8,24},{9,... | collective-permute-start | bytes 589832 | tf_op jit(solution)/shard_map/ppermute | solution.py:73
  51.8 6.1 %collective-permute-done.8 = bf16[3,64,512]{2,1,0:T(8,128)(2,1)S(1)} collective-permute-done((bf16[3,64,512]{2,1,0:T(8,128)(2,1)S(1)}, bf16[3,64,512]{2,1,0:T(8,128)(2,1)S(1)}, u32[]{:S(2)}, u32[]{:S(2)}) %collective-permute-start.8) | collective-permute-done | bytes 196640 | tf_op jit(solution)/shard_map/ppermute | solution.py:73
  58.0 2.1 %collective-permute-start.9 = (bf16[3,64,512]{2,1,0:T(8,128)(2,1)S(1)}, bf16[3,64,512]{2,1,0:T(8,128)(2,1)S(1)}, u32[]{:S(2)}, u32[]{:S(2)}) collective-permute-start(bf16[3,64,512]{2,1,0:T(8,128)(2,1)S(1)} %add_convert_fusion), channel_id=1, source_target_pairs={{0,2},{1,3},{2,0},{3,1},{4,6},{5,7},{6,4},{7,5},{8,10},{9,11},{10,... | collective-permute-start | bytes 589832 | tf_op jit(solution)/shard_map/ppermute | solution.py:73
  60.1 3.6 %collective-permute-done.9 = bf16[3,64,512]{2,1,0:T(8,128)(2,1)S(1)} collective-permute-done((bf16[3,64,512]{2,1,0:T(8,128)(2,1)S(1)}, bf16[3,64,512]{2,1,0:T(8,128)(2,1)S(1)}, u32[]{:S(2)}, u32[]{:S(2)}) %collective-permute-start.9) | collective-permute-done | bytes 196640 | tf_op jit(solution)/shard_map/ppermute | solution.py:73
  63.8 0.7 collective-permute-start.12
  64.5 1.4 %collective-permute-start.10 = (bf16[3,64,512]{2,1,0:T(8,128)(2,1)S(1)}, bf16[3,64,512]{2,1,0:T(8,128)(2,1)S(1)}, u32[]{:S(2)}, u32[]{:S(2)}) collective-permute-start(bf16[3,64,512]{2,1,0:T(8,128)(2,1)S(1)} %pad_maximum_fusion.2), channel_id=1, source_target_pairs={{0,8},{1,5},{2,10},{3,7},{4,12},{5,1},{6,14},{7,3},{8,0},{9,13},{1... | collective-permute-start | bytes 589832 | tf_op jit(solution)/shard_map/ppermute | solution.py:73
  65.9 5.7 %collective-permute-done.12 = bf16[3,64,512]{2,1,0:T(8,128)(2,1)S(1)} collective-permute-done((bf16[3,64,512]{2,1,0:T(8,128)(2,1)S(1)}, bf16[3,64,512]{2,1,0:T(8,128)(2,1)S(1)}, u32[]{:S(2)}, u32[]{:S(2)}) %collective-permute-start.12) | collective-permute-done | bytes 196640 | tf_op jit(solution)/shard_map/ppermute | solution.py:73
  71.7 0.1 collective-permute-start.13
  71.8 4.1 %collective-permute-done.10 = bf16[3,64,512]{2,1,0:T(8,128)(2,1)S(1)} collective-permute-done((bf16[3,64,512]{2,1,0:T(8,128)(2,1)S(1)}, bf16[3,64,512]{2,1,0:T(8,128)(2,1)S(1)}, u32[]{:S(2)}, u32[]{:S(2)}) %collective-permute-start.10) | collective-permute-done | bytes 196640 | tf_op jit(solution)/shard_map/ppermute | solution.py:73
  75.9 0.1 collective-permute-start.11
  76.0 5.0 %window_attention.1 = (f32[768,512]{1,0:T(8,128)S(1)}, f32[3,8,512]{2,1,0:T(8,128)S(1)}) custom-call(bf16[768,512]{1,0:T(8,128)(2,1)S(1)} %copy-done.2, bf16[768,512]{1,0:T(8,128)(2,1)S(1)} %copy-done, bf16[768,512]{1,0:T(8,128)(2,1)S(1)} %copy-done.1, bf16[512,512]{1,0:T(8,128)(2,1)S(1)} %collective-permute-done.1.prev_k_ref, ...), custom_call_target="tpu_custom_call" | custom-call | flops 1207959552 | bytes 3145728 | tf_op jit(solution)/shard_map/window_attention/pallas_call | solution.py:359
  81.1 2.7 %collective-permute-done.11.refs_1_ = bf16[3,128,512]{2,1,0:T(8,128)(2,1)S(1)} collective-permute-done((bf16[3,128,512]{2,1,0:T(8,128)(2,1)S(1)}, bf16[3,128,512]{2,1,0:T(8,128)(2,1)S(1)}, u32[]{:S(2)}, u32[]{:S(2)}) %collective-permute-start.11) | collective-permute-done | bytes 393248 | tf_op jit(solution)/shard_map/ppermute | solution.py:73
  83.8 3.5 %apply.1 = (f32[768,512]{1,0:T(8,128)S(1)}, f32[8,768]{1,0:T(8,128)S(1)}, bf16[32,512]{1,0:T(8,128)(2,1)}, bf16[32,512]{1,0:T(8,128)(2,1)}, bf16[32,512]{1,0:T(8,128)(2,1)}) custom-call(bf16[3,128,512]{2,1,0:T(8,128)(2,1)S(1)} %pad_maximum_fusion.refs_0_, bf16[3,128,512]{2,1,0:T(8,128)(2,1)S(1)} %collective-permute-done.11.refs_1_, ...), custom_call_target="tpu_custom_call" | custom-call | flops 1207959552 | bytes 4718592 | tf_op jit(solution)/shard_map/apply/pallas_call | solution.py:373
  87.2 1.2 %collective-permute-done.14.more_ref = f32[8,768]{1,0:T(8,128)S(1)} collective-permute-done((f32[8,768]{1,0:T(8,128)S(1)}, f32[8,768]{1,0:T(8,128)S(1)}, u32[]{:S(2)}, u32[]{:S(2)}) %collective-permute-start.14) | collective-permute-done | bytes 24608 | tf_op jit(solution)/shard_map/ppermute | solution.py:397
  88.4 1.2 %norm.1 = bf16[768,512]{1,0:T(8,128)(2,1)} custom-call(f32[768,512]{1,0:T(8,128)S(1)} %get-tuple-element.47.combined_ref, f32[8,768]{1,0:T(8,128)S(1)} %get-tuple-element.48.sums_ref, f32[8,768]{1,0:T(8,128)S(1)} %collective-permute-done.14.more_ref, f32[1,512]{1,0:T(1,128)S(1)} %bitcast.2), custom_call_target="tpu_custom_call" | custom-call | flops 1572864 | bytes 2359296 | tf_op jit(solution)/shard_map/norm/pallas_call | solution.py:405
  (35 shorter events, 0.3 us)
Async XLA Ops:
  2.8 21.8 %collective-permute-start.1 = (bf16[512,512]{1,0:T(8,128)(2,1)}, bf16[512,512]{1,0:T(8,128)(2,1)S(1)}, u32[]{:S(2)}, u32[]{:S(2)}) collective-permute-start(bf16[512,512]{1,0:T(8,128)(2,1)} %get-tuple-element.30), channel_id=1, source_target_pairs={{0,2},{2,4},{4,6},{6,8},{8,10},{10,12},{12,14},{14,16},{16,18},{18... | collective-permute-start | bytes 1572872 | tf_op jit(solution)/shard_map/ppermute | solution.py:96
  7.6 16.9 %collective-permute-start.2 = (bf16[512,512]{1,0:T(8,128)(2,1)}, bf16[512,512]{1,0:T(8,128)(2,1)}, u32[]{:S(2)}, u32[]{:S(2)}) collective-permute-start(bf16[512,512]{1,0:T(8,128)(2,1)} %get-tuple-element.31), channel_id=1, source_target_pairs={{2,6},{6,2},{10,14},{14,10},{18,22},{22,18},{26,30},{30,26},{3,7},... | collective-permute-start | bytes 1572872 | tf_op jit(solution)/shard_map/ppermute | solution.py:100
  9.1 15.4 %copy-start.9 = (bf16[512,512]{1,0:T(8,128)(2,1)S(1)}, bf16[512,512]{1,0:T(8,128)(2,1)}, u32[]{:S(2)}) copy-start(bf16[512,512]{1,0:T(8,128)(2,1)} %get-tuple-element.31) | copy-start | bytes 1572868
  16.5 15.6 %copy-start.7 = (f32[3,128,512]{2,1,0:T(8,128)S(1)}, f32[3,128,512]{2,1,0:T(8,128)}, u32[]{:S(2)}) copy-start(f32[3,128,512]{2,1,0:T(8,128)} %get-tuple-element.34.refs_0_) | copy-start | bytes 2359300
  16.5 17.3 %copy-start.6 = (f32[3,128,512]{2,1,0:T(8,128)S(1)}, f32[3,128,512]{2,1,0:T(8,128)}, u32[]{:S(2)}) copy-start(f32[3,128,512]{2,1,0:T(8,128)} %get-tuple-element.28.refs_0_) | copy-start | bytes 2359300
  16.5 8.1 %collective-permute-start = (bf16[3,128,512]{2,1,0:T(8,128)(2,1)}, bf16[3,128,512]{2,1,0:T(8,128)(2,1)S(1)}, u32[]{:S(2)}, u32[]{:S(2)}) collective-permute-start(bf16[3,128,512]{2,1,0:T(8,128)(2,1)} %get-tuple-element.29), channel_id=1, source_target_pairs={{0,4},{1,9},{2,6},{3,11},{4,0},{5,13},{6,2},{7,15},{8,12},{9,1},{1... | collective-permute-start | bytes 1179656 | tf_op jit(solution)/shard_map/ppermute | solution.py:73
  18.0 14.0 %collective-permute-start.3 = (bf16[3,128,512]{2,1,0:T(8,128)(2,1)}, bf16[3,128,512]{2,1,0:T(8,128)(2,1)S(1)}, u32[]{:S(2)}, u32[]{:S(2)}) collective-permute-start(bf16[3,128,512]{2,1,0:T(8,128)(2,1)} %get-tuple-element.35), channel_id=1, source_target_pairs={{0,4},{1,9},{2,6},{3,11},{4,0},{5,13},{6,2},{7,15},{8,12},{9,1},{1... | collective-permute-start | bytes 1179656 | tf_op jit(solution)/shard_map/ppermute | solution.py:73
  24.6 24.4 %collective-permute-start.7 = (bf16[512,512]{1,0:T(8,128)(2,1)S(1)}, bf16[512,512]{1,0:T(8,128)(2,1)S(1)}, u32[]{:S(2)}, u32[]{:S(2)}) collective-permute-start(bf16[512,512]{1,0:T(8,128)(2,1)S(1)} %broadcast_select_fusion), channel_id=1, source_target_pairs={{0,2},{4,6},{8,10},{12,14},{16,18},{20,22},{24,26},{28,30},{2,8},{... | collective-permute-start | bytes 1572872 | tf_op jit(solution)/shard_map/ppermute | solution.py:108
  32.2 5.7 %collective-permute-start.5 = (bf16[3,64,512]{2,1,0:T(8,128)(2,1)S(1)}, bf16[3,64,512]{2,1,0:T(8,128)(2,1)S(1)}, u32[]{:S(2)}, u32[]{:S(2)}) collective-permute-start(bf16[3,64,512]{2,1,0:T(8,128)(2,1)S(1)} %get-tuple-element.38), channel_id=1, source_target_pairs={{0,8},{1,5},{2,10},{3,7},{4,12},{5,1},{6,14},{7,3},{8,0},{9,13},{1... | collective-permute-start | bytes 589832 | tf_op jit(solution)/shard_map/ppermute | solution.py:73
  33.9 6.2 %collective-permute-start.4 = (bf16[3,64,512]{2,1,0:T(8,128)(2,1)S(1)}, bf16[3,64,512]{2,1,0:T(8,128)(2,1)S(1)}, u32[]{:S(2)}, u32[]{:S(2)}) collective-permute-start(bf16[3,64,512]{2,1,0:T(8,128)(2,1)S(1)} %get-tuple-element.37), channel_id=1, source_target_pairs={{0,8},{1,5},{2,10},{3,7},{4,12},{5,1},{6,14},{7,3},{8,0},{9,13},{1... | collective-permute-start | bytes 589832 | tf_op jit(solution)/shard_map/ppermute | solution.py:73
  40.1 9.0 %collective-permute-start.6 = (bf16[3,64,512]{2,1,0:T(8,128)(2,1)S(1)}, bf16[3,64,512]{2,1,0:T(8,128)(2,1)S(1)}, u32[]{:S(2)}, u32[]{:S(2)}) collective-permute-start(bf16[3,64,512]{2,1,0:T(8,128)(2,1)S(1)} %get-tuple-element.40), channel_id=1, source_target_pairs={{0,2},{1,3},{2,0},{3,1},{4,6},{5,7},{6,4},{7,5},{8,10},{9,11},{10,... | collective-permute-start | bytes 589832 | tf_op jit(solution)/shard_map/ppermute | solution.py:73
  49.1 26.9 %copy-start.5 = (bf16[512,512]{1,0:T(8,128)(2,1)S(1)}, bf16[512,512]{1,0:T(8,128)(2,1)}, u32[]{:S(2)}) copy-start(bf16[512,512]{1,0:T(8,128)(2,1)} %refs_7_.1) | copy-start | bytes 1572868
  49.1 8.7 %collective-permute-start.8 = (bf16[3,64,512]{2,1,0:T(8,128)(2,1)S(1)}, bf16[3,64,512]{2,1,0:T(8,128)(2,1)S(1)}, u32[]{:S(2)}, u32[]{:S(2)}) collective-permute-start(bf16[3,64,512]{2,1,0:T(8,128)(2,1)S(1)} %add_convert_fusion.1), channel_id=1, source_target_pairs={{0,16},{1,17},{2,18},{3,19},{4,20},{5,21},{6,22},{7,23},{8,24},{9,... | collective-permute-start | bytes 589832 | tf_op jit(solution)/shard_map/ppermute | solution.py:73
  57.9 18.1 %copy-start.4 = (bf16[512,512]{1,0:T(8,128)(2,1)S(1)}, bf16[512,512]{1,0:T(8,128)(2,1)}, u32[]{:S(2)}) copy-start(bf16[512,512]{1,0:T(8,128)(2,1)} %refs_6_.1) | copy-start | bytes 1572868
  57.9 18.1 %copy-start = (bf16[768,512]{1,0:T(8,128)(2,1)S(1)}, bf16[768,512]{1,0:T(8,128)(2,1)}, u32[]{:S(2)}) copy-start(bf16[768,512]{1,0:T(8,128)(2,1)} %k_ref.1) | copy-start | bytes 2359300
  57.9 18.1 %copy-start.1 = (bf16[768,512]{1,0:T(8,128)(2,1)S(1)}, bf16[768,512]{1,0:T(8,128)(2,1)}, u32[]{:S(2)}) copy-start(bf16[768,512]{1,0:T(8,128)(2,1)} %v_ref.1) | copy-start | bytes 2359300
  58.0 18.1 %copy-start.2 = (bf16[768,512]{1,0:T(8,128)(2,1)S(1)}, bf16[768,512]{1,0:T(8,128)(2,1)}, u32[]{:S(2)}) copy-start(bf16[768,512]{1,0:T(8,128)(2,1)} %refs_4_.3) | copy-start | bytes 2359300
  58.0 18.1 %copy-start.3 = (bf16[512,512]{1,0:T(8,128)(2,1)S(1)}, bf16[512,512]{1,0:T(8,128)(2,1)}, u32[]{:S(2)}) copy-start(bf16[512,512]{1,0:T(8,128)(2,1)} %refs_5_.1) | copy-start | bytes 1572868
  58.0 5.7 %collective-permute-start.9 = (bf16[3,64,512]{2,1,0:T(8,128)(2,1)S(1)}, bf16[3,64,512]{2,1,0:T(8,128)(2,1)S(1)}, u32[]{:S(2)}, u32[]{:S(2)}) collective-permute-start(bf16[3,64,512]{2,1,0:T(8,128)(2,1)S(1)} %add_convert_fusion), channel_id=1, source_target_pairs={{0,2},{1,3},{2,0},{3,1},{4,6},{5,7},{6,4},{7,5},{8,10},{9,11},{10,... | collective-permute-start | bytes 589832 | tf_op jit(solution)/shard_map/ppermute | solution.py:73
  63.8 7.9 %collective-permute-start.12 = (bf16[3,64,512]{2,1,0:T(8,128)(2,1)S(1)}, bf16[3,64,512]{2,1,0:T(8,128)(2,1)S(1)}, u32[]{:S(2)}, u32[]{:S(2)}) collective-permute-start(bf16[3,64,512]{2,1,0:T(8,128)(2,1)S(1)} %pad_maximum_fusion.3), channel_id=1, source_target_pairs={{0,8},{1,5},{2,10},{3,7},{4,12},{5,1},{6,14},{7,3},{8,0},{9,13},{1... | collective-permute-start | bytes 589832 | tf_op jit(solution)/shard_map/ppermute | solution.py:73
  64.5 11.4 %collective-permute-start.10 = (bf16[3,64,512]{2,1,0:T(8,128)(2,1)S(1)}, bf16[3,64,512]{2,1,0:T(8,128)(2,1)S(1)}, u32[]{:S(2)}, u32[]{:S(2)}) collective-permute-start(bf16[3,64,512]{2,1,0:T(8,128)(2,1)S(1)} %pad_maximum_fusion.2), channel_id=1, source_target_pairs={{0,8},{1,5},{2,10},{3,7},{4,12},{5,1},{6,14},{7,3},{8,0},{9,13},{1... | collective-permute-start | bytes 589832 | tf_op jit(solution)/shard_map/ppermute | solution.py:73
  71.7 9.4 %collective-permute-start.13 = (bf16[3,128,512]{2,1,0:T(8,128)(2,1)S(1)}, bf16[3,128,512]{2,1,0:T(8,128)(2,1)S(1)}, u32[]{:S(2)}, u32[]{:S(2)}) collective-permute-start(bf16[3,128,512]{2,1,0:T(8,128)(2,1)S(1)} %pad_maximum_fusion.1.refs_2_), channel_id=1, source_target_pairs={{0,4},{1,9},{2,6},{3,11},{4,0},{5,13},{6,2},{7,15},{8,12},{9,1},{1... | collective-permute-start | bytes 1179656 | tf_op jit(solution)/shard_map/ppermute | solution.py:73
  75.9 7.8 %collective-permute-start.11 = (bf16[3,128,512]{2,1,0:T(8,128)(2,1)S(1)}, bf16[3,128,512]{2,1,0:T(8,128)(2,1)S(1)}, u32[]{:S(2)}, u32[]{:S(2)}) collective-permute-start(bf16[3,128,512]{2,1,0:T(8,128)(2,1)S(1)} %pad_maximum_fusion.refs_0_), channel_id=1, source_target_pairs={{0,4},{1,9},{2,6},{3,11},{4,0},{5,13},{6,2},{7,15},{8,12},{9,1},{1... | collective-permute-start | bytes 1179656 | tf_op jit(solution)/shard_map/ppermute | solution.py:73
  83.7 4.7 %copy-start.8 = (f32[512]{0:T(512)S(1)}, f32[512]{0:T(512)}, u32[]{:S(2)}) copy-start(f32[512]{0:T(512)} %param.15) | copy-start | bytes 6148
  87.2 1.2 %collective-permute-start.14 = (f32[8,768]{1,0:T(8,128)S(1)}, f32[8,768]{1,0:T(8,128)S(1)}, u32[]{:S(2)}, u32[]{:S(2)}) collective-permute-start(f32[8,768]{1,0:T(8,128)S(1)} %get-tuple-element.48.sums_ref), channel_id=1, source_target_pairs={{0,1},{1,0},{2,3},{3,2},{4,5},{5,4},{6,7},{7,6},{8,9},{9,8},{10,11... | collective-permute-start | bytes 73736 | tf_op jit(solution)/shard_map/ppermute | solution.py:397

commit v3 on v2

--- a/solution.py
+++ b/solution.py
@@ -73,99 +73,76 @@
     return lax.ppermute(x, ("seq", "head"), pairs)
 
 
-def tails_kernel(v_hbm, k_hbm, v_out, k_out, v_ref, k_ref, sems):
-    rows = v_ref.shape[0]
-    moves = []
-    for source, held, target in ((v_hbm, v_ref, v_out), (k_hbm, k_ref, k_out)):
-        for start in range(0, rows, BLOCK // 2):
-            here = pl.ds(start, BLOCK // 2)
-            there = pl.ds(source.shape[0] - rows + start, BLOCK // 2)
-            moves.append((source.at[there], held.at[here], target.at[here]))
-    first = [pltpu.make_async_copy(a, b, sems.at[0, i]) for i, (a, b, _) in enumerate(moves)]
-    second = [pltpu.make_async_copy(b, c, sems.at[1, i]) for i, (_, b, c) in enumerate(moves)]
-    for copy in first:
-        copy.start()
-    for copy, after in zip(first, second):
-        copy.wait()
-        after.start()
-    for after in second:
-        after.wait()
-
-
-def shift_tail(x):
-    return lax.ppermute(x, "seq", [(i, i + 1) for i in range(lax.axis_size("seq") - 1)])
-
-
-def pass_odd(x):
-    return lax.ppermute(x, "seq", [(i, i ^ 2) for i in range(1, lax.axis_size("seq"), 2)])
-
-
-def shift_passed(x, passed):
+def trade(x):
     peers = lax.axis_size("seq")
-    odd = lax.axis_index("seq") % 2 == 1
-    pairs = [(i, i + 1) for i in range(0, peers, 2)]
-    pairs += [(i, (i ^ 2) + 1) for i in range(1, peers, 2) if (i ^ 2) + 1 < peers]
-    return lax.ppermute(jnp.where(odd, passed, x), "seq", pairs)
+    return lax.ppermute(x, "seq", [(i, i ^ 1) for i in range(peers)])
+
+
+def pass_on(x):
+    return lax.ppermute(x, "seq", [(i, i + 2) for i in range(0, lax.axis_size("seq") - 2, 2)])
 
 
 def grads_kernel(step, *refs):
-    k_hbm, v_hbm, gate_hbm, up_hbm, down_hbm, rate_ref = refs[:6]
-    sent_refs, kept_refs = refs[6 : 6 + CHUNKS], refs[6 + CHUNKS : 6 + 2 * CHUNKS]
-    k_ref, v_ref, gate_ref, up_ref, down_ref, order_ref, hidden_ref, sems = refs[6 + 2 * CHUNKS :]
-    copies = [
-        pltpu.make_async_copy(source, target, sems.at[at])
-        for at, (source, target) in enumerate(
-            (
-                (k_hbm, k_ref),
-                (gate_hbm, gate_ref),
-                (up_hbm, up_ref),
-                (v_hbm, v_ref),
-                (down_hbm, down_ref),
-            )
-        )
-    ]
+    k_hbm, v_hbm, gate_hbm, up_hbm, down_hbm, rate_ref, *tail_hbms = refs[:8]
+    outs = refs[8 : 8 + 2 * CHUNKS]
+    refs = refs[8 + 2 * CHUNKS :]
+    held, refs = refs[: 2 * CHUNKS], refs[2 * CHUNKS :]
+    k_ref, v_ref, gate_ref, up_ref, down_ref, order_ref, hidden_ref, target_ref, d_gate_ref, d_up_ref = refs[:10]
+    in_sems, tail_sems, out_sems = refs[10:]
+    moves = ((k_hbm, k_ref), (gate_hbm, gate_ref), (up_hbm, up_ref), (v_hbm, v_ref), (down_hbm, down_ref))
+    copies = [pltpu.make_async_copy(a, b, in_sems.at[at]) for at, (a, b) in enumerate(moves)]
     for copy in copies:
         copy.start()
     rows = k_ref.shape[0]
-    half = sent_refs[0].shape[1]
+    half = held[0].shape[1]
     bit = bit_here(step)
     places = []
     for chunk in range(CHUNKS):
-        for which in (1 - bit, bit):
-            start = pl.multiple_of((2 * chunk + which) * half, half)
-            places.append(pl.ds(start, half))
+        for to in (1 - bit, bit):
+            places.append(pl.ds(pl.multiple_of((2 * chunk + to) * half, half), half))
+    tail = pl.ds(rows - WINDOW, WINDOW)
+    tails = [
+        pltpu.make_async_copy(ref.at[tail], tail_hbms[at], tail_sems.at[at])
+        for at, ref in enumerate((k_ref, v_ref))
+    ]
     copies[0].wait()
-    key_rows = k_ref[...]
+    tails[0].start()
     for at, place in enumerate(places):
-        order_ref[:, at * half : (at + 1) * half] = k_ref[:, place]
-    copies[1].wait()
-    gate_pre = dot(key_rows, gate_ref[...])
-    copies[2].wait()
-    up_pre = dot(key_rows, up_ref[...])
-    sigmoid_val = jax.nn.sigmoid(gate_pre)
-    activated = gate_pre * sigmoid_val
-    hidden_ref[...] = (activated * up_pre).astype(BF16)
-    copies[3].wait()
+        order_ref[:, place] = k_ref[:, at * half : (at + 1) * half]
     rate_col = jnp.transpose(jnp.broadcast_to(rate_ref[...], (8, rows)))[:, :1]
-    target = (rate_col * v_ref[...].astype(F32)).astype(BF16)
-    copies[4].wait()
-    backward = outer_cols(target, down_ref[...])
-    derivative = sigmoid_val * (1.0 + gate_pre * (1.0 - sigmoid_val))
-    d_gate = (backward * up_pre * derivative).astype(BF16)
-    d_up = (backward * activated).astype(BF16)
-
-    def put(matrix, product):
+    for copy in copies[1:]:
+        copy.wait()
+    tails[1].start()
+    for start in range(0, rows, BLOCK):
+        here = slice(start, start + BLOCK)
+        gate_pre = dot(k_ref[here], gate_ref[...])
+        up_pre = dot(k_ref[here], up_ref[...])
+        target = (rate_col[here] * v_ref[here].astype(F32)).astype(BF16)
+        target_ref[here] = target
+        backward = outer_cols(target, down_ref[...])
+        sigmoid_val = jax.nn.sigmoid(gate_pre)
+        activated = gate_pre * sigmoid_val
+        hidden = (activated * up_pre).astype(BF16)
+        for at, place in enumerate(places):
+            hidden_ref[here, place] = hidden[:, at * half : (at + 1) * half]
+        d_up_ref[here] = (backward * activated).astype(BF16)
+        derivative = sigmoid_val * (1.0 + gate_pre * (1.0 - sigmoid_val))
+        d_gate_ref[here] = (backward * up_pre * derivative).astype(BF16)
+    results = []
+    for matrix, (left, right) in enumerate(
+        ((order_ref, d_gate_ref), (order_ref, d_up_ref), (hidden_ref, target_ref))
+    ):
+        product = inner_rows(left[...], right[...])
         for chunk in range(CHUNKS):
             start = 2 * chunk * half
-            sent_refs[chunk][matrix] = product[start : start + half].astype(BF16)
-            kept_refs[chunk][matrix] = product[start + half : start + 2 * half]
-
-    ordered = order_ref[...]
-    put(0, inner_rows(ordered, d_gate))
-    put(1, inner_rows(ordered, d_up))
-    for at, place in enumerate(places):
-        order_ref[:, at * half : (at + 1) * half] = hidden_ref[:, place]
-    put(2, inner_rows(order_ref[...], target))
+            held[chunk][matrix] = product[start : start + half].astype(BF16)
+            held[CHUNKS + chunk][matrix] = product[start + half : start + 2 * half]
+        for at in range(2 * CHUNKS):
+            copy = pltpu.make_async_copy(held[at].at[matrix], outs[at].at[matrix], out_sems.at[matrix, at])
+            copy.start()
+            results.append(copy)
+    for copy in tails + results:
+        copy.wait()
 
 
 def fold_kernel(step, *refs):
@@ -193,8 +170,24 @@
     )(*kept, *came)
 
 
-def attend_kernel(q_ref, k_ref, v_ref, prev_k_ref, prev_v_ref, gate_ref, up_ref, down_ref, out_ref, square_ref):
+def attend_kernel(
+    q_ref, k_ref, v_ref, odd_k, odd_v, even_k, even_v, gate_ref, up_ref, down_ref, out_ref, square_ref, prev_ref, sems
+):
     rows = q_ref.shape[0]
+    odd = lax.axis_index("seq") % 2 == 1
+
+    @pl.when(odd)
+    def _():
+        pltpu.make_async_copy(odd_k, prev_ref.at[0], sems.at[0]).start()
+        pltpu.make_async_copy(odd_v, prev_ref.at[1], sems.at[1]).start()
+
+    @pl.when(jnp.logical_not(odd))
+    def _():
+        pltpu.make_async_copy(even_k, prev_ref.at[0], sems.at[0]).start()
+        pltpu.make_async_copy(even_v, prev_ref.at[1], sems.at[1]).start()
+
+    pltpu.make_async_copy(even_k, prev_ref.at[0], sems.at[0]).wait()
+    pltpu.make_async_copy(even_v, prev_ref.at[1], sems.at[1]).wait()
     reach = WINDOW // BLOCK
     row_at = lax.broadcasted_iota(jnp.int32, (BLOCK, BLOCK), 0)
     col_at = lax.broadcasted_iota(jnp.int32, (BLOCK, BLOCK), 1)
@@ -211,7 +204,7 @@
             for other in range(block - reach, block + 1):
                 if other < 0:
                     there = slice((other + reach) * BLOCK, (other + reach + 1) * BLOCK)
-                    key, value = prev_k_ref[there, cols], prev_v_ref[there, cols]
+                    key, value = prev_ref[0, there, cols], prev_ref[1, there, cols]
                 else:
                     there = slice(other * BLOCK, (other + 1) * BLOCK)
                     key, value = k_ref[there, cols], v_ref[there, cols]
@@ -291,33 +284,20 @@
     w_rows, w_cols = w_gate.shape
     weights = (w_gate, w_up, w_down)
 
-    hbm = pl.BlockSpec(memory_space=pltpu.HBM)
-    tail_shape = jax.ShapeDtypeStruct((WINDOW, fw_dim), BF16)
-    value_tail, key_tail = pl.pallas_call(
-        tails_kernel,
-        out_shape=(tail_shape, tail_shape),
-        in_specs=[hbm, hbm],
-        out_specs=(hbm, hbm),
-        name="tails",
-        scratch_shapes=[
-            pltpu.VMEM((WINDOW, fw_dim), BF16),
-            pltpu.VMEM((WINDOW, fw_dim), BF16),
-            pltpu.SemaphoreType.DMA((2, 4 * WINDOW // BLOCK)),
-        ],
-        compiler_params=pltpu.CompilerParams(vmem_limit_bytes=VMEM_WHOLE),
-    )(values, keys)
-    prev_keys, passed = shift_tail(key_tail), pass_odd(value_tail)
-
     chunk_rows = w_rows // CHUNKS
     steps, others = exchange_masks(seq_count)
     half = chunk_rows // 2
-    parts = pl.pallas_call(
+    hbm = pl.BlockSpec(memory_space=pltpu.HBM)
+    halves = [((3, half, w_cols), kind) for kind in (BF16, F32) for _ in range(CHUNKS)]
+    key_tail, value_tail, *parts = pl.pallas_call(
         functools.partial(grads_kernel, steps[0]),
-        out_shape=[jax.ShapeDtypeStruct((3, half, w_cols), BF16)] * CHUNKS
-        + [jax.ShapeDtypeStruct((3, half, w_cols), F32)] * CHUNKS,
+        out_shape=[jax.ShapeDtypeStruct((WINDOW, fw_dim), BF16)] * 2
+        + [jax.ShapeDtypeStruct(*x) for x in halves],
         in_specs=[hbm] * 5 + [pl.BlockSpec(memory_space=pltpu.VMEM)],
+        out_specs=[hbm] * (2 + len(halves)),
         name="gradients",
-        scratch_shapes=[
+        scratch_shapes=[pltpu.VMEM(*x) for x in halves]
+        + [
             pltpu.VMEM(keys.shape, BF16),
             pltpu.VMEM(values.shape, BF16),
             pltpu.VMEM(w_gate.shape, BF16),
@@ -325,7 +305,12 @@
             pltpu.VMEM(w_down.shape, BF16),
             pltpu.VMEM(keys.shape, BF16),
             pltpu.VMEM((tok_rows, w_cols), BF16),
+            pltpu.VMEM(values.shape, BF16),
+            pltpu.VMEM((tok_rows, w_cols), BF16),
+            pltpu.VMEM((tok_rows, w_cols), BF16),
             pltpu.SemaphoreType.DMA((5,)),
+            pltpu.SemaphoreType.DMA((2,)),
+            pltpu.SemaphoreType.DMA((3, len(halves))),
         ],
         compiler_params=pltpu.CompilerParams(vmem_limit_bytes=VMEM_WHOLE),
         cost_estimate=pl.CostEstimate(
@@ -336,18 +321,23 @@
     )(keys, values, *weights, rates.reshape(1, tok_rows))
     sent, kept = parts[:CHUNKS], parts[CHUNKS:]
     came = [swap(x, steps[0]) for x in sent]
-    came[0], prev_keys, passed = lax.optimization_barrier((came[0], prev_keys, passed))
-    prev_values = shift_passed(value_tail, passed)
+    beside_k, beside_v = trade(key_tail), trade(value_tail)
     folded = [fold(steps[1], [k], [c]) for k, c in zip(kept, came)]
     came = [swap(x, steps[1]) for x, _ in folded]
+    came[0], beside_k = lax.optimization_barrier((came[0], beside_k))
+    before_k = pass_on(beside_k)
     sent, kept = fold(steps[2], [k for _, k in folded], came)
-    came, prev_values = lax.optimization_barrier((swap(sent, steps[2]), prev_values))
+    came, beside_v = lax.optimization_barrier((swap(sent, steps[2]), beside_v))
+    before_v = pass_on(beside_v)
     total = kept + came.astype(F32)
     for masks in others:
         total = total.astype(BF16)
-        total = total.astype(F32) + swap(total, masks).astype(F32)
+        came = swap(total, masks)
+        if masks == others[-1]:
+            came, before_k = lax.optimization_barrier((came, before_k))
+        total = total.astype(F32) + came.astype(F32)
     total = total.astype(BF16)
-    more = swap(total, steps[2])
+    more, before_v = lax.optimization_barrier((swap(total, steps[2]), before_v))
     rows = total.shape[1] // CHUNKS
     pieces = []
     for c in range(CHUNKS):
@@ -356,16 +346,24 @@
         piece = jnp.concatenate([piece, swap(piece, steps[1])], axis=1)
         pieces += [piece, swap(piece, steps[0])]
 
-    attended, squares = kernel_call(
+    attended, squares = pl.pallas_call(
         attend_kernel,
-        "window_attention",
-        (
+        out_shape=(
             jax.ShapeDtypeStruct((tok_rows, fw_dim), F32),
             jax.ShapeDtypeStruct((3, 8, w_cols), F32),
         ),
-        4 * tok_rows * (WINDOW + BLOCK) * fw_dim,
-        8 * tok_rows * fw_dim,
-    )(queries, keys, values, prev_keys, prev_values, *weights)
+        in_specs=[pl.BlockSpec(memory_space=pltpu.VMEM)] * 3
+        + [hbm] * 4
+        + [pl.BlockSpec(memory_space=pltpu.VMEM)] * 3,
+        name="window_attention",
+        scratch_shapes=[pltpu.VMEM((2, WINDOW, fw_dim), BF16), pltpu.SemaphoreType.DMA((2,))],
+        compiler_params=pltpu.CompilerParams(vmem_limit_bytes=VMEM_LIMIT),
+        cost_estimate=pl.CostEstimate(
+            flops=4 * tok_rows * (WINDOW + BLOCK) * fw_dim,
+            bytes_accessed=8 * tok_rows * fw_dim,
+            transcendentals=0,
+        ),
+    )(queries, keys, values, beside_k, beside_v, before_k, before_v, *weights)
 
     part_rows = w_rows // seq_count
     kept_rows = max(part_rows, SUBROWS)

time: 89.9 us -> 86.2 us (0.959)
  the two profiles are of different devices: /device:TPU:0 before, /device:TPU:17 now
where the time goes in v3:
time: 86.2 us; the launch traced here: 86 us
  waiting for transfers between devices  48.7 us (56%)
  starting transfers between devices  17.9 us (21%)
  Pallas kernels  17.2 us (20%)
  local copies, waits for them, and re-layouts  1.2 us (1%)
    ppermute x11, waiting for transfers between devices, swap(): return lax.ppermute(x, ('seq', 'head'), pairs)  32 us
    ppermute x2, waiting for transfers between devices, pass_on(): lax.ppermute(x, 'seq', [(i, i + 2) for i in range(0, lax.axis_size('seq')...  10.8 us
    ppermute x11, starting transfers between devices, swap(): return lax.ppermute(x, ('seq', 'head'), pairs)  8.3 us
    pallas_call x1, Pallas kernels, body(): pl.pallas_call(functools.partial(grads_kernel, steps[0]), out_shape=[jax....  6.93 us
    ppermute x2, starting transfers between devices, pass_on(): lax.ppermute(x, 'seq', [(i, i + 2) for i in range(0, lax.axis_size('seq')...  6.14 us
    pallas_call x1, Pallas kernels, body(): pl.pallas_call(attend_kernel, out_shape=(jax.ShapeDtypeStruct((tok_rows,...  5.3 us
    ppermute x2, waiting for transfers between devices, trade(): return lax.ppermute(x, 'seq', [(i, i ^ 1) for i in range(peers)])  5.06 us
    pallas_call x1, Pallas kernels, body(): pl.pallas_call(functools.partial(apply_kernel, steps, part_rows), out_sha...  3.51 us
  transfers between devices with their start and end apart: 16, of which 15 were waited for; matrix products, arithmetic and copies ran while one was open for 0% of the time, Pallas kernels for 6%

profile of v3, /device:TPU:17, one launch (start us, length us, event | category | flops | bytes accessed | tf_op | source)
XLA Modules:
  0.0 86.0 jit_solution(2121502037961334986)
XLA Ops:
  0.6 6.9 %gradients.1 = (bf16[512,512]{1,0:T(8,128)(2,1)}, bf16[512,512]{1,0:T(8,128)(2,1)}, bf16[3,128,512]{2,1,0:T(8,128)(2,1)}, bf16[3,128,512]{2,1,0:T(8,128)(2,1)}, ...) custom-call(bf16[768,512]{1,0:T(8,128)(2,1)} %k_ref.1, bf16[768,512]{1,0:T(8,128)(2,1)} %v_ref.1, ...), custom_call_target="tpu_custom_call" | custom-call | flops 2415919104 | bytes 6291456 | tf_op jit(solution)/shard_map/gradients/pallas_call | solution.py:292
  7.6 1.4 %collective-permute-start = (bf16[3,128,512]{2,1,0:T(8,128)(2,1)}, bf16[3,128,512]{2,1,0:T(8,128)(2,1)S(1)}, u32[]{:S(2)}, u32[]{:S(2)}) collective-permute-start(bf16[3,128,512]{2,1,0:T(8,128)(2,1)} %get-tuple-element.32), channel_id=1, source_target_pairs={{0,4},{1,9},{2,6},{3,11},{4,0},{5,13},{6,2},{7,15},{8,12},{9,1},{1... | collective-permute-start | bytes 1179656 | tf_op jit(solution)/shard_map/ppermute | solution.py:73
  9.1 1.2 %collective-permute-start.3 = (bf16[512,512]{1,0:T(8,128)(2,1)}, bf16[512,512]{1,0:T(8,128)(2,1)S(1)}, u32[]{:S(2)}, u32[]{:S(2)}) collective-permute-start(bf16[512,512]{1,0:T(8,128)(2,1)} %get-tuple-element.38), channel_id=1, source_target_pairs={{0,2},{2,0},{4,6},{6,4},{8,10},{10,8},{12,14},{14,12},{16,18},{18,... | collective-permute-start | bytes 1572872 | tf_op jit(solution)/shard_map/ppermute | solution.py:78
  10.3 0.3 collective-permute-start.6
  10.6 4.2 %collective-permute-done.refs_1_ = bf16[3,128,512]{2,1,0:T(8,128)(2,1)S(1)} collective-permute-done((bf16[3,128,512]{2,1,0:T(8,128)(2,1)}, bf16[3,128,512]{2,1,0:T(8,128)(2,1)S(1)}, u32[]{:S(2)}, u32[]{:S(2)}) %collective-permute-start) | collective-permute-done | bytes 393248 | tf_op jit(solution)/shard_map/ppermute | solution.py:73
  14.8 1.1 %copy-done.5 = f32[3,128,512]{2,1,0:T(8,128)S(1)} copy-done((f32[3,128,512]{2,1,0:T(8,128)S(1)}, f32[3,128,512]{2,1,0:T(8,128)}, u32[]{:S(2)}) %copy-start.5) | copy-done | bytes 786456
  16.0 1.3 %collective-permute-start.2 = (bf16[3,64,512]{2,1,0:T(8,128)(2,1)S(1)}, bf16[3,64,512]{2,1,0:T(8,128)(2,1)S(1)}, u32[]{:S(2)}, u32[]{:S(2)}) collective-permute-start(bf16[3,64,512]{2,1,0:T(8,128)(2,1)S(1)} %get-tuple-element.37), channel_id=1, source_target_pairs={{0,8},{1,5},{2,10},{3,7},{4,12},{5,1},{6,14},{7,3},{8,0},{9,13},{1... | collective-permute-start | bytes 589832 | tf_op jit(solution)/shard_map/ppermute | solution.py:73
  17.3 1.7 %collective-permute-done.1.refs_1_ = bf16[3,128,512]{2,1,0:T(8,128)(2,1)S(1)} collective-permute-done((bf16[3,128,512]{2,1,0:T(8,128)(2,1)}, bf16[3,128,512]{2,1,0:T(8,128)(2,1)S(1)}, u32[]{:S(2)}, u32[]{:S(2)}) %collective-permute-start.1) | collective-permute-done | bytes 393248 | tf_op jit(solution)/shard_map/ppermute | solution.py:73
  19.1 1.3 %collective-permute-start.4 = (bf16[3,64,512]{2,1,0:T(8,128)(2,1)S(1)}, bf16[3,64,512]{2,1,0:T(8,128)(2,1)S(1)}, u32[]{:S(2)}, u32[]{:S(2)}) collective-permute-start(bf16[3,64,512]{2,1,0:T(8,128)(2,1)S(1)} %get-tuple-element.40), channel_id=1, source_target_pairs={{0,8},{1,5},{2,10},{3,7},{4,12},{5,1},{6,14},{7,3},{8,0},{9,13},{1... | collective-permute-start | bytes 589832 | tf_op jit(solution)/shard_map/ppermute | solution.py:73
  20.4 1.1 %collective-permute-done.3.odd_k = bf16[512,512]{1,0:T(8,128)(2,1)S(1)} collective-permute-done((bf16[512,512]{1,0:T(8,128)(2,1)}, bf16[512,512]{1,0:T(8,128)(2,1)S(1)}, u32[]{:S(2)}, u32[]{:S(2)}) %collective-permute-start.3) | collective-permute-done | bytes 524320 | tf_op jit(solution)/shard_map/ppermute | solution.py:78
  21.5 0.7 collective-permute-done.2.refs_2_
  22.2 2.1 %collective-permute-done.4.refs_3_ = bf16[3,64,512]{2,1,0:T(8,128)(2,1)S(1)} collective-permute-done((bf16[3,64,512]{2,1,0:T(8,128)(2,1)S(1)}, bf16[3,64,512]{2,1,0:T(8,128)(2,1)S(1)}, u32[]{:S(2)}, u32[]{:S(2)}) %collective-permute-start.4) | collective-permute-done | bytes 196640 | tf_op jit(solution)/shard_map/ppermute | solution.py:73
  24.4 1.3 %collective-permute-start.5 = (bf16[3,64,512]{2,1,0:T(8,128)(2,1)S(1)}, bf16[3,64,512]{2,1,0:T(8,128)(2,1)S(1)}, u32[]{:S(2)}, u32[]{:S(2)}) collective-permute-start(bf16[3,64,512]{2,1,0:T(8,128)(2,1)S(1)} %get-tuple-element.42), channel_id=1, source_target_pairs={{0,2},{1,3},{2,0},{3,1},{4,6},{5,7},{6,4},{7,5},{8,10},{9,11},{10,... | collective-permute-start | bytes 589832 | tf_op jit(solution)/shard_map/ppermute | solution.py:73
  25.7 3.1 %collective-permute-start.8 = (bf16[512,512]{1,0:T(8,128)(2,1)S(1)}, bf16[512,512]{1,0:T(8,128)(2,1)S(1)}, u32[]{:S(2)}, u32[]{:S(2)}) collective-permute-start(bf16[512,512]{1,0:T(8,128)(2,1)S(1)} %collective-permute-done.3.odd_k), channel_id=1, source_target_pairs={{0,4},{4,8},{8,12},{12,16},{16,20},{20,24},{24,28},{1,5},{5,9},{9,... | collective-permute-start | bytes 1572872 | tf_op jit(solution)/shard_map/ppermute | solution.py:82
  28.8 3.9 %collective-permute-done.6.odd_v = bf16[512,512]{1,0:T(8,128)(2,1)S(1)} collective-permute-done((bf16[512,512]{1,0:T(8,128)(2,1)}, bf16[512,512]{1,0:T(8,128)(2,1)S(1)}, u32[]{:S(2)}, u32[]{:S(2)}) %collective-permute-start.6) | collective-permute-done | bytes 524320 | tf_op jit(solution)/shard_map/ppermute | solution.py:78
  32.7 4.2 %collective-permute-done.5 = bf16[3,64,512]{2,1,0:T(8,128)(2,1)S(1)} collective-permute-done((bf16[3,64,512]{2,1,0:T(8,128)(2,1)S(1)}, bf16[3,64,512]{2,1,0:T(8,128)(2,1)S(1)}, u32[]{:S(2)}, u32[]{:S(2)}) %collective-permute-start.5) | collective-permute-done | bytes 196640 | tf_op jit(solution)/shard_map/ppermute | solution.py:73
  37.0 0.4 collective-permute-start.7
  37.4 3.0 %collective-permute-start.10 = (bf16[512,512]{1,0:T(8,128)(2,1)S(1)}, bf16[512,512]{1,0:T(8,128)(2,1)S(1)}, u32[]{:S(2)}, u32[]{:S(2)}) collective-permute-start(bf16[512,512]{1,0:T(8,128)(2,1)S(1)} %collective-permute-done.6.odd_v), channel_id=1, source_target_pairs={{0,4},{4,8},{8,12},{12,16},{16,20},{20,24},{24,28},{1,5},{5,9},{9,... | collective-permute-start | bytes 1572872 | tf_op jit(solution)/shard_map/ppermute | solution.py:82
  40.4 5.0 %collective-permute-done.7 = bf16[3,64,512]{2,1,0:T(8,128)(2,1)S(1)} collective-permute-done((bf16[3,64,512]{2,1,0:T(8,128)(2,1)S(1)}, bf16[3,64,512]{2,1,0:T(8,128)(2,1)S(1)}, u32[]{:S(2)}, u32[]{:S(2)}) %collective-permute-start.7) | collective-permute-done | bytes 196640 | tf_op jit(solution)/shard_map/ppermute | solution.py:73
  45.5 0.8 collective-permute-start.9
  46.3 4.3 %collective-permute-done.9 = bf16[3,64,512]{2,1,0:T(8,128)(2,1)S(1)} collective-permute-done((bf16[3,64,512]{2,1,0:T(8,128)(2,1)S(1)}, bf16[3,64,512]{2,1,0:T(8,128)(2,1)S(1)}, u32[]{:S(2)}, u32[]{:S(2)}) %collective-permute-start.9) | collective-permute-done | bytes 196640 | tf_op jit(solution)/shard_map/ppermute | solution.py:73
  50.6 10.8 %collective-permute-done.10.even_v = bf16[512,512]{1,0:T(8,128)(2,1)S(1)} collective-permute-done((bf16[512,512]{1,0:T(8,128)(2,1)S(1)}, bf16[512,512]{1,0:T(8,128)(2,1)S(1)}, u32[]{:S(2)}, u32[]{:S(2)}) %collective-permute-start.10) | collective-permute-done | bytes 524320 | tf_op jit(solution)/shard_map/ppermute | solution.py:82
  61.6 1.5 %collective-permute-start.11 = (bf16[3,64,512]{2,1,0:T(8,128)(2,1)S(1)}, bf16[3,64,512]{2,1,0:T(8,128)(2,1)S(1)}, u32[]{:S(2)}, u32[]{:S(2)}) collective-permute-start(bf16[3,64,512]{2,1,0:T(8,128)(2,1)S(1)} %pad_maximum_fusion.2), channel_id=1, source_target_pairs={{0,8},{1,5},{2,10},{3,7},{4,12},{5,1},{6,14},{7,3},{8,0},{9,13},{1... | collective-permute-start | bytes 589832 | tf_op jit(solution)/shard_map/ppermute | solution.py:73
  63.1 3.3 %collective-permute-done.13 = bf16[3,64,512]{2,1,0:T(8,128)(2,1)S(1)} collective-permute-done((bf16[3,64,512]{2,1,0:T(8,128)(2,1)S(1)}, bf16[3,64,512]{2,1,0:T(8,128)(2,1)S(1)}, u32[]{:S(2)}, u32[]{:S(2)}) %collective-permute-start.13) | collective-permute-done | bytes 196640 | tf_op jit(solution)/shard_map/ppermute | solution.py:73
  66.5 2.0 %collective-permute-done.11 = bf16[3,64,512]{2,1,0:T(8,128)(2,1)S(1)} collective-permute-done((bf16[3,64,512]{2,1,0:T(8,128)(2,1)S(1)}, bf16[3,64,512]{2,1,0:T(8,128)(2,1)S(1)}, u32[]{:S(2)}, u32[]{:S(2)}) %collective-permute-start.11) | collective-permute-done | bytes 196640 | tf_op jit(solution)/shard_map/ppermute | solution.py:73
  68.7 5.3 %window_attention.1 = (f32[768,512]{1,0:T(8,128)S(1)}, f32[3,8,512]{2,1,0:T(8,128)S(1)}) custom-call(bf16[768,512]{1,0:T(8,128)(2,1)S(1)} %copy-done, bf16[768,512]{1,0:T(8,128)(2,1)S(1)} %copy-done.6, bf16[768,512]{1,0:T(8,128)(2,1)S(1)} %copy-done.7, bf16[512,512]{1,0:T(8,128)(2,1)S(1)} %collective-permute-done.3.odd_k, ...), custom_call_target="tpu_custom_call" | custom-call | flops 1207959552 | bytes 3145728 | tf_op jit(solution)/shard_map/window_attention/pallas_call | solution.py:349
  74.0 0.2 collective-permute-done.14.refs_3_
  74.2 4.2 %collective-permute-done.12.refs_1_ = bf16[3,128,512]{2,1,0:T(8,128)(2,1)S(1)} collective-permute-done((bf16[3,128,512]{2,1,0:T(8,128)(2,1)S(1)}, bf16[3,128,512]{2,1,0:T(8,128)(2,1)S(1)}, u32[]{:S(2)}, u32[]{:S(2)}) %collective-permute-start.12) | collective-permute-done | bytes 393248 | tf_op jit(solution)/shard_map/ppermute | solution.py:73
  78.4 3.5 %apply.1 = (f32[768,512]{1,0:T(8,128)S(1)}, f32[8,768]{1,0:T(8,128)S(1)}, bf16[32,512]{1,0:T(8,128)(2,1)}, bf16[32,512]{1,0:T(8,128)(2,1)}, bf16[32,512]{1,0:T(8,128)(2,1)}) custom-call(bf16[3,128,512]{2,1,0:T(8,128)(2,1)S(1)} %pad_maximum_fusion.refs_0_, bf16[3,128,512]{2,1,0:T(8,128)(2,1)S(1)} %collective-permute-done.12.refs_1_, ...), custom_call_target="tpu_custom_call" | custom-call | flops 1207959552 | bytes 4718592 | tf_op jit(solution)/shard_map/apply/pallas_call | solution.py:371
  81.9 1.9 %collective-permute-start.15 = (f32[8,768]{1,0:T(8,128)S(1)}, f32[8,768]{1,0:T(8,128)S(1)}, u32[]{:S(2)}, u32[]{:S(2)}) collective-permute-start(f32[8,768]{1,0:T(8,128)S(1)} %get-tuple-element.54.sums_ref), channel_id=1, source_target_pairs={{0,1},{1,0},{2,3},{3,2},{4,5},{5,4},{6,7},{7,6},{8,9},{9,8},{10,11... | collective-permute-start | bytes 73736 | tf_op jit(solution)/shard_map/ppermute | solution.py:395
  83.9 0.8 collective-permute-done.15.more_ref
  84.7 1.2 %norm.1 = bf16[768,512]{1,0:T(8,128)(2,1)} custom-call(f32[768,512]{1,0:T(8,128)S(1)} %get-tuple-element.53.combined_ref, f32[8,768]{1,0:T(8,128)S(1)} %get-tuple-element.54.sums_ref, f32[8,768]{1,0:T(8,128)S(1)} %collective-permute-done.15.more_ref, f32[1,512]{1,0:T(1,128)S(1)} %bitcast.2), custom_call_target="tpu_custom_call" | custom-call | flops 1572864 | bytes 2359296 | tf_op jit(solution)/shard_map/norm/pallas_call | solution.py:403
  (33 shorter events, 0.8 us)
Async XLA Ops:
  7.6 11.4 %copy-start.4 = (f32[3,128,512]{2,1,0:T(8,128)S(1)}, f32[3,128,512]{2,1,0:T(8,128)}, u32[]{:S(2)}) copy-start(f32[3,128,512]{2,1,0:T(8,128)} %get-tuple-element.34.refs_0_) | copy-start | bytes 2359300
  7.6 7.2 %collective-permute-start = (bf16[3,128,512]{2,1,0:T(8,128)(2,1)}, bf16[3,128,512]{2,1,0:T(8,128)(2,1)S(1)}, u32[]{:S(2)}, u32[]{:S(2)}) collective-permute-start(bf16[3,128,512]{2,1,0:T(8,128)(2,1)} %get-tuple-element.32), channel_id=1, source_target_pairs={{0,4},{1,9},{2,6},{3,11},{4,0},{5,13},{6,2},{7,15},{8,12},{9,1},{1... | collective-permute-start | bytes 1179656 | tf_op jit(solution)/shard_map/ppermute | solution.py:73
  8.9 10.1 %collective-permute-start.1 = (bf16[3,128,512]{2,1,0:T(8,128)(2,1)}, bf16[3,128,512]{2,1,0:T(8,128)(2,1)S(1)}, u32[]{:S(2)}, u32[]{:S(2)}) collective-permute-start(bf16[3,128,512]{2,1,0:T(8,128)(2,1)} %get-tuple-element.35), channel_id=1, source_target_pairs={{0,4},{1,9},{2,6},{3,11},{4,0},{5,13},{6,2},{7,15},{8,12},{9,1},{1... | collective-permute-start | bytes 1179656 | tf_op jit(solution)/shard_map/ppermute | solution.py:73
  9.1 12.4 %collective-permute-start.3 = (bf16[512,512]{1,0:T(8,128)(2,1)}, bf16[512,512]{1,0:T(8,128)(2,1)S(1)}, u32[]{:S(2)}, u32[]{:S(2)}) collective-permute-start(bf16[512,512]{1,0:T(8,128)(2,1)} %get-tuple-element.38), channel_id=1, source_target_pairs={{0,2},{2,0},{4,6},{6,4},{8,10},{10,8},{12,14},{14,12},{16,18},{18,... | collective-permute-start | bytes 1572872 | tf_op jit(solution)/shard_map/ppermute | solution.py:78
  10.3 22.4 %collective-permute-start.6 = (bf16[512,512]{1,0:T(8,128)(2,1)}, bf16[512,512]{1,0:T(8,128)(2,1)S(1)}, u32[]{:S(2)}, u32[]{:S(2)}) collective-permute-start(bf16[512,512]{1,0:T(8,128)(2,1)} %get-tuple-element.43), channel_id=1, source_target_pairs={{0,2},{2,0},{4,6},{6,4},{8,10},{10,8},{12,14},{14,12},{16,18},{18,... | collective-permute-start | bytes 1572872 | tf_op jit(solution)/shard_map/ppermute | solution.py:78
  14.8 1.1 %copy-start.5 = (f32[3,128,512]{2,1,0:T(8,128)S(1)}, f32[3,128,512]{2,1,0:T(8,128)}, u32[]{:S(2)}) copy-start(f32[3,128,512]{2,1,0:T(8,128)} %get-tuple-element.31.refs_0_) | copy-start | bytes 2359300
  16.0 6.3 %collective-permute-start.2 = (bf16[3,64,512]{2,1,0:T(8,128)(2,1)S(1)}, bf16[3,64,512]{2,1,0:T(8,128)(2,1)S(1)}, u32[]{:S(2)}, u32[]{:S(2)}) collective-permute-start(bf16[3,64,512]{2,1,0:T(8,128)(2,1)S(1)} %get-tuple-element.37), channel_id=1, source_target_pairs={{0,8},{1,5},{2,10},{3,7},{4,12},{5,1},{6,14},{7,3},{8,0},{9,13},{1... | collective-permute-start | bytes 589832 | tf_op jit(solution)/shard_map/ppermute | solution.py:73
  19.1 5.3 %collective-permute-start.4 = (bf16[3,64,512]{2,1,0:T(8,128)(2,1)S(1)}, bf16[3,64,512]{2,1,0:T(8,128)(2,1)S(1)}, u32[]{:S(2)}, u32[]{:S(2)}) collective-permute-start(bf16[3,64,512]{2,1,0:T(8,128)(2,1)S(1)} %get-tuple-element.40), channel_id=1, source_target_pairs={{0,8},{1,5},{2,10},{3,7},{4,12},{5,1},{6,14},{7,3},{8,0},{9,13},{1... | collective-permute-start | bytes 589832 | tf_op jit(solution)/shard_map/ppermute | solution.py:73
  24.4 12.6 %collective-permute-start.5 = (bf16[3,64,512]{2,1,0:T(8,128)(2,1)S(1)}, bf16[3,64,512]{2,1,0:T(8,128)(2,1)S(1)}, u32[]{:S(2)}, u32[]{:S(2)}) collective-permute-start(bf16[3,64,512]{2,1,0:T(8,128)(2,1)S(1)} %get-tuple-element.42), channel_id=1, source_target_pairs={{0,2},{1,3},{2,0},{3,1},{4,6},{5,7},{6,4},{7,5},{8,10},{9,11},{10,... | collective-permute-start | bytes 589832 | tf_op jit(solution)/shard_map/ppermute | solution.py:73
  25.7 19.7 %collective-permute-start.8 = (bf16[512,512]{1,0:T(8,128)(2,1)S(1)}, bf16[512,512]{1,0:T(8,128)(2,1)S(1)}, u32[]{:S(2)}, u32[]{:S(2)}) collective-permute-start(bf16[512,512]{1,0:T(8,128)(2,1)S(1)} %collective-permute-done.3.odd_k), channel_id=1, source_target_pairs={{0,4},{4,8},{8,12},{12,16},{16,20},{20,24},{24,28},{1,5},{5,9},{9,... | collective-permute-start | bytes 1572872 | tf_op jit(solution)/shard_map/ppermute | solution.py:82
  36.9 31.7 %copy-start.7 = (bf16[768,512]{1,0:T(8,128)(2,1)S(1)}, bf16[768,512]{1,0:T(8,128)(2,1)}, u32[]{:S(2)}) copy-start(bf16[768,512]{1,0:T(8,128)(2,1)} %v_ref.1) | copy-start | bytes 2359300
  37.0 8.4 %collective-permute-start.7 = (bf16[3,64,512]{2,1,0:T(8,128)(2,1)S(1)}, bf16[3,64,512]{2,1,0:T(8,128)(2,1)S(1)}, u32[]{:S(2)}, u32[]{:S(2)}) collective-permute-start(bf16[3,64,512]{2,1,0:T(8,128)(2,1)S(1)} %add_convert_fusion.1), channel_id=1, source_target_pairs={{0,16},{1,17},{2,18},{3,19},{4,20},{5,21},{6,22},{7,23},{8,24},{9,... | collective-permute-start | bytes 589832 | tf_op jit(solution)/shard_map/ppermute | solution.py:73
  37.4 24.1 %collective-permute-start.10 = (bf16[512,512]{1,0:T(8,128)(2,1)S(1)}, bf16[512,512]{1,0:T(8,128)(2,1)S(1)}, u32[]{:S(2)}, u32[]{:S(2)}) collective-permute-start(bf16[512,512]{1,0:T(8,128)(2,1)S(1)} %collective-permute-done.6.odd_v), channel_id=1, source_target_pairs={{0,4},{4,8},{8,12},{12,16},{16,20},{20,24},{24,28},{1,5},{5,9},{9,... | collective-permute-start | bytes 1572872 | tf_op jit(solution)/shard_map/ppermute | solution.py:82
  45.4 23.2 %copy-start = (bf16[768,512]{1,0:T(8,128)(2,1)S(1)}, bf16[768,512]{1,0:T(8,128)(2,1)}, u32[]{:S(2)}) copy-start(bf16[768,512]{1,0:T(8,128)(2,1)} %refs_4_.3) | copy-start | bytes 2359300
  45.5 23.2 %copy-start.1 = (bf16[512,512]{1,0:T(8,128)(2,1)S(1)}, bf16[512,512]{1,0:T(8,128)(2,1)}, u32[]{:S(2)}) copy-start(bf16[512,512]{1,0:T(8,128)(2,1)} %refs_5_.1) | copy-start | bytes 1572868
  45.5 23.2 %copy-start.2 = (bf16[512,512]{1,0:T(8,128)(2,1)S(1)}, bf16[512,512]{1,0:T(8,128)(2,1)}, u32[]{:S(2)}) copy-start(bf16[512,512]{1,0:T(8,128)(2,1)} %refs_6_.1) | copy-start | bytes 1572868
  45.5 23.2 %copy-start.3 = (bf16[512,512]{1,0:T(8,128)(2,1)S(1)}, bf16[512,512]{1,0:T(8,128)(2,1)}, u32[]{:S(2)}) copy-start(bf16[512,512]{1,0:T(8,128)(2,1)} %refs_7_.1) | copy-start | bytes 1572868
  45.5 23.2 %copy-start.6 = (bf16[768,512]{1,0:T(8,128)(2,1)S(1)}, bf16[768,512]{1,0:T(8,128)(2,1)}, u32[]{:S(2)}) copy-start(bf16[768,512]{1,0:T(8,128)(2,1)} %k_ref.1) | copy-start | bytes 2359300
  45.5 5.1 %collective-permute-start.9 = (bf16[3,64,512]{2,1,0:T(8,128)(2,1)S(1)}, bf16[3,64,512]{2,1,0:T(8,128)(2,1)S(1)}, u32[]{:S(2)}, u32[]{:S(2)}) collective-permute-start(bf16[3,64,512]{2,1,0:T(8,128)(2,1)S(1)} %add_convert_fusion), channel_id=1, source_target_pairs={{0,2},{1,3},{2,0},{3,1},{4,6},{5,7},{6,4},{7,5},{8,10},{9,11},{10,... | collective-permute-start | bytes 589832 | tf_op jit(solution)/shard_map/ppermute | solution.py:73
  61.5 4.9 %collective-permute-start.13 = (bf16[3,64,512]{2,1,0:T(8,128)(2,1)S(1)}, bf16[3,64,512]{2,1,0:T(8,128)(2,1)S(1)}, u32[]{:S(2)}, u32[]{:S(2)}) collective-permute-start(bf16[3,64,512]{2,1,0:T(8,128)(2,1)S(1)} %pad_maximum_fusion.3), channel_id=1, source_target_pairs={{0,8},{1,5},{2,10},{3,7},{4,12},{5,1},{6,14},{7,3},{8,0},{9,13},{1... | collective-permute-start | bytes 589832 | tf_op jit(solution)/shard_map/ppermute | solution.py:73
  61.6 6.9 %collective-permute-start.11 = (bf16[3,64,512]{2,1,0:T(8,128)(2,1)S(1)}, bf16[3,64,512]{2,1,0:T(8,128)(2,1)S(1)}, u32[]{:S(2)}, u32[]{:S(2)}) collective-permute-start(bf16[3,64,512]{2,1,0:T(8,128)(2,1)S(1)} %pad_maximum_fusion.2), channel_id=1, source_target_pairs={{0,8},{1,5},{2,10},{3,7},{4,12},{5,1},{6,14},{7,3},{8,0},{9,13},{1... | collective-permute-start | bytes 589832 | tf_op jit(solution)/shard_map/ppermute | solution.py:73
  66.4 7.8 %collective-permute-start.14 = (bf16[3,128,512]{2,1,0:T(8,128)(2,1)S(1)}, bf16[3,128,512]{2,1,0:T(8,128)(2,1)S(1)}, u32[]{:S(2)}, u32[]{:S(2)}) collective-permute-start(bf16[3,128,512]{2,1,0:T(8,128)(2,1)S(1)} %pad_maximum_fusion.1.refs_2_), channel_id=1, source_target_pairs={{0,4},{1,9},{2,6},{3,11},{4,0},{5,13},{6,2},{7,15},{8,12},{9,1},{1... | collective-permute-start | bytes 1179656 | tf_op jit(solution)/shard_map/ppermute | solution.py:73
  68.5 9.9 %collective-permute-start.12 = (bf16[3,128,512]{2,1,0:T(8,128)(2,1)S(1)}, bf16[3,128,512]{2,1,0:T(8,128)(2,1)S(1)}, u32[]{:S(2)}, u32[]{:S(2)}) collective-permute-start(bf16[3,128,512]{2,1,0:T(8,128)(2,1)S(1)} %pad_maximum_fusion.refs_0_), channel_id=1, source_target_pairs={{0,4},{1,9},{2,6},{3,11},{4,0},{5,13},{6,2},{7,15},{8,12},{9,1},{1... | collective-permute-start | bytes 1179656 | tf_op jit(solution)/shard_map/ppermute | solution.py:73
  78.4 6.3 %copy-start.8 = (f32[512]{0:T(512)S(1)}, f32[512]{0:T(512)}, u32[]{:S(2)}) copy-start(f32[512]{0:T(512)} %param.15) | copy-start | bytes 6148
  81.9 2.8 %collective-permute-start.15 = (f32[8,768]{1,0:T(8,128)S(1)}, f32[8,768]{1,0:T(8,128)S(1)}, u32[]{:S(2)}, u32[]{:S(2)}) collective-permute-start(f32[8,768]{1,0:T(8,128)S(1)} %get-tuple-element.54.sums_ref), channel_id=1, source_target_pairs={{0,1},{1,0},{2,3},{3,2},{4,5},{5,4},{6,7},{7,6},{8,9},{9,8},{10,11... | collective-permute-start | bytes 73736 | tf_op jit(solution)/shard_map/ppermute | solution.py:395

commit v4 on v3

--- a/solution.py
+++ b/solution.py
@@ -337,13 +337,16 @@
             came, before_k = lax.optimization_barrier((came, before_k))
         total = total.astype(F32) + came.astype(F32)
     total = total.astype(BF16)
-    more, before_v = lax.optimization_barrier((swap(total, steps[2]), before_v))
+    more = swap(total, steps[2])
     rows = total.shape[1] // CHUNKS
     pieces = []
     for c in range(CHUNKS):
         here = slice(c * rows, (c + 1) * rows)
         piece = jnp.concatenate([total[:, here], more[:, here]], axis=1)
-        piece = jnp.concatenate([piece, swap(piece, steps[1])], axis=1)
+        came = swap(piece, steps[1])
+        if c == 1:
+            came, before_v = lax.optimization_barrier((came, before_v))
+        piece = jnp.concatenate([piece, came], axis=1)
         pieces += [piece, swap(piece, steps[0])]
 
     attended, squares = pl.pallas_call(

time: 86.2 us -> 81 us (0.940)
  waiting for transfers between devices: 48.7 us -> 45.2 us
  starting transfers between devices: 17.9 us -> 16.2 us
    ppermute x11, waiting for transfers between devices: 32 us -> 30 us  [swap(): return lax.ppermute(x, ('seq', 'head'), pairs)]
    ppermute x1, starting transfers between devices: 1.95 us -> 0.29 us  [body(): more = [lax.ppermute(sums, 'head', [(0, 1), (1, 0)])]]
    ppermute x2, waiting for transfers between devices: 10.8 us -> 9.23 us  [pass_on(): lax.ppermute(x, 'seq', [(i, i + 2) for i in range(0, lax.axis_size('seq')...]
  transfers between devices with their start and end apart: 16 -> 16, of which waited for: 15 -> 14; matrix products, arithmetic and copies ran while one was open for 0% -> 0% of each run, Pallas kernels for 6% -> 7%
where the time goes in v4:
time: 81 us; the launch traced here: 80.8 us
  waiting for transfers between devices  45.2 us (56%)
  Pallas kernels  17.2 us (21%)
  starting transfers between devices  16.2 us (20%)
  local copies, waits for them, and re-layouts  1.2 us (1%)
  between operations  0.84 us (1%)
    ppermute x11, waiting for transfers between devices, swap(): return lax.ppermute(x, ('seq', 'head'), pairs)  30 us
    ppermute x2, waiting for transfers between devices, pass_on(): lax.ppermute(x, 'seq', [(i, i + 2) for i in range(0, lax.axis_size('seq')...  9.23 us
    ppermute x11, starting transfers between devices, swap(): return lax.ppermute(x, ('seq', 'head'), pairs)  8.31 us
    pallas_call x1, Pallas kernels, body(): pl.pallas_call(functools.partial(grads_kernel, steps[0]), out_shape=[jax....  6.93 us
    ppermute x2, starting transfers between devices, pass_on(): lax.ppermute(x, 'seq', [(i, i + 2) for i in range(0, lax.axis_size('seq')...  6.14 us
    pallas_call x1, Pallas kernels, body(): pl.pallas_call(attend_kernel, out_shape=(jax.ShapeDtypeStruct((tok_rows,...  5.3 us
    ppermute x2, waiting for transfers between devices, trade(): return lax.ppermute(x, 'seq', [(i, i ^ 1) for i in range(peers)])  5.06 us
    pallas_call x1, Pallas kernels, body(): pl.pallas_call(functools.partial(apply_kernel, steps, part_rows), out_sha...  3.52 us
  transfers between devices with their start and end apart: 16, of which 14 were waited for; matrix products, arithmetic and copies ran while one was open for 0% of the time, Pallas kernels for 7%

profile of v4, /device:TPU:17, one launch (start us, length us, event | category | flops | bytes accessed | tf_op | source)
XLA Modules:
  0.0 80.8 jit_solution(10659768131299211897)
XLA Ops:
  0.6 6.9 %gradients.1 = (bf16[512,512]{1,0:T(8,128)(2,1)}, bf16[512,512]{1,0:T(8,128)(2,1)}, bf16[3,128,512]{2,1,0:T(8,128)(2,1)}, bf16[3,128,512]{2,1,0:T(8,128)(2,1)}, ...) custom-call(bf16[768,512]{1,0:T(8,128)(2,1)} %k_ref.1, bf16[768,512]{1,0:T(8,128)(2,1)} %v_ref.1, ...), custom_call_target="tpu_custom_call" | custom-call | flops 2415919104 | bytes 6291456 | tf_op jit(solution)/shard_map/gradients/pallas_call | solution.py:292
  7.6 1.4 %collective-permute-start = (bf16[3,128,512]{2,1,0:T(8,128)(2,1)}, bf16[3,128,512]{2,1,0:T(8,128)(2,1)S(1)}, u32[]{:S(2)}, u32[]{:S(2)}) collective-permute-start(bf16[3,128,512]{2,1,0:T(8,128)(2,1)} %get-tuple-element.32), channel_id=1, source_target_pairs={{0,4},{1,9},{2,6},{3,11},{4,0},{5,13},{6,2},{7,15},{8,12},{9,1},{1... | collective-permute-start | bytes 1179656 | tf_op jit(solution)/shard_map/ppermute | solution.py:73
  9.1 1.2 %collective-permute-start.3 = (bf16[512,512]{1,0:T(8,128)(2,1)}, bf16[512,512]{1,0:T(8,128)(2,1)S(1)}, u32[]{:S(2)}, u32[]{:S(2)}) collective-permute-start(bf16[512,512]{1,0:T(8,128)(2,1)} %get-tuple-element.38), channel_id=1, source_target_pairs={{0,2},{2,0},{4,6},{6,4},{8,10},{10,8},{12,14},{14,12},{16,18},{18,... | collective-permute-start | bytes 1572872 | tf_op jit(solution)/shard_map/ppermute | solution.py:78
  10.3 0.3 collective-permute-start.6
  10.6 4.2 %collective-permute-done.refs_1_ = bf16[3,128,512]{2,1,0:T(8,128)(2,1)S(1)} collective-permute-done((bf16[3,128,512]{2,1,0:T(8,128)(2,1)}, bf16[3,128,512]{2,1,0:T(8,128)(2,1)S(1)}, u32[]{:S(2)}, u32[]{:S(2)}) %collective-permute-start) | collective-permute-done | bytes 393248 | tf_op jit(solution)/shard_map/ppermute | solution.py:73
  14.8 1.1 %copy-done.5 = f32[3,128,512]{2,1,0:T(8,128)S(1)} copy-done((f32[3,128,512]{2,1,0:T(8,128)S(1)}, f32[3,128,512]{2,1,0:T(8,128)}, u32[]{:S(2)}) %copy-start.5) | copy-done | bytes 786456
  16.0 1.3 %collective-permute-start.2 = (bf16[3,64,512]{2,1,0:T(8,128)(2,1)S(1)}, bf16[3,64,512]{2,1,0:T(8,128)(2,1)S(1)}, u32[]{:S(2)}, u32[]{:S(2)}) collective-permute-start(bf16[3,64,512]{2,1,0:T(8,128)(2,1)S(1)} %get-tuple-element.37), channel_id=1, source_target_pairs={{0,8},{1,5},{2,10},{3,7},{4,12},{5,1},{6,14},{7,3},{8,0},{9,13},{1... | collective-permute-start | bytes 589832 | tf_op jit(solution)/shard_map/ppermute | solution.py:73
  17.3 1.7 %collective-permute-done.1.refs_1_ = bf16[3,128,512]{2,1,0:T(8,128)(2,1)S(1)} collective-permute-done((bf16[3,128,512]{2,1,0:T(8,128)(2,1)}, bf16[3,128,512]{2,1,0:T(8,128)(2,1)S(1)}, u32[]{:S(2)}, u32[]{:S(2)}) %collective-permute-start.1) | collective-permute-done | bytes 393248 | tf_op jit(solution)/shard_map/ppermute | solution.py:73
  19.1 1.3 %collective-permute-start.4 = (bf16[3,64,512]{2,1,0:T(8,128)(2,1)S(1)}, bf16[3,64,512]{2,1,0:T(8,128)(2,1)S(1)}, u32[]{:S(2)}, u32[]{:S(2)}) collective-permute-start(bf16[3,64,512]{2,1,0:T(8,128)(2,1)S(1)} %get-tuple-element.40), channel_id=1, source_target_pairs={{0,8},{1,5},{2,10},{3,7},{4,12},{5,1},{6,14},{7,3},{8,0},{9,13},{1... | collective-permute-start | bytes 589832 | tf_op jit(solution)/shard_map/ppermute | solution.py:73
  20.4 1.1 %collective-permute-done.3.odd_k = bf16[512,512]{1,0:T(8,128)(2,1)S(1)} collective-permute-done((bf16[512,512]{1,0:T(8,128)(2,1)}, bf16[512,512]{1,0:T(8,128)(2,1)S(1)}, u32[]{:S(2)}, u32[]{:S(2)}) %collective-permute-start.3) | collective-permute-done | bytes 524320 | tf_op jit(solution)/shard_map/ppermute | solution.py:78
  21.5 0.7 collective-permute-done.2.refs_2_
  22.2 2.1 %collective-permute-done.4.refs_3_ = bf16[3,64,512]{2,1,0:T(8,128)(2,1)S(1)} collective-permute-done((bf16[3,64,512]{2,1,0:T(8,128)(2,1)S(1)}, bf16[3,64,512]{2,1,0:T(8,128)(2,1)S(1)}, u32[]{:S(2)}, u32[]{:S(2)}) %collective-permute-start.4) | collective-permute-done | bytes 196640 | tf_op jit(solution)/shard_map/ppermute | solution.py:73
  24.4 1.3 %collective-permute-start.5 = (bf16[3,64,512]{2,1,0:T(8,128)(2,1)S(1)}, bf16[3,64,512]{2,1,0:T(8,128)(2,1)S(1)}, u32[]{:S(2)}, u32[]{:S(2)}) collective-permute-start(bf16[3,64,512]{2,1,0:T(8,128)(2,1)S(1)} %get-tuple-element.42), channel_id=1, source_target_pairs={{0,2},{1,3},{2,0},{3,1},{4,6},{5,7},{6,4},{7,5},{8,10},{9,11},{10,... | collective-permute-start | bytes 589832 | tf_op jit(solution)/shard_map/ppermute | solution.py:73
  25.7 3.1 %collective-permute-start.8 = (bf16[512,512]{1,0:T(8,128)(2,1)S(1)}, bf16[512,512]{1,0:T(8,128)(2,1)S(1)}, u32[]{:S(2)}, u32[]{:S(2)}) collective-permute-start(bf16[512,512]{1,0:T(8,128)(2,1)S(1)} %collective-permute-done.3.odd_k), channel_id=1, source_target_pairs={{0,4},{4,8},{8,12},{12,16},{16,20},{20,24},{24,28},{1,5},{5,9},{9,... | collective-permute-start | bytes 1572872 | tf_op jit(solution)/shard_map/ppermute | solution.py:82
  28.8 3.9 %collective-permute-done.6.odd_v = bf16[512,512]{1,0:T(8,128)(2,1)S(1)} collective-permute-done((bf16[512,512]{1,0:T(8,128)(2,1)}, bf16[512,512]{1,0:T(8,128)(2,1)S(1)}, u32[]{:S(2)}, u32[]{:S(2)}) %collective-permute-start.6) | collective-permute-done | bytes 524320 | tf_op jit(solution)/shard_map/ppermute | solution.py:78
  32.7 4.2 %collective-permute-done.5 = bf16[3,64,512]{2,1,0:T(8,128)(2,1)S(1)} collective-permute-done((bf16[3,64,512]{2,1,0:T(8,128)(2,1)S(1)}, bf16[3,64,512]{2,1,0:T(8,128)(2,1)S(1)}, u32[]{:S(2)}, u32[]{:S(2)}) %collective-permute-start.5) | collective-permute-done | bytes 196640 | tf_op jit(solution)/shard_map/ppermute | solution.py:73
  37.0 0.4 collective-permute-start.7
  37.4 3.0 %collective-permute-start.13 = (bf16[512,512]{1,0:T(8,128)(2,1)S(1)}, bf16[512,512]{1,0:T(8,128)(2,1)S(1)}, u32[]{:S(2)}, u32[]{:S(2)}) collective-permute-start(bf16[512,512]{1,0:T(8,128)(2,1)S(1)} %collective-permute-done.6.odd_v), channel_id=1, source_target_pairs={{0,4},{4,8},{8,12},{12,16},{16,20},{20,24},{24,28},{1,5},{5,9},{9,... | collective-permute-start | bytes 1572872 | tf_op jit(solution)/shard_map/ppermute | solution.py:82
  40.4 5.0 %collective-permute-done.7 = bf16[3,64,512]{2,1,0:T(8,128)(2,1)S(1)} collective-permute-done((bf16[3,64,512]{2,1,0:T(8,128)(2,1)S(1)}, bf16[3,64,512]{2,1,0:T(8,128)(2,1)S(1)}, u32[]{:S(2)}, u32[]{:S(2)}) %collective-permute-start.7) | collective-permute-done | bytes 196640 | tf_op jit(solution)/shard_map/ppermute | solution.py:73
  45.5 0.8 collective-permute-start.9
  46.3 4.3 %collective-permute-done.9 = bf16[3,64,512]{2,1,0:T(8,128)(2,1)S(1)} collective-permute-done((bf16[3,64,512]{2,1,0:T(8,128)(2,1)S(1)}, bf16[3,64,512]{2,1,0:T(8,128)(2,1)S(1)}, u32[]{:S(2)}, u32[]{:S(2)}) %collective-permute-start.9) | collective-permute-done | bytes 196640 | tf_op jit(solution)/shard_map/ppermute | solution.py:73
  50.7 0.5 collective-permute-start.12
  51.2 1.1 %collective-permute-start.10 = (bf16[3,64,512]{2,1,0:T(8,128)(2,1)S(1)}, bf16[3,64,512]{2,1,0:T(8,128)(2,1)S(1)}, u32[]{:S(2)}, u32[]{:S(2)}) collective-permute-start(bf16[3,64,512]{2,1,0:T(8,128)(2,1)S(1)} %pad_maximum_fusion.2), channel_id=1, source_target_pairs={{0,8},{1,5},{2,10},{3,7},{4,12},{5,1},{6,14},{7,3},{8,0},{9,13},{1... | collective-permute-start | bytes 589832 | tf_op jit(solution)/shard_map/ppermute | solution.py:73
  52.3 9.2 %collective-permute-done.13.even_v = bf16[512,512]{1,0:T(8,128)(2,1)S(1)} collective-permute-done((bf16[512,512]{1,0:T(8,128)(2,1)S(1)}, bf16[512,512]{1,0:T(8,128)(2,1)S(1)}, u32[]{:S(2)}, u32[]{:S(2)}) %collective-permute-start.13) | collective-permute-done | bytes 524320 | tf_op jit(solution)/shard_map/ppermute | solution.py:82
  61.5 2.4 %collective-permute-done.12 = bf16[3,64,512]{2,1,0:T(8,128)(2,1)S(1)} collective-permute-done((bf16[3,64,512]{2,1,0:T(8,128)(2,1)S(1)}, bf16[3,64,512]{2,1,0:T(8,128)(2,1)S(1)}, u32[]{:S(2)}, u32[]{:S(2)}) %collective-permute-start.12) | collective-permute-done | bytes 196640 | tf_op jit(solution)/shard_map/ppermute | solution.py:73
  64.0 2.7 %collective-permute-done.10 = bf16[3,64,512]{2,1,0:T(8,128)(2,1)S(1)} collective-permute-done((bf16[3,64,512]{2,1,0:T(8,128)(2,1)S(1)}, bf16[3,64,512]{2,1,0:T(8,128)(2,1)S(1)}, u32[]{:S(2)}, u32[]{:S(2)}) %collective-permute-start.10) | collective-permute-done | bytes 196640 | tf_op jit(solution)/shard_map/ppermute | solution.py:73
  66.9 5.3 %window_attention.1 = (f32[768,512]{1,0:T(8,128)S(1)}, f32[3,8,512]{2,1,0:T(8,128)S(1)}) custom-call(bf16[768,512]{1,0:T(8,128)(2,1)S(1)} %copy-done, bf16[768,512]{1,0:T(8,128)(2,1)S(1)} %copy-done.6, bf16[768,512]{1,0:T(8,128)(2,1)S(1)} %copy-done.7, bf16[512,512]{1,0:T(8,128)(2,1)S(1)} %collective-permute-done.3.odd_k, ...), custom_call_target="tpu_custom_call" | custom-call | flops 1207959552 | bytes 3145728 | tf_op jit(solution)/shard_map/window_attention/pallas_call | solution.py:352
  72.2 2.7 %collective-permute-done.11.refs_1_ = bf16[3,128,512]{2,1,0:T(8,128)(2,1)S(1)} collective-permute-done((bf16[3,128,512]{2,1,0:T(8,128)(2,1)S(1)}, bf16[3,128,512]{2,1,0:T(8,128)(2,1)S(1)}, u32[]{:S(2)}, u32[]{:S(2)}) %collective-permute-start.11) | collective-permute-done | bytes 393248 | tf_op jit(solution)/shard_map/ppermute | solution.py:73
  74.9 3.5 %apply.1 = (f32[768,512]{1,0:T(8,128)S(1)}, f32[8,768]{1,0:T(8,128)S(1)}, bf16[32,512]{1,0:T(8,128)(2,1)}, bf16[32,512]{1,0:T(8,128)(2,1)}, bf16[32,512]{1,0:T(8,128)(2,1)}) custom-call(bf16[3,128,512]{2,1,0:T(8,128)(2,1)S(1)} %pad_maximum_fusion.refs_0_, bf16[3,128,512]{2,1,0:T(8,128)(2,1)S(1)} %collective-permute-done.11.refs_1_, ...), custom_call_target="tpu_custom_call" | custom-call | flops 1207959552 | bytes 4718592 | tf_op jit(solution)/shard_map/apply/pallas_call | solution.py:374
  78.4 0.3 collective-permute-start.15
  78.7 0.9 %collective-permute-done.15.more_ref = f32[8,768]{1,0:T(8,128)S(1)} collective-permute-done((f32[8,768]{1,0:T(8,128)S(1)}, f32[8,768]{1,0:T(8,128)S(1)}, u32[]{:S(2)}, u32[]{:S(2)}) %collective-permute-start.15) | collective-permute-done | bytes 24608 | tf_op jit(solution)/shard_map/ppermute | solution.py:398
  79.6 1.2 %norm.1 = bf16[768,512]{1,0:T(8,128)(2,1)} custom-call(f32[768,512]{1,0:T(8,128)S(1)} %get-tuple-element.53.combined_ref, f32[8,768]{1,0:T(8,128)S(1)} %get-tuple-element.54.sums_ref, f32[8,768]{1,0:T(8,128)S(1)} %collective-permute-done.15.more_ref, f32[1,512]{1,0:T(1,128)S(1)} %bitcast.2), custom_call_target="tpu_custom_call" | custom-call | flops 1572864 | bytes 2359296 | tf_op jit(solution)/shard_map/norm/pallas_call | solution.py:406
  (33 shorter events, 0.8 us)
Async XLA Ops:
  7.6 11.4 %copy-start.4 = (f32[3,128,512]{2,1,0:T(8,128)S(1)}, f32[3,128,512]{2,1,0:T(8,128)}, u32[]{:S(2)}) copy-start(f32[3,128,512]{2,1,0:T(8,128)} %get-tuple-element.34.refs_0_) | copy-start | bytes 2359300
  7.6 7.2 %collective-permute-start = (bf16[3,128,512]{2,1,0:T(8,128)(2,1)}, bf16[3,128,512]{2,1,0:T(8,128)(2,1)S(1)}, u32[]{:S(2)}, u32[]{:S(2)}) collective-permute-start(bf16[3,128,512]{2,1,0:T(8,128)(2,1)} %get-tuple-element.32), channel_id=1, source_target_pairs={{0,4},{1,9},{2,6},{3,11},{4,0},{5,13},{6,2},{7,15},{8,12},{9,1},{1... | collective-permute-start | bytes 1179656 | tf_op jit(solution)/shard_map/ppermute | solution.py:73
  8.9 10.1 %collective-permute-start.1 = (bf16[3,128,512]{2,1,0:T(8,128)(2,1)}, bf16[3,128,512]{2,1,0:T(8,128)(2,1)S(1)}, u32[]{:S(2)}, u32[]{:S(2)}) collective-permute-start(bf16[3,128,512]{2,1,0:T(8,128)(2,1)} %get-tuple-element.35), channel_id=1, source_target_pairs={{0,4},{1,9},{2,6},{3,11},{4,0},{5,13},{6,2},{7,15},{8,12},{9,1},{1... | collective-permute-start | bytes 1179656 | tf_op jit(solution)/shard_map/ppermute | solution.py:73
  9.1 12.4 %collective-permute-start.3 = (bf16[512,512]{1,0:T(8,128)(2,1)}, bf16[512,512]{1,0:T(8,128)(2,1)S(1)}, u32[]{:S(2)}, u32[]{:S(2)}) collective-permute-start(bf16[512,512]{1,0:T(8,128)(2,1)} %get-tuple-element.38), channel_id=1, source_target_pairs={{0,2},{2,0},{4,6},{6,4},{8,10},{10,8},{12,14},{14,12},{16,18},{18,... | collective-permute-start | bytes 1572872 | tf_op jit(solution)/shard_map/ppermute | solution.py:78
  10.3 22.4 %collective-permute-start.6 = (bf16[512,512]{1,0:T(8,128)(2,1)}, bf16[512,512]{1,0:T(8,128)(2,1)S(1)}, u32[]{:S(2)}, u32[]{:S(2)}) collective-permute-start(bf16[512,512]{1,0:T(8,128)(2,1)} %get-tuple-element.43), channel_id=1, source_target_pairs={{0,2},{2,0},{4,6},{6,4},{8,10},{10,8},{12,14},{14,12},{16,18},{18,... | collective-permute-start | bytes 1572872 | tf_op jit(solution)/shard_map/ppermute | solution.py:78
  14.8 1.1 %copy-start.5 = (f32[3,128,512]{2,1,0:T(8,128)S(1)}, f32[3,128,512]{2,1,0:T(8,128)}, u32[]{:S(2)}) copy-start(f32[3,128,512]{2,1,0:T(8,128)} %get-tuple-element.31.refs_0_) | copy-start | bytes 2359300
  16.0 6.3 %collective-permute-start.2 = (bf16[3,64,512]{2,1,0:T(8,128)(2,1)S(1)}, bf16[3,64,512]{2,1,0:T(8,128)(2,1)S(1)}, u32[]{:S(2)}, u32[]{:S(2)}) collective-permute-start(bf16[3,64,512]{2,1,0:T(8,128)(2,1)S(1)} %get-tuple-element.37), channel_id=1, source_target_pairs={{0,8},{1,5},{2,10},{3,7},{4,12},{5,1},{6,14},{7,3},{8,0},{9,13},{1... | collective-permute-start | bytes 589832 | tf_op jit(solution)/shard_map/ppermute | solution.py:73
  19.1 5.3 %collective-permute-start.4 = (bf16[3,64,512]{2,1,0:T(8,128)(2,1)S(1)}, bf16[3,64,512]{2,1,0:T(8,128)(2,1)S(1)}, u32[]{:S(2)}, u32[]{:S(2)}) collective-permute-start(bf16[3,64,512]{2,1,0:T(8,128)(2,1)S(1)} %get-tuple-element.40), channel_id=1, source_target_pairs={{0,8},{1,5},{2,10},{3,7},{4,12},{5,1},{6,14},{7,3},{8,0},{9,13},{1... | collective-permute-start | bytes 589832 | tf_op jit(solution)/shard_map/ppermute | solution.py:73
  24.4 12.6 %collective-permute-start.5 = (bf16[3,64,512]{2,1,0:T(8,128)(2,1)S(1)}, bf16[3,64,512]{2,1,0:T(8,128)(2,1)S(1)}, u32[]{:S(2)}, u32[]{:S(2)}) collective-permute-start(bf16[3,64,512]{2,1,0:T(8,128)(2,1)S(1)} %get-tuple-element.42), channel_id=1, source_target_pairs={{0,2},{1,3},{2,0},{3,1},{4,6},{5,7},{6,4},{7,5},{8,10},{9,11},{10,... | collective-permute-start | bytes 589832 | tf_op jit(solution)/shard_map/ppermute | solution.py:73
  25.7 19.7 %collective-permute-start.8 = (bf16[512,512]{1,0:T(8,128)(2,1)S(1)}, bf16[512,512]{1,0:T(8,128)(2,1)S(1)}, u32[]{:S(2)}, u32[]{:S(2)}) collective-permute-start(bf16[512,512]{1,0:T(8,128)(2,1)S(1)} %collective-permute-done.3.odd_k), channel_id=1, source_target_pairs={{0,4},{4,8},{8,12},{12,16},{16,20},{20,24},{24,28},{1,5},{5,9},{9,... | collective-permute-start | bytes 1572872 | tf_op jit(solution)/shard_map/ppermute | solution.py:82
  36.9 29.9 %copy-start.7 = (bf16[768,512]{1,0:T(8,128)(2,1)S(1)}, bf16[768,512]{1,0:T(8,128)(2,1)}, u32[]{:S(2)}) copy-start(bf16[768,512]{1,0:T(8,128)(2,1)} %v_ref.1) | copy-start | bytes 2359300
  37.0 8.4 %collective-permute-start.7 = (bf16[3,64,512]{2,1,0:T(8,128)(2,1)S(1)}, bf16[3,64,512]{2,1,0:T(8,128)(2,1)S(1)}, u32[]{:S(2)}, u32[]{:S(2)}) collective-permute-start(bf16[3,64,512]{2,1,0:T(8,128)(2,1)S(1)} %add_convert_fusion.1), channel_id=1, source_target_pairs={{0,16},{1,17},{2,18},{3,19},{4,20},{5,21},{6,22},{7,23},{8,24},{9,... | collective-permute-start | bytes 589832 | tf_op jit(solution)/shard_map/ppermute | solution.py:73
  37.4 24.2 %collective-permute-start.13 = (bf16[512,512]{1,0:T(8,128)(2,1)S(1)}, bf16[512,512]{1,0:T(8,128)(2,1)S(1)}, u32[]{:S(2)}, u32[]{:S(2)}) collective-permute-start(bf16[512,512]{1,0:T(8,128)(2,1)S(1)} %collective-permute-done.6.odd_v), channel_id=1, source_target_pairs={{0,4},{4,8},{8,12},{12,16},{16,20},{20,24},{24,28},{1,5},{5,9},{9,... | collective-permute-start | bytes 1572872 | tf_op jit(solution)/shard_map/ppermute | solution.py:82
  45.4 21.4 %copy-start = (bf16[768,512]{1,0:T(8,128)(2,1)S(1)}, bf16[768,512]{1,0:T(8,128)(2,1)}, u32[]{:S(2)}) copy-start(bf16[768,512]{1,0:T(8,128)(2,1)} %refs_4_.3) | copy-start | bytes 2359300
  45.5 21.4 %copy-start.1 = (bf16[512,512]{1,0:T(8,128)(2,1)S(1)}, bf16[512,512]{1,0:T(8,128)(2,1)}, u32[]{:S(2)}) copy-start(bf16[512,512]{1,0:T(8,128)(2,1)} %refs_5_.1) | copy-start | bytes 1572868
  45.5 21.4 %copy-start.2 = (bf16[512,512]{1,0:T(8,128)(2,1)S(1)}, bf16[512,512]{1,0:T(8,128)(2,1)}, u32[]{:S(2)}) copy-start(bf16[512,512]{1,0:T(8,128)(2,1)} %refs_6_.1) | copy-start | bytes 1572868
  45.5 21.4 %copy-start.3 = (bf16[512,512]{1,0:T(8,128)(2,1)S(1)}, bf16[512,512]{1,0:T(8,128)(2,1)}, u32[]{:S(2)}) copy-start(bf16[512,512]{1,0:T(8,128)(2,1)} %refs_7_.1) | copy-start | bytes 1572868
  45.5 21.4 %copy-start.6 = (bf16[768,512]{1,0:T(8,128)(2,1)S(1)}, bf16[768,512]{1,0:T(8,128)(2,1)}, u32[]{:S(2)}) copy-start(bf16[768,512]{1,0:T(8,128)(2,1)} %k_ref.1) | copy-start | bytes 2359300
  45.5 5.1 %collective-permute-start.9 = (bf16[3,64,512]{2,1,0:T(8,128)(2,1)S(1)}, bf16[3,64,512]{2,1,0:T(8,128)(2,1)S(1)}, u32[]{:S(2)}, u32[]{:S(2)}) collective-permute-start(bf16[3,64,512]{2,1,0:T(8,128)(2,1)S(1)} %add_convert_fusion), channel_id=1, source_target_pairs={{0,2},{1,3},{2,0},{3,1},{4,6},{5,7},{6,4},{7,5},{8,10},{9,11},{10,... | collective-permute-start | bytes 589832 | tf_op jit(solution)/shard_map/ppermute | solution.py:73
  50.7 13.2 %collective-permute-start.12 = (bf16[3,64,512]{2,1,0:T(8,128)(2,1)S(1)}, bf16[3,64,512]{2,1,0:T(8,128)(2,1)S(1)}, u32[]{:S(2)}, u32[]{:S(2)}) collective-permute-start(bf16[3,64,512]{2,1,0:T(8,128)(2,1)S(1)} %pad_maximum_fusion.3), channel_id=1, source_target_pairs={{0,8},{1,5},{2,10},{3,7},{4,12},{5,1},{6,14},{7,3},{8,0},{9,13},{1... | collective-permute-start | bytes 589832 | tf_op jit(solution)/shard_map/ppermute | solution.py:73
  51.2 15.5 %collective-permute-start.10 = (bf16[3,64,512]{2,1,0:T(8,128)(2,1)S(1)}, bf16[3,64,512]{2,1,0:T(8,128)(2,1)S(1)}, u32[]{:S(2)}, u32[]{:S(2)}) collective-permute-start(bf16[3,64,512]{2,1,0:T(8,128)(2,1)S(1)} %pad_maximum_fusion.2), channel_id=1, source_target_pairs={{0,8},{1,5},{2,10},{3,7},{4,12},{5,1},{6,14},{7,3},{8,0},{9,13},{1... | collective-permute-start | bytes 589832 | tf_op jit(solution)/shard_map/ppermute | solution.py:73
  63.9 8.2 %collective-permute-start.14 = (bf16[3,128,512]{2,1,0:T(8,128)(2,1)S(1)}, bf16[3,128,512]{2,1,0:T(8,128)(2,1)S(1)}, u32[]{:S(2)}, u32[]{:S(2)}) collective-permute-start(bf16[3,128,512]{2,1,0:T(8,128)(2,1)S(1)} %pad_maximum_fusion.1.refs_2_), channel_id=1, source_target_pairs={{0,4},{1,9},{2,6},{3,11},{4,0},{5,13},{6,2},{7,15},{8,12},{9,1},{1... | collective-permute-start | bytes 1179656 | tf_op jit(solution)/shard_map/ppermute | solution.py:73
  66.7 8.1 %collective-permute-start.11 = (bf16[3,128,512]{2,1,0:T(8,128)(2,1)S(1)}, bf16[3,128,512]{2,1,0:T(8,128)(2,1)S(1)}, u32[]{:S(2)}, u32[]{:S(2)}) collective-permute-start(bf16[3,128,512]{2,1,0:T(8,128)(2,1)S(1)} %pad_maximum_fusion.refs_0_), channel_id=1, source_target_pairs={{0,4},{1,9},{2,6},{3,11},{4,0},{5,13},{6,2},{7,15},{8,12},{9,1},{1... | collective-permute-start | bytes 1179656 | tf_op jit(solution)/shard_map/ppermute | solution.py:73
  74.9 4.7 %copy-start.8 = (f32[512]{0:T(512)S(1)}, f32[512]{0:T(512)}, u32[]{:S(2)}) copy-start(f32[512]{0:T(512)} %param.15) | copy-start | bytes 6148
  78.4 1.2 %collective-permute-start.15 = (f32[8,768]{1,0:T(8,128)S(1)}, f32[8,768]{1,0:T(8,128)S(1)}, u32[]{:S(2)}, u32[]{:S(2)}) collective-permute-start(f32[8,768]{1,0:T(8,128)S(1)} %get-tuple-element.54.sums_ref), channel_id=1, source_target_pairs={{0,1},{1,0},{2,3},{3,2},{4,5},{5,4},{6,7},{7,6},{8,9},{9,8},{10,11... | collective-permute-start | bytes 73736 | tf_op jit(solution)/shard_map/ppermute | solution.py:398

commit v5 on v4

--- a/solution.py
+++ b/solution.py
@@ -71,6 +71,17 @@
         for h in range(heads)
     ]
     return lax.ppermute(x, ("seq", "head"), pairs)
+
+
+def pass_odd(x):
+    return lax.ppermute(x, "seq", [(i, i + 2) for i in range(1, lax.axis_size("seq") - 2, 2)])
+
+
+def shift_passed(x, passed):
+    peers = lax.axis_size("seq")
+    odd = lax.axis_index("seq") % 2 == 1
+    pairs = [(i, i + 1) for i in range(0, peers, 2)] + [(i, i - 1) for i in range(1, peers, 2)]
+    return lax.ppermute(jnp.where(odd, passed, x), "seq", pairs)
 
 
 def trade(x):
@@ -171,23 +182,23 @@
 
 
 def attend_kernel(
-    q_ref, k_ref, v_ref, odd_k, odd_v, even_k, even_v, gate_ref, up_ref, down_ref, out_ref, square_ref, prev_ref, sems
+    q_ref, k_ref, v_ref, odd_k, even_k, prev_v, gate_ref, up_ref, down_ref, out_ref, square_ref, prev_ref, sems
 ):
     rows = q_ref.shape[0]
     odd = lax.axis_index("seq") % 2 == 1
+    value_copy = pltpu.make_async_copy(prev_v, prev_ref.at[1], sems.at[1])
+    value_copy.start()
 
     @pl.when(odd)
     def _():
         pltpu.make_async_copy(odd_k, prev_ref.at[0], sems.at[0]).start()
-        pltpu.make_async_copy(odd_v, prev_ref.at[1], sems.at[1]).start()
 
     @pl.when(jnp.logical_not(odd))
     def _():
         pltpu.make_async_copy(even_k, prev_ref.at[0], sems.at[0]).start()
-        pltpu.make_async_copy(even_v, prev_ref.at[1], sems.at[1]).start()
 
     pltpu.make_async_copy(even_k, prev_ref.at[0], sems.at[0]).wait()
-    pltpu.make_async_copy(even_v, prev_ref.at[1], sems.at[1]).wait()
+    value_copy.wait()
     reach = WINDOW // BLOCK
     row_at = lax.broadcasted_iota(jnp.int32, (BLOCK, BLOCK), 0)
     col_at = lax.broadcasted_iota(jnp.int32, (BLOCK, BLOCK), 1)
@@ -321,20 +332,18 @@
     )(keys, values, *weights, rates.reshape(1, tok_rows))
     sent, kept = parts[:CHUNKS], parts[CHUNKS:]
     came = [swap(x, steps[0]) for x in sent]
-    beside_k, beside_v = trade(key_tail), trade(value_tail)
+    beside_k = trade(key_tail)
     folded = [fold(steps[1], [k], [c]) for k, c in zip(kept, came)]
     came = [swap(x, steps[1]) for x, _ in folded]
     came[0], beside_k = lax.optimization_barrier((came[0], beside_k))
     before_k = pass_on(beside_k)
+    passed = pass_odd(value_tail)
     sent, kept = fold(steps[2], [k for _, k in folded], came)
-    came, beside_v = lax.optimization_barrier((swap(sent, steps[2]), beside_v))
-    before_v = pass_on(beside_v)
+    came = swap(sent, steps[2])
     total = kept + came.astype(F32)
     for masks in others:
         total = total.astype(BF16)
         came = swap(total, masks)
-        if masks == others[-1]:
-            came, before_k = lax.optimization_barrier((came, before_k))
         total = total.astype(F32) + came.astype(F32)
     total = total.astype(BF16)
     more = swap(total, steps[2])
@@ -344,8 +353,11 @@
         here = slice(c * rows, (c + 1) * rows)
         piece = jnp.concatenate([total[:, here], more[:, here]], axis=1)
         came = swap(piece, steps[1])
+        if c == 0:
+            came, passed = lax.optimization_barrier((came, passed))
+            prev_v = shift_passed(value_tail, passed)
         if c == 1:
-            came, before_v = lax.optimization_barrier((came, before_v))
+            came, before_k = lax.optimization_barrier((came, before_k))
         piece = jnp.concatenate([piece, came], axis=1)
         pieces += [piece, swap(piece, steps[0])]
 
@@ -356,7 +368,7 @@
             jax.ShapeDtypeStruct((3, 8, w_cols), F32),
         ),
         in_specs=[pl.BlockSpec(memory_space=pltpu.VMEM)] * 3
-        + [hbm] * 4
+        + [hbm] * 3
         + [pl.BlockSpec(memory_space=pltpu.VMEM)] * 3,
         name="window_attention",
         scratch_shapes=[pltpu.VMEM((2, WINDOW, fw_dim), BF16), pltpu.SemaphoreType.DMA((2,))],
@@ -366,7 +378,7 @@
             bytes_accessed=8 * tok_rows * fw_dim,
             transcendentals=0,
         ),
-    )(queries, keys, values, beside_k, beside_v, before_k, before_v, *weights)
+    )(queries, keys, values, beside_k, before_k, prev_v, *weights)
 
     part_rows = w_rows // seq_count
     kept_rows = max(part_rows, SUBROWS)

time: 81 us -> 79.2 us (0.978)
  waiting for transfers between devices: 45.2 us -> 41.6 us
  other arithmetic: 0.17 us -> 1.15 us
    ppermute x0 -> x2, waiting for transfers between devices: none -> 9.39 us  [the longest x1 9.38 us: shift_passed(): return lax.ppermute(jnp.where(odd, passed, x), 'seq', pairs)]
    ppermute x2 -> x1, waiting for transfers between devices: 9.23 us -> 0.01 us  [pass_on(): lax.ppermute(x, 'seq', [(i, i + 2) for i in range(0, lax.axis_size('seq')...]
    ppermute x2 -> x1, waiting for transfers between devices: 5.06 us -> 1.14 us  [trade(): return lax.ppermute(x, 'seq', [(i, i ^ 1) for i in range(peers)])]
    ppermute x2 -> x1, starting transfers between devices: 6.14 us -> 3.17 us  [pass_on(): lax.ppermute(x, 'seq', [(i, i + 2) for i in range(0, lax.axis_size('seq')...]
    ppermute x0 -> x2, starting transfers between devices: none -> 1.97 us  [the longest x1 1.28 us: shift_passed(): return lax.ppermute(jnp.where(odd, passed, x), 'seq', pairs)]
    ppermute x11, starting transfers between devices: 8.31 us -> 9.96 us  [swap(): return lax.ppermute(x, ('seq', 'head'), pairs)]
    concatenate x2, other arithmetic: 0.05 us -> 0.98 us  [body(): piece = jnp.concatenate([piece, came], axis=1)]
  transfers between devices with their start and end apart: 16 -> 16, of which waited for: 14 -> 12; matrix products, arithmetic and copies ran while one was open for 0% -> 1% of each run, Pallas kernels for 7% -> 7%
where the time goes in v5:
time: 79.2 us; the launch traced here: 79 us
  waiting for transfers between devices  41.6 us (53%)
  Pallas kernels  17.2 us (22%)
  starting transfers between devices  17 us (21%)
  local copies, waits for them, and re-layouts  1.21 us (2%)
  other arithmetic  1.15 us (1%)
  between operations  0.85 us (1%)
    ppermute x11, waiting for transfers between devices, swap(): return lax.ppermute(x, ('seq', 'head'), pairs)  30.2 us
    ppermute x11, starting transfers between devices, swap(): return lax.ppermute(x, ('seq', 'head'), pairs)  9.96 us
    ppermute x1, waiting for transfers between devices, shift_passed(): return lax.ppermute(jnp.where(odd, passed, x), 'seq', pairs)  9.38 us
    pallas_call x1, Pallas kernels, body(): pl.pallas_call(functools.partial(grads_kernel, steps[0]), out_shape=[jax....  6.94 us
    pallas_call x1, Pallas kernels, body(): pl.pallas_call(attend_kernel, out_shape=(jax.ShapeDtypeStruct((tok_rows,...  5.3 us
    pallas_call x1, Pallas kernels, body(): pl.pallas_call(functools.partial(apply_kernel, steps, part_rows), out_sha...  3.51 us
    ppermute x1, starting transfers between devices, pass_on(): lax.ppermute(x, 'seq', [(i, i + 2) for i in range(0, lax.axis_size('seq')...  3.17 us
  transfers between devices with their start and end apart: 16, of which 12 were waited for; matrix products, arithmetic and copies ran while one was open for 1% of the time, Pallas kernels for 7%

profile of v5, /device:TPU:17, one launch (start us, length us, event | category | flops | bytes accessed | tf_op | source)
XLA Modules:
  0.0 79.0 jit_solution(3739168408187974427)
XLA Ops:
  0.6 6.9 %gradients.1 = (bf16[512,512]{1,0:T(8,128)(2,1)}, bf16[512,512]{1,0:T(8,128)(2,1)}, bf16[3,128,512]{2,1,0:T(8,128)(2,1)}, bf16[3,128,512]{2,1,0:T(8,128)(2,1)}, ...) custom-call(bf16[768,512]{1,0:T(8,128)(2,1)} %k_ref.1, bf16[768,512]{1,0:T(8,128)(2,1)} %v_ref.1, ...), custom_call_target="tpu_custom_call" | custom-call | flops 2415919104 | bytes 6291456 | tf_op jit(solution)/shard_map/gradients/pallas_call | solution.py:303
  7.6 1.4 %collective-permute-start = (bf16[3,128,512]{2,1,0:T(8,128)(2,1)}, bf16[3,128,512]{2,1,0:T(8,128)(2,1)S(1)}, u32[]{:S(2)}, u32[]{:S(2)}) collective-permute-start(bf16[3,128,512]{2,1,0:T(8,128)(2,1)} %get-tuple-element.30), channel_id=1, source_target_pairs={{0,4},{1,9},{2,6},{3,11},{4,0},{5,13},{6,2},{7,15},{8,12},{9,1},{1... | collective-permute-start | bytes 1179656 | tf_op jit(solution)/shard_map/ppermute | solution.py:73
  9.1 1.2 %collective-permute-start.3 = (bf16[512,512]{1,0:T(8,128)(2,1)}, bf16[512,512]{1,0:T(8,128)(2,1)S(1)}, u32[]{:S(2)}, u32[]{:S(2)}) collective-permute-start(bf16[512,512]{1,0:T(8,128)(2,1)} %get-tuple-element.36), channel_id=1, source_target_pairs={{0,2},{2,0},{4,6},{6,4},{8,10},{10,8},{12,14},{14,12},{16,18},{18,... | collective-permute-start | bytes 1572872 | tf_op jit(solution)/shard_map/ppermute | solution.py:89
  10.3 4.5 %collective-permute-done.refs_1_ = bf16[3,128,512]{2,1,0:T(8,128)(2,1)S(1)} collective-permute-done((bf16[3,128,512]{2,1,0:T(8,128)(2,1)}, bf16[3,128,512]{2,1,0:T(8,128)(2,1)S(1)}, u32[]{:S(2)}, u32[]{:S(2)}) %collective-permute-start) | collective-permute-done | bytes 393248 | tf_op jit(solution)/shard_map/ppermute | solution.py:73
  14.8 1.1 %copy-done.5 = f32[3,128,512]{2,1,0:T(8,128)S(1)} copy-done((f32[3,128,512]{2,1,0:T(8,128)S(1)}, f32[3,128,512]{2,1,0:T(8,128)}, u32[]{:S(2)}) %copy-start.5) | copy-done | bytes 786456
  16.0 1.3 %collective-permute-start.2 = (bf16[3,64,512]{2,1,0:T(8,128)(2,1)S(1)}, bf16[3,64,512]{2,1,0:T(8,128)(2,1)S(1)}, u32[]{:S(2)}, u32[]{:S(2)}) collective-permute-start(bf16[3,64,512]{2,1,0:T(8,128)(2,1)S(1)} %get-tuple-element.35), channel_id=1, source_target_pairs={{0,8},{1,5},{2,10},{3,7},{4,12},{5,1},{6,14},{7,3},{8,0},{9,13},{1... | collective-permute-start | bytes 589832 | tf_op jit(solution)/shard_map/ppermute | solution.py:73
  17.3 1.7 %collective-permute-done.1.refs_1_ = bf16[3,128,512]{2,1,0:T(8,128)(2,1)S(1)} collective-permute-done((bf16[3,128,512]{2,1,0:T(8,128)(2,1)}, bf16[3,128,512]{2,1,0:T(8,128)(2,1)S(1)}, u32[]{:S(2)}, u32[]{:S(2)}) %collective-permute-start.1) | collective-permute-done | bytes 393248 | tf_op jit(solution)/shard_map/ppermute | solution.py:73
  19.1 1.3 %collective-permute-start.4 = (bf16[3,64,512]{2,1,0:T(8,128)(2,1)S(1)}, bf16[3,64,512]{2,1,0:T(8,128)(2,1)S(1)}, u32[]{:S(2)}, u32[]{:S(2)}) collective-permute-start(bf16[3,64,512]{2,1,0:T(8,128)(2,1)S(1)} %get-tuple-element.38), channel_id=1, source_target_pairs={{0,8},{1,5},{2,10},{3,7},{4,12},{5,1},{6,14},{7,3},{8,0},{9,13},{1... | collective-permute-start | bytes 589832 | tf_op jit(solution)/shard_map/ppermute | solution.py:73
  20.4 1.1 %collective-permute-done.3.odd_k = bf16[512,512]{1,0:T(8,128)(2,1)S(1)} collective-permute-done((bf16[512,512]{1,0:T(8,128)(2,1)}, bf16[512,512]{1,0:T(8,128)(2,1)S(1)}, u32[]{:S(2)}, u32[]{:S(2)}) %collective-permute-start.3) | collective-permute-done | bytes 524320 | tf_op jit(solution)/shard_map/ppermute | solution.py:89
  21.5 0.7 collective-permute-done.2.refs_2_
  22.2 1.8 %collective-permute-done.4.refs_3_ = bf16[3,64,512]{2,1,0:T(8,128)(2,1)S(1)} collective-permute-done((bf16[3,64,512]{2,1,0:T(8,128)(2,1)S(1)}, bf16[3,64,512]{2,1,0:T(8,128)(2,1)S(1)}, u32[]{:S(2)}, u32[]{:S(2)}) %collective-permute-start.4) | collective-permute-done | bytes 196640 | tf_op jit(solution)/shard_map/ppermute | solution.py:73
  24.1 1.3 %collective-permute-start.5 = (bf16[3,64,512]{2,1,0:T(8,128)(2,1)S(1)}, bf16[3,64,512]{2,1,0:T(8,128)(2,1)S(1)}, u32[]{:S(2)}, u32[]{:S(2)}) collective-permute-start(bf16[3,64,512]{2,1,0:T(8,128)(2,1)S(1)} %get-tuple-element.40), channel_id=1, source_target_pairs={{0,2},{1,3},{2,0},{3,1},{4,6},{5,7},{6,4},{7,5},{8,10},{9,11},{10,... | collective-permute-start | bytes 589832 | tf_op jit(solution)/shard_map/ppermute | solution.py:73
  25.4 3.3 %collective-permute-done.5 = bf16[3,64,512]{2,1,0:T(8,128)(2,1)S(1)} collective-permute-done((bf16[3,64,512]{2,1,0:T(8,128)(2,1)S(1)}, bf16[3,64,512]{2,1,0:T(8,128)(2,1)S(1)}, u32[]{:S(2)}, u32[]{:S(2)}) %collective-permute-start.5) | collective-permute-done | bytes 196640 | tf_op jit(solution)/shard_map/ppermute | solution.py:73
  28.8 0.7 collective-permute-start.9
  29.5 3.2 %collective-permute-start.12 = (bf16[512,512]{1,0:T(8,128)(2,1)S(1)}, bf16[512,512]{1,0:T(8,128)(2,1)S(1)}, u32[]{:S(2)}, u32[]{:S(2)}) collective-permute-start(bf16[512,512]{1,0:T(8,128)(2,1)S(1)} %collective-permute-done.3.odd_k), channel_id=1, source_target_pairs={{0,4},{4,8},{8,12},{12,16},{16,20},{20,24},{24,28},{1,5},{5,9},{9,... | collective-permute-start | bytes 1572872 | tf_op jit(solution)/shard_map/ppermute | solution.py:93
  32.7 1.6 %collective-permute-done.6 = bf16[3,64,512]{2,1,0:T(8,128)(2,1)S(1)} collective-permute-done((bf16[3,64,512]{2,1,0:T(8,128)(2,1)S(1)}, bf16[3,64,512]{2,1,0:T(8,128)(2,1)S(1)}, u32[]{:S(2)}, u32[]{:S(2)}) %collective-permute-start.6) | collective-permute-done | bytes 196640 | tf_op jit(solution)/shard_map/ppermute | solution.py:73
  34.4 1.3 %collective-permute-start.7 = (bf16[3,64,512]{2,1,0:T(8,128)(2,1)S(1)}, bf16[3,64,512]{2,1,0:T(8,128)(2,1)S(1)}, u32[]{:S(2)}, u32[]{:S(2)}) collective-permute-start(bf16[3,64,512]{2,1,0:T(8,128)(2,1)S(1)} %add_convert_fusion), channel_id=1, source_target_pairs={{0,2},{1,3},{2,0},{3,1},{4,6},{5,7},{6,4},{7,5},{8,10},{9,11},{10,... | collective-permute-start | bytes 589832 | tf_op jit(solution)/shard_map/ppermute | solution.py:73
  35.7 3.6 %collective-permute-done.7 = bf16[3,64,512]{2,1,0:T(8,128)(2,1)S(1)} collective-permute-done((bf16[3,64,512]{2,1,0:T(8,128)(2,1)S(1)}, bf16[3,64,512]{2,1,0:T(8,128)(2,1)S(1)}, u32[]{:S(2)}, u32[]{:S(2)}) %collective-permute-start.7) | collective-permute-done | bytes 196640 | tf_op jit(solution)/shard_map/ppermute | solution.py:73
  39.3 1.3 %collective-permute-start.8 = (bf16[3,64,512]{2,1,0:T(8,128)(2,1)S(1)}, bf16[3,64,512]{2,1,0:T(8,128)(2,1)}, u32[]{:S(2)}, u32[]{:S(2)}) collective-permute-start(bf16[3,64,512]{2,1,0:T(8,128)(2,1)S(1)} %pad_maximum_fusion.2), channel_id=1, source_target_pairs={{0,8},{1,5},{2,10},{3,7},{4,12},{5,1},{6,14},{7,3},{8,0},{9,13},{1... | collective-permute-start | bytes 589832 | tf_op jit(solution)/shard_map/ppermute | solution.py:73
  40.7 0.3 collective-permute-start.11
  41.0 12.5 %collective-permute-done.8 = bf16[3,64,512]{2,1,0:T(8,128)(2,1)} collective-permute-done((bf16[3,64,512]{2,1,0:T(8,128)(2,1)S(1)}, bf16[3,64,512]{2,1,0:T(8,128)(2,1)}, u32[]{:S(2)}, u32[]{:S(2)}) %collective-permute-start.8) | collective-permute-done | bytes 196640 | tf_op jit(solution)/shard_map/ppermute | solution.py:73
  53.6 1.3 %collective-permute-start.14 = (bf16[512,512]{1,0:T(8,128)(2,1)S(1)}, bf16[512,512]{1,0:T(8,128)(2,1)S(1)}, u32[]{:S(2)}, u32[]{:S(2)}) collective-permute-start(bf16[512,512]{1,0:T(8,128)(2,1)S(1)} %broadcast_select_fusion), channel_id=1, source_target_pairs={{0,2},{4,6},{8,10},{12,14},{16,18},{20,22},{24,26},{28,30},{2,0},{... | collective-permute-start | bytes 1572872 | tf_op jit(solution)/shard_map/ppermute | solution.py:84
  54.9 0.5 collective-permute-done.11
  55.4 0.2 collective-permute-start.13
  55.5 1.0 %pad_maximum_fusion.refs_0_ = bf16[3,128,512]{2,1,0:T(8,128)(2,1)S(1)} fusion(bf16[3,64,512]{2,1,0:T(8,128)(2,1)} %collective-permute-done.8, bf16[3,32,512]{2,1,0:T(8,128)(2,1)S(1)} %get-tuple-element.57, bf16[3,32,512]{2,1,0:T(8,128)(2,1)S(1)} %get-tuple-element.55), kind=kLoop, calls=%fused_computation.1 | loop fusion | flops 1179648 | bytes 786432 | tf_op jit(solution)/shard_map/concatenate | solution.py:361
  56.5 1.4 %collective-permute-start.10 = (bf16[3,128,512]{2,1,0:T(8,128)(2,1)S(1)}, bf16[3,128,512]{2,1,0:T(8,128)(2,1)S(1)}, u32[]{:S(2)}, u32[]{:S(2)}) collective-permute-start(bf16[3,128,512]{2,1,0:T(8,128)(2,1)S(1)} %pad_maximum_fusion.refs_0_), channel_id=1, source_target_pairs={{0,4},{1,9},{2,6},{3,11},{4,0},{5,13},{6,2},{7,15},{8,12},{9,1},{1... | collective-permute-start | bytes 1179656 | tf_op jit(solution)/shard_map/ppermute | solution.py:73
  57.9 9.4 %collective-permute-done.14.prev_v = bf16[512,512]{1,0:T(8,128)(2,1)S(1)} collective-permute-done((bf16[512,512]{1,0:T(8,128)(2,1)S(1)}, bf16[512,512]{1,0:T(8,128)(2,1)S(1)}, u32[]{:S(2)}, u32[]{:S(2)}) %collective-permute-start.14) | collective-permute-done | bytes 524320 | tf_op jit(solution)/shard_map/ppermute | solution.py:84
  67.3 5.3 %window_attention.1 = (f32[768,512]{1,0:T(8,128)S(1)}, f32[3,8,512]{2,1,0:T(8,128)S(1)}) custom-call(bf16[768,512]{1,0:T(8,128)(2,1)S(1)} %copy-done, bf16[768,512]{1,0:T(8,128)(2,1)S(1)} %copy-done.6, bf16[768,512]{1,0:T(8,128)(2,1)S(1)} %copy-done.7, bf16[512,512]{1,0:T(8,128)(2,1)S(1)} %collective-permute-done.3.odd_k, ...), custom_call_target="tpu_custom_call" | custom-call | flops 1207959552 | bytes 3145728 | tf_op jit(solution)/shard_map/window_attention/pallas_call | solution.py:364
  72.7 3.5 %apply.1 = (f32[768,512]{1,0:T(8,128)S(1)}, f32[8,768]{1,0:T(8,128)S(1)}, bf16[32,512]{1,0:T(8,128)(2,1)}, bf16[32,512]{1,0:T(8,128)(2,1)}, bf16[32,512]{1,0:T(8,128)(2,1)}) custom-call(bf16[3,128,512]{2,1,0:T(8,128)(2,1)S(1)} %pad_maximum_fusion.refs_0_, bf16[3,128,512]{2,1,0:T(8,128)(2,1)S(1)} %collective-permute-done.10.refs_1_, ...), custom_call_target="tpu_custom_call" | custom-call | flops 1207959552 | bytes 4718592 | tf_op jit(solution)/shard_map/apply/pallas_call | solution.py:386
  76.2 0.7 collective-permute-start.15
  76.9 0.8 %collective-permute-done.15.more_ref = f32[8,768]{1,0:T(8,128)S(1)} collective-permute-done((f32[8,768]{1,0:T(8,128)S(1)}, f32[8,768]{1,0:T(8,128)S(1)}, u32[]{:S(2)}, u32[]{:S(2)}) %collective-permute-start.15) | collective-permute-done | bytes 24608 | tf_op jit(solution)/shard_map/ppermute | solution.py:410
  77.7 1.2 %norm.1 = bf16[768,512]{1,0:T(8,128)(2,1)} custom-call(f32[768,512]{1,0:T(8,128)S(1)} %get-tuple-element.49.combined_ref, f32[8,768]{1,0:T(8,128)S(1)} %get-tuple-element.50.sums_ref, f32[8,768]{1,0:T(8,128)S(1)} %collective-permute-done.15.more_ref, f32[1,512]{1,0:T(1,128)S(1)} %bitcast.2), custom_call_target="tpu_custom_call" | custom-call | flops 1572864 | bytes 2359296 | tf_op jit(solution)/shard_map/norm/pallas_call | solution.py:418
  (36 shorter events, 0.7 us)
Async XLA Ops:
  7.6 11.4 %copy-start.4 = (f32[3,128,512]{2,1,0:T(8,128)S(1)}, f32[3,128,512]{2,1,0:T(8,128)}, u32[]{:S(2)}) copy-start(f32[3,128,512]{2,1,0:T(8,128)} %get-tuple-element.32.refs_0_) | copy-start | bytes 2359300
  7.6 7.2 %collective-permute-start = (bf16[3,128,512]{2,1,0:T(8,128)(2,1)}, bf16[3,128,512]{2,1,0:T(8,128)(2,1)S(1)}, u32[]{:S(2)}, u32[]{:S(2)}) collective-permute-start(bf16[3,128,512]{2,1,0:T(8,128)(2,1)} %get-tuple-element.30), channel_id=1, source_target_pairs={{0,4},{1,9},{2,6},{3,11},{4,0},{5,13},{6,2},{7,15},{8,12},{9,1},{1... | collective-permute-start | bytes 1179656 | tf_op jit(solution)/shard_map/ppermute | solution.py:73
  8.9 10.1 %collective-permute-start.1 = (bf16[3,128,512]{2,1,0:T(8,128)(2,1)}, bf16[3,128,512]{2,1,0:T(8,128)(2,1)S(1)}, u32[]{:S(2)}, u32[]{:S(2)}) collective-permute-start(bf16[3,128,512]{2,1,0:T(8,128)(2,1)} %get-tuple-element.33), channel_id=1, source_target_pairs={{0,4},{1,9},{2,6},{3,11},{4,0},{5,13},{6,2},{7,15},{8,12},{9,1},{1... | collective-permute-start | bytes 1179656 | tf_op jit(solution)/shard_map/ppermute | solution.py:73
  9.1 12.4 %collective-permute-start.3 = (bf16[512,512]{1,0:T(8,128)(2,1)}, bf16[512,512]{1,0:T(8,128)(2,1)S(1)}, u32[]{:S(2)}, u32[]{:S(2)}) collective-permute-start(bf16[512,512]{1,0:T(8,128)(2,1)} %get-tuple-element.36), channel_id=1, source_target_pairs={{0,2},{2,0},{4,6},{6,4},{8,10},{10,8},{12,14},{14,12},{16,18},{18,... | collective-permute-start | bytes 1572872 | tf_op jit(solution)/shard_map/ppermute | solution.py:89
  14.8 1.1 %copy-start.5 = (f32[3,128,512]{2,1,0:T(8,128)S(1)}, f32[3,128,512]{2,1,0:T(8,128)}, u32[]{:S(2)}) copy-start(f32[3,128,512]{2,1,0:T(8,128)} %get-tuple-element.29.refs_0_) | copy-start | bytes 2359300
  16.0 6.3 %collective-permute-start.2 = (bf16[3,64,512]{2,1,0:T(8,128)(2,1)S(1)}, bf16[3,64,512]{2,1,0:T(8,128)(2,1)S(1)}, u32[]{:S(2)}, u32[]{:S(2)}) collective-permute-start(bf16[3,64,512]{2,1,0:T(8,128)(2,1)S(1)} %get-tuple-element.35), channel_id=1, source_target_pairs={{0,8},{1,5},{2,10},{3,7},{4,12},{5,1},{6,14},{7,3},{8,0},{9,13},{1... | collective-permute-start | bytes 589832 | tf_op jit(solution)/shard_map/ppermute | solution.py:73
  19.0 9.8 %copy-start.9 = (bf16[512,512]{1,0:T(8,128)(2,1)S(1)}, bf16[512,512]{1,0:T(8,128)(2,1)}, u32[]{:S(2)}) copy-start(bf16[512,512]{1,0:T(8,128)(2,1)} %get-tuple-element.41) | copy-start | bytes 1572868
  19.1 5.0 %collective-permute-start.4 = (bf16[3,64,512]{2,1,0:T(8,128)(2,1)S(1)}, bf16[3,64,512]{2,1,0:T(8,128)(2,1)S(1)}, u32[]{:S(2)}, u32[]{:S(2)}) collective-permute-start(bf16[3,64,512]{2,1,0:T(8,128)(2,1)S(1)} %get-tuple-element.38), channel_id=1, source_target_pairs={{0,8},{1,5},{2,10},{3,7},{4,12},{5,1},{6,14},{7,3},{8,0},{9,13},{1... | collective-permute-start | bytes 589832 | tf_op jit(solution)/shard_map/ppermute | solution.py:73
  24.1 4.6 %collective-permute-start.5 = (bf16[3,64,512]{2,1,0:T(8,128)(2,1)S(1)}, bf16[3,64,512]{2,1,0:T(8,128)(2,1)S(1)}, u32[]{:S(2)}, u32[]{:S(2)}) collective-permute-start(bf16[3,64,512]{2,1,0:T(8,128)(2,1)S(1)} %get-tuple-element.40), channel_id=1, source_target_pairs={{0,2},{1,3},{2,0},{3,1},{4,6},{5,7},{6,4},{7,5},{8,10},{9,11},{10,... | collective-permute-start | bytes 589832 | tf_op jit(solution)/shard_map/ppermute | solution.py:73
  28.7 5.6 %collective-permute-start.6 = (bf16[3,64,512]{2,1,0:T(8,128)(2,1)S(1)}, bf16[3,64,512]{2,1,0:T(8,128)(2,1)S(1)}, u32[]{:S(2)}, u32[]{:S(2)}) collective-permute-start(bf16[3,64,512]{2,1,0:T(8,128)(2,1)S(1)} %add_convert_fusion.1), channel_id=1, source_target_pairs={{0,16},{1,17},{2,18},{3,19},{4,20},{5,21},{6,22},{7,23},{8,24},{9,... | collective-permute-start | bytes 589832 | tf_op jit(solution)/shard_map/ppermute | solution.py:73
  28.8 12.2 %collective-permute-start.9 = (bf16[512,512]{1,0:T(8,128)(2,1)S(1)}, bf16[512,512]{1,0:T(8,128)(2,1)S(1)}, u32[]{:S(2)}, u32[]{:S(2)}) collective-permute-start(bf16[512,512]{1,0:T(8,128)(2,1)S(1)} %copy-done.9), channel_id=1, source_target_pairs={{2,6},{6,10},{10,14},{14,18},{18,22},{22,26},{26,30},{3,7},{7,11},... | collective-permute-start | bytes 1572872 | tf_op jit(solution)/shard_map/ppermute | solution.py:77
  29.5 25.3 %collective-permute-start.12 = (bf16[512,512]{1,0:T(8,128)(2,1)S(1)}, bf16[512,512]{1,0:T(8,128)(2,1)S(1)}, u32[]{:S(2)}, u32[]{:S(2)}) collective-permute-start(bf16[512,512]{1,0:T(8,128)(2,1)S(1)} %collective-permute-done.3.odd_k), channel_id=1, source_target_pairs={{0,4},{4,8},{8,12},{12,16},{16,20},{20,24},{24,28},{1,5},{5,9},{9,... | collective-permute-start | bytes 1572872 | tf_op jit(solution)/shard_map/ppermute | solution.py:93
  34.4 4.9 %collective-permute-start.7 = (bf16[3,64,512]{2,1,0:T(8,128)(2,1)S(1)}, bf16[3,64,512]{2,1,0:T(8,128)(2,1)S(1)}, u32[]{:S(2)}, u32[]{:S(2)}) collective-permute-start(bf16[3,64,512]{2,1,0:T(8,128)(2,1)S(1)} %add_convert_fusion), channel_id=1, source_target_pairs={{0,2},{1,3},{2,0},{3,1},{4,6},{5,7},{6,4},{7,5},{8,10},{9,11},{10,... | collective-permute-start | bytes 589832 | tf_op jit(solution)/shard_map/ppermute | solution.py:73
  39.3 28.0 %copy-start.7 = (bf16[768,512]{1,0:T(8,128)(2,1)S(1)}, bf16[768,512]{1,0:T(8,128)(2,1)}, u32[]{:S(2)}) copy-start(bf16[768,512]{1,0:T(8,128)(2,1)} %v_ref.1) | copy-start | bytes 2359300
  39.3 14.2 %collective-permute-start.8 = (bf16[3,64,512]{2,1,0:T(8,128)(2,1)S(1)}, bf16[3,64,512]{2,1,0:T(8,128)(2,1)}, u32[]{:S(2)}, u32[]{:S(2)}) collective-permute-start(bf16[3,64,512]{2,1,0:T(8,128)(2,1)S(1)} %pad_maximum_fusion.2), channel_id=1, source_target_pairs={{0,8},{1,5},{2,10},{3,7},{4,12},{5,1},{6,14},{7,3},{8,0},{9,13},{1... | collective-permute-start | bytes 589832 | tf_op jit(solution)/shard_map/ppermute | solution.py:73
  40.6 26.7 %copy-start = (bf16[768,512]{1,0:T(8,128)(2,1)S(1)}, bf16[768,512]{1,0:T(8,128)(2,1)}, u32[]{:S(2)}) copy-start(bf16[768,512]{1,0:T(8,128)(2,1)} %refs_4_.3) | copy-start | bytes 2359300
  40.7 26.7 %copy-start.1 = (bf16[512,512]{1,0:T(8,128)(2,1)S(1)}, bf16[512,512]{1,0:T(8,128)(2,1)}, u32[]{:S(2)}) copy-start(bf16[512,512]{1,0:T(8,128)(2,1)} %refs_5_.1) | copy-start | bytes 1572868
  40.7 26.7 %copy-start.2 = (bf16[512,512]{1,0:T(8,128)(2,1)S(1)}, bf16[512,512]{1,0:T(8,128)(2,1)}, u32[]{:S(2)}) copy-start(bf16[512,512]{1,0:T(8,128)(2,1)} %refs_6_.1) | copy-start | bytes 1572868
  40.7 26.6 %copy-start.3 = (bf16[512,512]{1,0:T(8,128)(2,1)S(1)}, bf16[512,512]{1,0:T(8,128)(2,1)}, u32[]{:S(2)}) copy-start(bf16[512,512]{1,0:T(8,128)(2,1)} %refs_7_.1) | copy-start | bytes 1572868
  40.7 26.6 %copy-start.6 = (bf16[768,512]{1,0:T(8,128)(2,1)S(1)}, bf16[768,512]{1,0:T(8,128)(2,1)}, u32[]{:S(2)}) copy-start(bf16[768,512]{1,0:T(8,128)(2,1)} %k_ref.1) | copy-start | bytes 2359300
  40.7 14.6 %collective-permute-start.11 = (bf16[3,64,512]{2,1,0:T(8,128)(2,1)S(1)}, bf16[3,64,512]{2,1,0:T(8,128)(2,1)S(1)}, u32[]{:S(2)}, u32[]{:S(2)}) collective-permute-start(bf16[3,64,512]{2,1,0:T(8,128)(2,1)S(1)} %pad_maximum_fusion.3), channel_id=1, source_target_pairs={{0,8},{1,5},{2,10},{3,7},{4,12},{5,1},{6,14},{7,3},{8,0},{9,13},{1... | collective-permute-start | bytes 589832 | tf_op jit(solution)/shard_map/ppermute | solution.py:73
  53.6 13.7 %collective-permute-start.14 = (bf16[512,512]{1,0:T(8,128)(2,1)S(1)}, bf16[512,512]{1,0:T(8,128)(2,1)S(1)}, u32[]{:S(2)}, u32[]{:S(2)}) collective-permute-start(bf16[512,512]{1,0:T(8,128)(2,1)S(1)} %broadcast_select_fusion), channel_id=1, source_target_pairs={{0,2},{4,6},{8,10},{12,14},{16,18},{20,22},{24,26},{28,30},{2,0},{... | collective-permute-start | bytes 1572872 | tf_op jit(solution)/shard_map/ppermute | solution.py:84
  55.4 17.3 %collective-permute-start.13 = (bf16[3,128,512]{2,1,0:T(8,128)(2,1)S(1)}, bf16[3,128,512]{2,1,0:T(8,128)(2,1)S(1)}, u32[]{:S(2)}, u32[]{:S(2)}) collective-permute-start(bf16[3,128,512]{2,1,0:T(8,128)(2,1)S(1)} %pad_maximum_fusion.1.refs_2_), channel_id=1, source_target_pairs={{0,4},{1,9},{2,6},{3,11},{4,0},{5,13},{6,2},{7,15},{8,12},{9,1},{1... | collective-permute-start | bytes 1179656 | tf_op jit(solution)/shard_map/ppermute | solution.py:73
  56.5 16.2 %collective-permute-start.10 = (bf16[3,128,512]{2,1,0:T(8,128)(2,1)S(1)}, bf16[3,128,512]{2,1,0:T(8,128)(2,1)S(1)}, u32[]{:S(2)}, u32[]{:S(2)}) collective-permute-start(bf16[3,128,512]{2,1,0:T(8,128)(2,1)S(1)} %pad_maximum_fusion.refs_0_), channel_id=1, source_target_pairs={{0,4},{1,9},{2,6},{3,11},{4,0},{5,13},{6,2},{7,15},{8,12},{9,1},{1... | collective-permute-start | bytes 1179656 | tf_op jit(solution)/shard_map/ppermute | solution.py:73
  72.7 5.1 %copy-start.8 = (f32[512]{0:T(512)S(1)}, f32[512]{0:T(512)}, u32[]{:S(2)}) copy-start(f32[512]{0:T(512)} %param.15) | copy-start | bytes 6148
  76.2 1.5 %collective-permute-start.15 = (f32[8,768]{1,0:T(8,128)S(1)}, f32[8,768]{1,0:T(8,128)S(1)}, u32[]{:S(2)}, u32[]{:S(2)}) collective-permute-start(f32[8,768]{1,0:T(8,128)S(1)} %get-tuple-element.50.sums_ref), channel_id=1, source_target_pairs={{0,1},{1,0},{2,3},{3,2},{4,5},{5,4},{6,7},{7,6},{8,9},{9,8},{10,11... | collective-permute-start | bytes 73736 | tf_op jit(solution)/shard_map/ppermute | solution.py:410

commit v6 on v5

--- a/solution.py
+++ b/solution.py
@@ -51,7 +51,7 @@
 
 def exchange_masks(peers):
     bits = [1 << at for at in range(peers.bit_length() - 1)]
-    halving = [(bits[1], bits[2]), (bits[2], bits[1]), (bits[0], bits[0])]
+    halving = [(bits[2], bits[1]), (bits[1], bits[2]), (bits[0], bits[0])]
     return halving, [(b, b) for b in bits[3:]]
 
 

time: 79.2 us -> 78.2 us (0.987)
  waiting for transfers between devices: 41.6 us -> 27.5 us
  starting transfers between devices: 17 us -> 29.4 us
    ppermute x11, waiting for transfers between devices: 30.2 us -> 22.6 us  [swap(): return lax.ppermute(x, ('seq', 'head'), pairs)]
    ppermute x1, waiting for transfers between devices: 9.38 us -> 2.95 us  [shift_passed(): return lax.ppermute(jnp.where(odd, passed, x), 'seq', pairs)]
    ppermute x1, starting transfers between devices: 0.68 us -> 5.92 us  [body(): more = [lax.ppermute(sums, 'head', [(0, 1), (1, 0)])]]
    ppermute x1, starting transfers between devices: 1.28 us -> 5.23 us  [shift_passed(): return lax.ppermute(jnp.where(odd, passed, x), 'seq', pairs)]
    ppermute x11, starting transfers between devices: 9.96 us -> 13.2 us  [swap(): return lax.ppermute(x, ('seq', 'head'), pairs)]
where the time goes in v6:
time: 78.2 us; the launch traced here: 77.2 us
  starting transfers between devices  29.4 us (38%)
  waiting for transfers between devices  27.5 us (35%)
  Pallas kernels  17.2 us (22%)
  local copies, waits for them, and re-layouts  1.21 us (2%)
  other arithmetic  1.15 us (1%)
  between operations  0.84 us (1%)
    ppermute x11, waiting for transfers between devices, swap(): return lax.ppermute(x, ('seq', 'head'), pairs)  22.6 us
    ppermute x11, starting transfers between devices, swap(): return lax.ppermute(x, ('seq', 'head'), pairs)  13.2 us
    pallas_call x1, Pallas kernels, body(): pl.pallas_call(functools.partial(grads_kernel, steps[0]), out_shape=[jax....  6.94 us
    ppermute x1, starting transfers between devices, body(): more = [lax.ppermute(sums, 'head', [(0, 1), (1, 0)])]  5.92 us
    pallas_call x1, Pallas kernels, body(): pl.pallas_call(attend_kernel, out_shape=(jax.ShapeDtypeStruct((tok_rows,...  5.3 us
    ppermute x1, starting transfers between devices, shift_passed(): return lax.ppermute(jnp.where(odd, passed, x), 'seq', pairs)  5.23 us
    pallas_call x1, Pallas kernels, body(): pl.pallas_call(functools.partial(apply_kernel, steps, part_rows), out_sha...  3.5 us
    ppermute x1, starting transfers between devices, pass_on(): lax.ppermute(x, 'seq', [(i, i + 2) for i in range(0, lax.axis_size('seq')...  3.17 us
  transfers between devices with their start and end apart: 16, of which 12 were waited for; matrix products, arithmetic and copies ran while one was open for 1% of the time, Pallas kernels for 7%

profile of v6, /device:TPU:17, one launch (start us, length us, event | category | flops | bytes accessed | tf_op | source)
XLA Modules:
  0.0 77.2 jit_solution(14238968351548516937)
XLA Ops:
  0.6 6.9 %gradients.1 = (bf16[512,512]{1,0:T(8,128)(2,1)}, bf16[512,512]{1,0:T(8,128)(2,1)}, bf16[3,128,512]{2,1,0:T(8,128)(2,1)}, bf16[3,128,512]{2,1,0:T(8,128)(2,1)}, ...) custom-call(bf16[768,512]{1,0:T(8,128)(2,1)} %k_ref.1, bf16[768,512]{1,0:T(8,128)(2,1)} %v_ref.1, ...), custom_call_target="tpu_custom_call" | custom-call | flops 2415919104 | bytes 6291456 | tf_op jit(solution)/shard_map/gradients/pallas_call | solution.py:303
  7.6 1.3 %collective-permute-start = (bf16[3,128,512]{2,1,0:T(8,128)(2,1)}, bf16[3,128,512]{2,1,0:T(8,128)(2,1)S(1)}, u32[]{:S(2)}, u32[]{:S(2)}) collective-permute-start(bf16[3,128,512]{2,1,0:T(8,128)(2,1)} %get-tuple-element.30), channel_id=1, source_target_pairs={{0,8},{1,5},{2,10},{3,7},{4,12},{5,1},{6,14},{7,3},{8,0},{9,13},{1... | collective-permute-start | bytes 1179656 | tf_op jit(solution)/shard_map/ppermute | solution.py:73
  8.9 0.2 collective-permute-start.1
  9.1 1.2 %collective-permute-start.3 = (bf16[512,512]{1,0:T(8,128)(2,1)}, bf16[512,512]{1,0:T(8,128)(2,1)S(1)}, u32[]{:S(2)}, u32[]{:S(2)}) collective-permute-start(bf16[512,512]{1,0:T(8,128)(2,1)} %get-tuple-element.36), channel_id=1, source_target_pairs={{0,2},{2,0},{4,6},{6,4},{8,10},{10,8},{12,14},{14,12},{16,18},{18,... | collective-permute-start | bytes 1572872 | tf_op jit(solution)/shard_map/ppermute | solution.py:89
  10.3 4.5 %collective-permute-done.refs_1_ = bf16[3,128,512]{2,1,0:T(8,128)(2,1)S(1)} collective-permute-done((bf16[3,128,512]{2,1,0:T(8,128)(2,1)}, bf16[3,128,512]{2,1,0:T(8,128)(2,1)S(1)}, u32[]{:S(2)}, u32[]{:S(2)}) %collective-permute-start) | collective-permute-done | bytes 393248 | tf_op jit(solution)/shard_map/ppermute | solution.py:73
  14.8 1.1 %copy-done.5 = f32[3,128,512]{2,1,0:T(8,128)S(1)} copy-done((f32[3,128,512]{2,1,0:T(8,128)S(1)}, f32[3,128,512]{2,1,0:T(8,128)}, u32[]{:S(2)}) %copy-start.5) | copy-done | bytes 786456
  16.0 1.4 %collective-permute-start.2 = (bf16[3,64,512]{2,1,0:T(8,128)(2,1)S(1)}, bf16[3,64,512]{2,1,0:T(8,128)(2,1)S(1)}, u32[]{:S(2)}, u32[]{:S(2)}) collective-permute-start(bf16[3,64,512]{2,1,0:T(8,128)(2,1)S(1)} %get-tuple-element.35), channel_id=1, source_target_pairs={{0,4},{1,9},{2,6},{3,11},{4,0},{5,13},{6,2},{7,15},{8,12},{9,1},{1... | collective-permute-start | bytes 589832 | tf_op jit(solution)/shard_map/ppermute | solution.py:73
  17.3 1.7 %collective-permute-done.1.refs_1_ = bf16[3,128,512]{2,1,0:T(8,128)(2,1)S(1)} collective-permute-done((bf16[3,128,512]{2,1,0:T(8,128)(2,1)}, bf16[3,128,512]{2,1,0:T(8,128)(2,1)S(1)}, u32[]{:S(2)}, u32[]{:S(2)}) %collective-permute-start.1) | collective-permute-done | bytes 393248 | tf_op jit(solution)/shard_map/ppermute | solution.py:73
  19.1 1.4 %collective-permute-start.4 = (bf16[3,64,512]{2,1,0:T(8,128)(2,1)S(1)}, bf16[3,64,512]{2,1,0:T(8,128)(2,1)S(1)}, u32[]{:S(2)}, u32[]{:S(2)}) collective-permute-start(bf16[3,64,512]{2,1,0:T(8,128)(2,1)S(1)} %get-tuple-element.38), channel_id=1, source_target_pairs={{0,4},{1,9},{2,6},{3,11},{4,0},{5,13},{6,2},{7,15},{8,12},{9,1},{1... | collective-permute-start | bytes 589832 | tf_op jit(solution)/shard_map/ppermute | solution.py:73
  20.4 1.1 %collective-permute-done.3.odd_k = bf16[512,512]{1,0:T(8,128)(2,1)S(1)} collective-permute-done((bf16[512,512]{1,0:T(8,128)(2,1)}, bf16[512,512]{1,0:T(8,128)(2,1)S(1)}, u32[]{:S(2)}, u32[]{:S(2)}) %collective-permute-start.3) | collective-permute-done | bytes 524320 | tf_op jit(solution)/shard_map/ppermute | solution.py:89
  21.5 0.7 collective-permute-done.2.refs_2_
  22.2 1.8 %collective-permute-done.4.refs_3_ = bf16[3,64,512]{2,1,0:T(8,128)(2,1)S(1)} collective-permute-done((bf16[3,64,512]{2,1,0:T(8,128)(2,1)S(1)}, bf16[3,64,512]{2,1,0:T(8,128)(2,1)S(1)}, u32[]{:S(2)}, u32[]{:S(2)}) %collective-permute-start.4) | collective-permute-done | bytes 196640 | tf_op jit(solution)/shard_map/ppermute | solution.py:73
  24.1 1.3 %collective-permute-start.5 = (bf16[3,64,512]{2,1,0:T(8,128)(2,1)S(1)}, bf16[3,64,512]{2,1,0:T(8,128)(2,1)S(1)}, u32[]{:S(2)}, u32[]{:S(2)}) collective-permute-start(bf16[3,64,512]{2,1,0:T(8,128)(2,1)S(1)} %get-tuple-element.40), channel_id=1, source_target_pairs={{0,2},{1,3},{2,0},{3,1},{4,6},{5,7},{6,4},{7,5},{8,10},{9,11},{10,... | collective-permute-start | bytes 589832 | tf_op jit(solution)/shard_map/ppermute | solution.py:73
  25.4 3.3 %collective-permute-done.5 = bf16[3,64,512]{2,1,0:T(8,128)(2,1)S(1)} collective-permute-done((bf16[3,64,512]{2,1,0:T(8,128)(2,1)S(1)}, bf16[3,64,512]{2,1,0:T(8,128)(2,1)S(1)}, u32[]{:S(2)}, u32[]{:S(2)}) %collective-permute-start.5) | collective-permute-done | bytes 196640 | tf_op jit(solution)/shard_map/ppermute | solution.py:73
  28.8 0.7 collective-permute-start.9
  29.5 3.2 %collective-permute-start.12 = (bf16[512,512]{1,0:T(8,128)(2,1)S(1)}, bf16[512,512]{1,0:T(8,128)(2,1)S(1)}, u32[]{:S(2)}, u32[]{:S(2)}) collective-permute-start(bf16[512,512]{1,0:T(8,128)(2,1)S(1)} %collective-permute-done.3.odd_k), channel_id=1, source_target_pairs={{0,4},{4,8},{8,12},{12,16},{16,20},{20,24},{24,28},{1,5},{5,9},{9,... | collective-permute-start | bytes 1572872 | tf_op jit(solution)/shard_map/ppermute | solution.py:93
  32.7 1.6 %collective-permute-done.6 = bf16[3,64,512]{2,1,0:T(8,128)(2,1)S(1)} collective-permute-done((bf16[3,64,512]{2,1,0:T(8,128)(2,1)S(1)}, bf16[3,64,512]{2,1,0:T(8,128)(2,1)S(1)}, u32[]{:S(2)}, u32[]{:S(2)}) %collective-permute-start.6) | collective-permute-done | bytes 196640 | tf_op jit(solution)/shard_map/ppermute | solution.py:73
  34.4 1.3 %collective-permute-start.7 = (bf16[3,64,512]{2,1,0:T(8,128)(2,1)S(1)}, bf16[3,64,512]{2,1,0:T(8,128)(2,1)S(1)}, u32[]{:S(2)}, u32[]{:S(2)}) collective-permute-start(bf16[3,64,512]{2,1,0:T(8,128)(2,1)S(1)} %add_convert_fusion), channel_id=1, source_target_pairs={{0,2},{1,3},{2,0},{3,1},{4,6},{5,7},{6,4},{7,5},{8,10},{9,11},{10,... | collective-permute-start | bytes 589832 | tf_op jit(solution)/shard_map/ppermute | solution.py:73
  35.7 3.6 %collective-permute-done.7 = bf16[3,64,512]{2,1,0:T(8,128)(2,1)S(1)} collective-permute-done((bf16[3,64,512]{2,1,0:T(8,128)(2,1)S(1)}, bf16[3,64,512]{2,1,0:T(8,128)(2,1)S(1)}, u32[]{:S(2)}, u32[]{:S(2)}) %collective-permute-start.7) | collective-permute-done | bytes 196640 | tf_op jit(solution)/shard_map/ppermute | solution.py:73
  39.3 3.3 %collective-permute-start.8 = (bf16[3,64,512]{2,1,0:T(8,128)(2,1)S(1)}, bf16[3,64,512]{2,1,0:T(8,128)(2,1)}, u32[]{:S(2)}, u32[]{:S(2)}) collective-permute-start(bf16[3,64,512]{2,1,0:T(8,128)(2,1)S(1)} %pad_maximum_fusion.2), channel_id=1, source_target_pairs={{0,4},{1,9},{2,6},{3,11},{4,0},{5,13},{6,2},{7,15},{8,12},{9,1},{1... | collective-permute-start | bytes 589832 | tf_op jit(solution)/shard_map/ppermute | solution.py:73
  42.7 0.1 collective-permute-start.11
  42.8 3.2 %collective-permute-done.8 = bf16[3,64,512]{2,1,0:T(8,128)(2,1)} collective-permute-done((bf16[3,64,512]{2,1,0:T(8,128)(2,1)S(1)}, bf16[3,64,512]{2,1,0:T(8,128)(2,1)}, u32[]{:S(2)}, u32[]{:S(2)}) %collective-permute-start.8) | collective-permute-done | bytes 196640 | tf_op jit(solution)/shard_map/ppermute | solution.py:73
  46.0 5.2 %collective-permute-start.14 = (bf16[512,512]{1,0:T(8,128)(2,1)S(1)}, bf16[512,512]{1,0:T(8,128)(2,1)S(1)}, u32[]{:S(2)}, u32[]{:S(2)}) collective-permute-start(bf16[512,512]{1,0:T(8,128)(2,1)S(1)} %broadcast_select_fusion), channel_id=1, source_target_pairs={{0,2},{4,6},{8,10},{12,14},{16,18},{20,22},{24,26},{28,30},{2,0},{... | collective-permute-start | bytes 1572872 | tf_op jit(solution)/shard_map/ppermute | solution.py:84
  51.3 2.8 %collective-permute-start.13 = (bf16[3,128,512]{2,1,0:T(8,128)(2,1)S(1)}, bf16[3,128,512]{2,1,0:T(8,128)(2,1)S(1)}, u32[]{:S(2)}, u32[]{:S(2)}) collective-permute-start(bf16[3,128,512]{2,1,0:T(8,128)(2,1)S(1)} %pad_maximum_fusion.1.refs_2_), channel_id=1, source_target_pairs={{0,8},{1,5},{2,10},{3,7},{4,12},{5,1},{6,14},{7,3},{8,0},{9,13},{1... | collective-permute-start | bytes 1179656 | tf_op jit(solution)/shard_map/ppermute | solution.py:73
  54.1 1.0 %pad_maximum_fusion.refs_0_ = bf16[3,128,512]{2,1,0:T(8,128)(2,1)S(1)} fusion(bf16[3,64,512]{2,1,0:T(8,128)(2,1)} %collective-permute-done.8, bf16[3,32,512]{2,1,0:T(8,128)(2,1)S(1)} %get-tuple-element.57, bf16[3,32,512]{2,1,0:T(8,128)(2,1)S(1)} %get-tuple-element.55), kind=kLoop, calls=%fused_computation.1 | loop fusion | flops 1179648 | bytes 786432 | tf_op jit(solution)/shard_map/concatenate | solution.py:361
  55.1 2.9 %collective-permute-done.14.prev_v = bf16[512,512]{1,0:T(8,128)(2,1)S(1)} collective-permute-done((bf16[512,512]{1,0:T(8,128)(2,1)S(1)}, bf16[512,512]{1,0:T(8,128)(2,1)S(1)}, u32[]{:S(2)}, u32[]{:S(2)}) %collective-permute-start.14) | collective-permute-done | bytes 524320 | tf_op jit(solution)/shard_map/ppermute | solution.py:84
  58.1 5.3 %window_attention.1 = (f32[768,512]{1,0:T(8,128)S(1)}, f32[3,8,512]{2,1,0:T(8,128)S(1)}) custom-call(bf16[768,512]{1,0:T(8,128)(2,1)S(1)} %copy-done, bf16[768,512]{1,0:T(8,128)(2,1)S(1)} %copy-done.6, bf16[768,512]{1,0:T(8,128)(2,1)S(1)} %copy-done.7, bf16[512,512]{1,0:T(8,128)(2,1)S(1)} %collective-permute-done.3.odd_k, ...), custom_call_target="tpu_custom_call" | custom-call | flops 1207959552 | bytes 3145728 | tf_op jit(solution)/shard_map/window_attention/pallas_call | solution.py:364
  63.4 2.3 %collective-permute-done.10.refs_1_ = bf16[3,128,512]{2,1,0:T(8,128)(2,1)S(1)} collective-permute-done((bf16[3,128,512]{2,1,0:T(8,128)(2,1)S(1)}, bf16[3,128,512]{2,1,0:T(8,128)(2,1)S(1)}, u32[]{:S(2)}, u32[]{:S(2)}) %collective-permute-start.10) | collective-permute-done | bytes 393248 | tf_op jit(solution)/shard_map/ppermute | solution.py:73
  65.7 3.5 %apply.1 = (f32[768,512]{1,0:T(8,128)S(1)}, f32[8,768]{1,0:T(8,128)S(1)}, bf16[32,512]{1,0:T(8,128)(2,1)}, bf16[32,512]{1,0:T(8,128)(2,1)}, bf16[32,512]{1,0:T(8,128)(2,1)}) custom-call(bf16[3,128,512]{2,1,0:T(8,128)(2,1)S(1)} %pad_maximum_fusion.refs_0_, bf16[3,128,512]{2,1,0:T(8,128)(2,1)S(1)} %collective-permute-done.10.refs_1_, ...), custom_call_target="tpu_custom_call" | custom-call | flops 1207959552 | bytes 4718592 | tf_op jit(solution)/shard_map/apply/pallas_call | solution.py:386
  69.2 5.9 %collective-permute-start.15 = (f32[8,768]{1,0:T(8,128)S(1)}, f32[8,768]{1,0:T(8,128)S(1)}, u32[]{:S(2)}, u32[]{:S(2)}) collective-permute-start(f32[8,768]{1,0:T(8,128)S(1)} %get-tuple-element.50.sums_ref), channel_id=1, source_target_pairs={{0,1},{1,0},{2,3},{3,2},{4,5},{5,4},{6,7},{7,6},{8,9},{9,8},{10,11... | collective-permute-start | bytes 73736 | tf_op jit(solution)/shard_map/ppermute | solution.py:410
  75.1 0.8 %collective-permute-done.15.more_ref = f32[8,768]{1,0:T(8,128)S(1)} collective-permute-done((f32[8,768]{1,0:T(8,128)S(1)}, f32[8,768]{1,0:T(8,128)S(1)}, u32[]{:S(2)}, u32[]{:S(2)}) %collective-permute-start.15) | collective-permute-done | bytes 24608 | tf_op jit(solution)/shard_map/ppermute | solution.py:410
  76.0 1.2 %norm.1 = bf16[768,512]{1,0:T(8,128)(2,1)} custom-call(f32[768,512]{1,0:T(8,128)S(1)} %get-tuple-element.49.combined_ref, f32[8,768]{1,0:T(8,128)S(1)} %get-tuple-element.50.sums_ref, f32[8,768]{1,0:T(8,128)S(1)} %collective-permute-done.15.more_ref, f32[1,512]{1,0:T(1,128)S(1)} %bitcast.2), custom_call_target="tpu_custom_call" | custom-call | flops 1572864 | bytes 2359296 | tf_op jit(solution)/shard_map/norm/pallas_call | solution.py:418
  (36 shorter events, 0.6 us)
Async XLA Ops:
  7.6 11.4 %copy-start.4 = (f32[3,128,512]{2,1,0:T(8,128)S(1)}, f32[3,128,512]{2,1,0:T(8,128)}, u32[]{:S(2)}) copy-start(f32[3,128,512]{2,1,0:T(8,128)} %get-tuple-element.32.refs_0_) | copy-start | bytes 2359300
  7.6 7.2 %collective-permute-start = (bf16[3,128,512]{2,1,0:T(8,128)(2,1)}, bf16[3,128,512]{2,1,0:T(8,128)(2,1)S(1)}, u32[]{:S(2)}, u32[]{:S(2)}) collective-permute-start(bf16[3,128,512]{2,1,0:T(8,128)(2,1)} %get-tuple-element.30), channel_id=1, source_target_pairs={{0,8},{1,5},{2,10},{3,7},{4,12},{5,1},{6,14},{7,3},{8,0},{9,13},{1... | collective-permute-start | bytes 1179656 | tf_op jit(solution)/shard_map/ppermute | solution.py:73
  8.9 10.1 %collective-permute-start.1 = (bf16[3,128,512]{2,1,0:T(8,128)(2,1)}, bf16[3,128,512]{2,1,0:T(8,128)(2,1)S(1)}, u32[]{:S(2)}, u32[]{:S(2)}) collective-permute-start(bf16[3,128,512]{2,1,0:T(8,128)(2,1)} %get-tuple-element.33), channel_id=1, source_target_pairs={{0,8},{1,5},{2,10},{3,7},{4,12},{5,1},{6,14},{7,3},{8,0},{9,13},{1... | collective-permute-start | bytes 1179656 | tf_op jit(solution)/shard_map/ppermute | solution.py:73
  9.1 12.4 %collective-permute-start.3 = (bf16[512,512]{1,0:T(8,128)(2,1)}, bf16[512,512]{1,0:T(8,128)(2,1)S(1)}, u32[]{:S(2)}, u32[]{:S(2)}) collective-permute-start(bf16[512,512]{1,0:T(8,128)(2,1)} %get-tuple-element.36), channel_id=1, source_target_pairs={{0,2},{2,0},{4,6},{6,4},{8,10},{10,8},{12,14},{14,12},{16,18},{18,... | collective-permute-start | bytes 1572872 | tf_op jit(solution)/shard_map/ppermute | solution.py:89
  14.8 1.1 %copy-start.5 = (f32[3,128,512]{2,1,0:T(8,128)S(1)}, f32[3,128,512]{2,1,0:T(8,128)}, u32[]{:S(2)}) copy-start(f32[3,128,512]{2,1,0:T(8,128)} %get-tuple-element.29.refs_0_) | copy-start | bytes 2359300
  16.0 6.3 %collective-permute-start.2 = (bf16[3,64,512]{2,1,0:T(8,128)(2,1)S(1)}, bf16[3,64,512]{2,1,0:T(8,128)(2,1)S(1)}, u32[]{:S(2)}, u32[]{:S(2)}) collective-permute-start(bf16[3,64,512]{2,1,0:T(8,128)(2,1)S(1)} %get-tuple-element.35), channel_id=1, source_target_pairs={{0,4},{1,9},{2,6},{3,11},{4,0},{5,13},{6,2},{7,15},{8,12},{9,1},{1... | collective-permute-start | bytes 589832 | tf_op jit(solution)/shard_map/ppermute | solution.py:73
  19.0 9.8 %copy-start.9 = (bf16[512,512]{1,0:T(8,128)(2,1)S(1)}, bf16[512,512]{1,0:T(8,128)(2,1)}, u32[]{:S(2)}) copy-start(bf16[512,512]{1,0:T(8,128)(2,1)} %get-tuple-element.41) | copy-start | bytes 1572868
  19.1 5.0 %collective-permute-start.4 = (bf16[3,64,512]{2,1,0:T(8,128)(2,1)S(1)}, bf16[3,64,512]{2,1,0:T(8,128)(2,1)S(1)}, u32[]{:S(2)}, u32[]{:S(2)}) collective-permute-start(bf16[3,64,512]{2,1,0:T(8,128)(2,1)S(1)} %get-tuple-element.38), channel_id=1, source_target_pairs={{0,4},{1,9},{2,6},{3,11},{4,0},{5,13},{6,2},{7,15},{8,12},{9,1},{1... | collective-permute-start | bytes 589832 | tf_op jit(solution)/shard_map/ppermute | solution.py:73
  24.1 4.6 %collective-permute-start.5 = (bf16[3,64,512]{2,1,0:T(8,128)(2,1)S(1)}, bf16[3,64,512]{2,1,0:T(8,128)(2,1)S(1)}, u32[]{:S(2)}, u32[]{:S(2)}) collective-permute-start(bf16[3,64,512]{2,1,0:T(8,128)(2,1)S(1)} %get-tuple-element.40), channel_id=1, source_target_pairs={{0,2},{1,3},{2,0},{3,1},{4,6},{5,7},{6,4},{7,5},{8,10},{9,11},{10,... | collective-permute-start | bytes 589832 | tf_op jit(solution)/shard_map/ppermute | solution.py:73
  28.7 5.6 %collective-permute-start.6 = (bf16[3,64,512]{2,1,0:T(8,128)(2,1)S(1)}, bf16[3,64,512]{2,1,0:T(8,128)(2,1)S(1)}, u32[]{:S(2)}, u32[]{:S(2)}) collective-permute-start(bf16[3,64,512]{2,1,0:T(8,128)(2,1)S(1)} %add_convert_fusion.1), channel_id=1, source_target_pairs={{0,16},{1,17},{2,18},{3,19},{4,20},{5,21},{6,22},{7,23},{8,24},{9,... | collective-permute-start | bytes 589832 | tf_op jit(solution)/shard_map/ppermute | solution.py:73
  28.8 13.9 %collective-permute-start.9 = (bf16[512,512]{1,0:T(8,128)(2,1)S(1)}, bf16[512,512]{1,0:T(8,128)(2,1)S(1)}, u32[]{:S(2)}, u32[]{:S(2)}) collective-permute-start(bf16[512,512]{1,0:T(8,128)(2,1)S(1)} %copy-done.9), channel_id=1, source_target_pairs={{2,6},{6,10},{10,14},{14,18},{18,22},{22,26},{26,30},{3,7},{7,11},... | collective-permute-start | bytes 1572872 | tf_op jit(solution)/shard_map/ppermute | solution.py:77
  29.5 21.7 %collective-permute-start.12 = (bf16[512,512]{1,0:T(8,128)(2,1)S(1)}, bf16[512,512]{1,0:T(8,128)(2,1)S(1)}, u32[]{:S(2)}, u32[]{:S(2)}) collective-permute-start(bf16[512,512]{1,0:T(8,128)(2,1)S(1)} %collective-permute-done.3.odd_k), channel_id=1, source_target_pairs={{0,4},{4,8},{8,12},{12,16},{16,20},{20,24},{24,28},{1,5},{5,9},{9,... | collective-permute-start | bytes 1572872 | tf_op jit(solution)/shard_map/ppermute | solution.py:93
  34.4 4.9 %collective-permute-start.7 = (bf16[3,64,512]{2,1,0:T(8,128)(2,1)S(1)}, bf16[3,64,512]{2,1,0:T(8,128)(2,1)S(1)}, u32[]{:S(2)}, u32[]{:S(2)}) collective-permute-start(bf16[3,64,512]{2,1,0:T(8,128)(2,1)S(1)} %add_convert_fusion), channel_id=1, source_target_pairs={{0,2},{1,3},{2,0},{3,1},{4,6},{5,7},{6,4},{7,5},{8,10},{9,11},{10,... | collective-permute-start | bytes 589832 | tf_op jit(solution)/shard_map/ppermute | solution.py:73
  39.3 18.8 %copy-start.7 = (bf16[768,512]{1,0:T(8,128)(2,1)S(1)}, bf16[768,512]{1,0:T(8,128)(2,1)}, u32[]{:S(2)}) copy-start(bf16[768,512]{1,0:T(8,128)(2,1)} %v_ref.1) | copy-start | bytes 2359300
  39.3 6.6 %collective-permute-start.8 = (bf16[3,64,512]{2,1,0:T(8,128)(2,1)S(1)}, bf16[3,64,512]{2,1,0:T(8,128)(2,1)}, u32[]{:S(2)}, u32[]{:S(2)}) collective-permute-start(bf16[3,64,512]{2,1,0:T(8,128)(2,1)S(1)} %pad_maximum_fusion.2), channel_id=1, source_target_pairs={{0,4},{1,9},{2,6},{3,11},{4,0},{5,13},{6,2},{7,15},{8,12},{9,1},{1... | collective-permute-start | bytes 589832 | tf_op jit(solution)/shard_map/ppermute | solution.py:73
  42.6 15.5 %copy-start = (bf16[768,512]{1,0:T(8,128)(2,1)S(1)}, bf16[768,512]{1,0:T(8,128)(2,1)}, u32[]{:S(2)}) copy-start(bf16[768,512]{1,0:T(8,128)(2,1)} %refs_4_.3) | copy-start | bytes 2359300
  42.6 15.5 %copy-start.1 = (bf16[512,512]{1,0:T(8,128)(2,1)S(1)}, bf16[512,512]{1,0:T(8,128)(2,1)}, u32[]{:S(2)}) copy-start(bf16[512,512]{1,0:T(8,128)(2,1)} %refs_5_.1) | copy-start | bytes 1572868
  42.6 15.5 %copy-start.2 = (bf16[512,512]{1,0:T(8,128)(2,1)S(1)}, bf16[512,512]{1,0:T(8,128)(2,1)}, u32[]{:S(2)}) copy-start(bf16[512,512]{1,0:T(8,128)(2,1)} %refs_6_.1) | copy-start | bytes 1572868
  42.6 15.5 %copy-start.3 = (bf16[512,512]{1,0:T(8,128)(2,1)S(1)}, bf16[512,512]{1,0:T(8,128)(2,1)}, u32[]{:S(2)}) copy-start(bf16[512,512]{1,0:T(8,128)(2,1)} %refs_7_.1) | copy-start | bytes 1572868
  42.6 15.5 %copy-start.6 = (bf16[768,512]{1,0:T(8,128)(2,1)S(1)}, bf16[768,512]{1,0:T(8,128)(2,1)}, u32[]{:S(2)}) copy-start(bf16[768,512]{1,0:T(8,128)(2,1)} %k_ref.1) | copy-start | bytes 2359300
  42.7 8.6 %collective-permute-start.11 = (bf16[3,64,512]{2,1,0:T(8,128)(2,1)S(1)}, bf16[3,64,512]{2,1,0:T(8,128)(2,1)S(1)}, u32[]{:S(2)}, u32[]{:S(2)}) collective-permute-start(bf16[3,64,512]{2,1,0:T(8,128)(2,1)S(1)} %pad_maximum_fusion.3), channel_id=1, source_target_pairs={{0,4},{1,9},{2,6},{3,11},{4,0},{5,13},{6,2},{7,15},{8,12},{9,1},{1... | collective-permute-start | bytes 589832 | tf_op jit(solution)/shard_map/ppermute | solution.py:73
  46.0 12.1 %collective-permute-start.14 = (bf16[512,512]{1,0:T(8,128)(2,1)S(1)}, bf16[512,512]{1,0:T(8,128)(2,1)S(1)}, u32[]{:S(2)}, u32[]{:S(2)}) collective-permute-start(bf16[512,512]{1,0:T(8,128)(2,1)S(1)} %broadcast_select_fusion), channel_id=1, source_target_pairs={{0,2},{4,6},{8,10},{12,14},{16,18},{20,22},{24,26},{28,30},{2,0},{... | collective-permute-start | bytes 1572872 | tf_op jit(solution)/shard_map/ppermute | solution.py:84
  51.3 12.2 %collective-permute-start.13 = (bf16[3,128,512]{2,1,0:T(8,128)(2,1)S(1)}, bf16[3,128,512]{2,1,0:T(8,128)(2,1)S(1)}, u32[]{:S(2)}, u32[]{:S(2)}) collective-permute-start(bf16[3,128,512]{2,1,0:T(8,128)(2,1)S(1)} %pad_maximum_fusion.1.refs_2_), channel_id=1, source_target_pairs={{0,8},{1,5},{2,10},{3,7},{4,12},{5,1},{6,14},{7,3},{8,0},{9,13},{1... | collective-permute-start | bytes 1179656 | tf_op jit(solution)/shard_map/ppermute | solution.py:73
  55.1 10.7 %collective-permute-start.10 = (bf16[3,128,512]{2,1,0:T(8,128)(2,1)S(1)}, bf16[3,128,512]{2,1,0:T(8,128)(2,1)S(1)}, u32[]{:S(2)}, u32[]{:S(2)}) collective-permute-start(bf16[3,128,512]{2,1,0:T(8,128)(2,1)S(1)} %pad_maximum_fusion.refs_0_), channel_id=1, source_target_pairs={{0,8},{1,5},{2,10},{3,7},{4,12},{5,1},{6,14},{7,3},{8,0},{9,13},{1... | collective-permute-start | bytes 1179656 | tf_op jit(solution)/shard_map/ppermute | solution.py:73
  65.7 10.3 %copy-start.8 = (f32[512]{0:T(512)S(1)}, f32[512]{0:T(512)}, u32[]{:S(2)}) copy-start(f32[512]{0:T(512)} %param.15) | copy-start | bytes 6148
  69.2 6.8 %collective-permute-start.15 = (f32[8,768]{1,0:T(8,128)S(1)}, f32[8,768]{1,0:T(8,128)S(1)}, u32[]{:S(2)}, u32[]{:S(2)}) collective-permute-start(f32[8,768]{1,0:T(8,128)S(1)} %get-tuple-element.50.sums_ref), channel_id=1, source_target_pairs={{0,1},{1,0},{2,3},{3,2},{4,5},{5,4},{6,7},{7,6},{8,9},{9,8},{10,11... | collective-permute-start | bytes 73736 | tf_op jit(solution)/shard_map/ppermute | solution.py:410

commit v7 on v6

--- a/solution.py
+++ b/solution.py
@@ -241,6 +241,8 @@
     next_refs = refs[11:]
     bits = [bit_here(m) for m in steps]
     seq_index = lax.axis_index("seq")
+    blocks = [slice(start, start + BLOCK) for start in range(0, q_ref.shape[0], BLOCK)]
+    ahead = []
     for at, (old_ref, new_ref) in enumerate(zip((gate_ref, up_ref, down_ref), next_refs)):
         size = old_ref.shape[0] * old_ref.shape[1]
         chunk_rows = old_ref.shape[0] // CHUNKS
@@ -264,16 +266,14 @@
                     there = pl.ds(pl.multiple_of(start, unit), unit)
                     grad = piece[at, block * unit : (block + 1) * unit].astype(F32)
                     new_ref[there] = (old_ref[there].astype(F32) + factor * grad).astype(BF16)
+        if at < 2:
+            ahead.append([dot(q_ref[here], new_ref[...]) for here in blocks])
     for new_ref, part_ref in zip(next_refs, (next_gate_ref, next_up_ref, next_down_ref)):
         kept = part_ref.shape[0]
         start = (seq_index * part_rows) // kept * kept
         part_ref[...] = new_ref[pl.ds(pl.multiple_of(start, kept), kept)]
     ones = jnp.ones((8, attended_ref.shape[1]), BF16)
-    for block in range(q_ref.shape[0] // BLOCK):
-        here = slice(block * BLOCK, (block + 1) * BLOCK)
-        query = q_ref[here]
-        gate_pre = dot(query, next_refs[0][...])
-        up_pre = dot(query, next_refs[1][...])
+    for here, gate_pre, up_pre in zip(blocks, *ahead):
         hidden = (gate_pre * jax.nn.sigmoid(gate_pre) * up_pre).astype(BF16)
         combined = attended_ref[here] + dot(hidden, next_refs[2][...])
         combined_ref[here] = combined

time: 78.2 us -> 77.5 us (level)
  Pallas kernels: 17.2 us -> 16.4 us
where the time goes in v7:
time: 77.5 us; the launch traced here: 76.5 us
  starting transfers between devices  29.4 us (38%)
  waiting for transfers between devices  27.5 us (35%)
  Pallas kernels  16.4 us (21%)
  local copies, waits for them, and re-layouts  1.21 us (2%)
  other arithmetic  1.15 us (1%)
  between operations  0.84 us (1%)
    ppermute x11, waiting for transfers between devices, swap(): return lax.ppermute(x, ('seq', 'head'), pairs)  22.6 us
    ppermute x11, starting transfers between devices, swap(): return lax.ppermute(x, ('seq', 'head'), pairs)  13.2 us
    pallas_call x1, Pallas kernels, body(): pl.pallas_call(functools.partial(grads_kernel, steps[0]), out_shape=[jax....  6.94 us
    ppermute x1, starting transfers between devices, body(): more = [lax.ppermute(sums, 'head', [(0, 1), (1, 0)])]  5.97 us
    pallas_call x1, Pallas kernels, body(): pl.pallas_call(attend_kernel, out_shape=(jax.ShapeDtypeStruct((tok_rows,...  5.3 us
    ppermute x1, starting transfers between devices, shift_passed(): return lax.ppermute(jnp.where(odd, passed, x), 'seq', pairs)  5.23 us
    ppermute x1, starting transfers between devices, pass_on(): lax.ppermute(x, 'seq', [(i, i + 2) for i in range(0, lax.axis_size('seq')...  3.17 us
    ppermute x1, waiting for transfers between devices, shift_passed(): return lax.ppermute(jnp.where(odd, passed, x), 'seq', pairs)  2.95 us
  transfers between devices with their start and end apart: 16, of which 12 were waited for; matrix products, arithmetic and copies ran while one was open for 1% of the time, Pallas kernels for 7%

profile of v7, /device:TPU:17, one launch (start us, length us, event | category | flops | bytes accessed | tf_op | source)
XLA Modules:
  0.0 76.5 jit_solution(3213500906424672512)
XLA Ops:
  0.6 6.9 %gradients.1 = (bf16[512,512]{1,0:T(8,128)(2,1)}, bf16[512,512]{1,0:T(8,128)(2,1)}, bf16[3,128,512]{2,1,0:T(8,128)(2,1)}, bf16[3,128,512]{2,1,0:T(8,128)(2,1)}, ...) custom-call(bf16[768,512]{1,0:T(8,128)(2,1)} %k_ref.1, bf16[768,512]{1,0:T(8,128)(2,1)} %v_ref.1, ...), custom_call_target="tpu_custom_call" | custom-call | flops 2415919104 | bytes 6291456 | tf_op jit(solution)/shard_map/gradients/pallas_call | solution.py:303
  7.6 1.3 %collective-permute-start = (bf16[3,128,512]{2,1,0:T(8,128)(2,1)}, bf16[3,128,512]{2,1,0:T(8,128)(2,1)S(1)}, u32[]{:S(2)}, u32[]{:S(2)}) collective-permute-start(bf16[3,128,512]{2,1,0:T(8,128)(2,1)} %get-tuple-element.30), channel_id=1, source_target_pairs={{0,8},{1,5},{2,10},{3,7},{4,12},{5,1},{6,14},{7,3},{8,0},{9,13},{1... | collective-permute-start | bytes 1179656 | tf_op jit(solution)/shard_map/ppermute | solution.py:73
  8.9 0.2 collective-permute-start.1
  9.1 1.2 %collective-permute-start.3 = (bf16[512,512]{1,0:T(8,128)(2,1)}, bf16[512,512]{1,0:T(8,128)(2,1)S(1)}, u32[]{:S(2)}, u32[]{:S(2)}) collective-permute-start(bf16[512,512]{1,0:T(8,128)(2,1)} %get-tuple-element.36), channel_id=1, source_target_pairs={{0,2},{2,0},{4,6},{6,4},{8,10},{10,8},{12,14},{14,12},{16,18},{18,... | collective-permute-start | bytes 1572872 | tf_op jit(solution)/shard_map/ppermute | solution.py:89
  10.3 4.5 %collective-permute-done.refs_1_ = bf16[3,128,512]{2,1,0:T(8,128)(2,1)S(1)} collective-permute-done((bf16[3,128,512]{2,1,0:T(8,128)(2,1)}, bf16[3,128,512]{2,1,0:T(8,128)(2,1)S(1)}, u32[]{:S(2)}, u32[]{:S(2)}) %collective-permute-start) | collective-permute-done | bytes 393248 | tf_op jit(solution)/shard_map/ppermute | solution.py:73
  14.8 1.1 %copy-done.5 = f32[3,128,512]{2,1,0:T(8,128)S(1)} copy-done((f32[3,128,512]{2,1,0:T(8,128)S(1)}, f32[3,128,512]{2,1,0:T(8,128)}, u32[]{:S(2)}) %copy-start.5) | copy-done | bytes 786456
  16.0 1.4 %collective-permute-start.2 = (bf16[3,64,512]{2,1,0:T(8,128)(2,1)S(1)}, bf16[3,64,512]{2,1,0:T(8,128)(2,1)S(1)}, u32[]{:S(2)}, u32[]{:S(2)}) collective-permute-start(bf16[3,64,512]{2,1,0:T(8,128)(2,1)S(1)} %get-tuple-element.35), channel_id=1, source_target_pairs={{0,4},{1,9},{2,6},{3,11},{4,0},{5,13},{6,2},{7,15},{8,12},{9,1},{1... | collective-permute-start | bytes 589832 | tf_op jit(solution)/shard_map/ppermute | solution.py:73
  17.3 1.7 %collective-permute-done.1.refs_1_ = bf16[3,128,512]{2,1,0:T(8,128)(2,1)S(1)} collective-permute-done((bf16[3,128,512]{2,1,0:T(8,128)(2,1)}, bf16[3,128,512]{2,1,0:T(8,128)(2,1)S(1)}, u32[]{:S(2)}, u32[]{:S(2)}) %collective-permute-start.1) | collective-permute-done | bytes 393248 | tf_op jit(solution)/shard_map/ppermute | solution.py:73
  19.1 1.4 %collective-permute-start.4 = (bf16[3,64,512]{2,1,0:T(8,128)(2,1)S(1)}, bf16[3,64,512]{2,1,0:T(8,128)(2,1)S(1)}, u32[]{:S(2)}, u32[]{:S(2)}) collective-permute-start(bf16[3,64,512]{2,1,0:T(8,128)(2,1)S(1)} %get-tuple-element.38), channel_id=1, source_target_pairs={{0,4},{1,9},{2,6},{3,11},{4,0},{5,13},{6,2},{7,15},{8,12},{9,1},{1... | collective-permute-start | bytes 589832 | tf_op jit(solution)/shard_map/ppermute | solution.py:73
  20.4 1.1 %collective-permute-done.3.odd_k = bf16[512,512]{1,0:T(8,128)(2,1)S(1)} collective-permute-done((bf16[512,512]{1,0:T(8,128)(2,1)}, bf16[512,512]{1,0:T(8,128)(2,1)S(1)}, u32[]{:S(2)}, u32[]{:S(2)}) %collective-permute-start.3) | collective-permute-done | bytes 524320 | tf_op jit(solution)/shard_map/ppermute | solution.py:89
  21.5 0.7 collective-permute-done.2.refs_2_
  22.2 1.8 %collective-permute-done.4.refs_3_ = bf16[3,64,512]{2,1,0:T(8,128)(2,1)S(1)} collective-permute-done((bf16[3,64,512]{2,1,0:T(8,128)(2,1)S(1)}, bf16[3,64,512]{2,1,0:T(8,128)(2,1)S(1)}, u32[]{:S(2)}, u32[]{:S(2)}) %collective-permute-start.4) | collective-permute-done | bytes 196640 | tf_op jit(solution)/shard_map/ppermute | solution.py:73
  24.1 1.3 %collective-permute-start.5 = (bf16[3,64,512]{2,1,0:T(8,128)(2,1)S(1)}, bf16[3,64,512]{2,1,0:T(8,128)(2,1)S(1)}, u32[]{:S(2)}, u32[]{:S(2)}) collective-permute-start(bf16[3,64,512]{2,1,0:T(8,128)(2,1)S(1)} %get-tuple-element.40), channel_id=1, source_target_pairs={{0,2},{1,3},{2,0},{3,1},{4,6},{5,7},{6,4},{7,5},{8,10},{9,11},{10,... | collective-permute-start | bytes 589832 | tf_op jit(solution)/shard_map/ppermute | solution.py:73
  25.4 3.3 %collective-permute-done.5 = bf16[3,64,512]{2,1,0:T(8,128)(2,1)S(1)} collective-permute-done((bf16[3,64,512]{2,1,0:T(8,128)(2,1)S(1)}, bf16[3,64,512]{2,1,0:T(8,128)(2,1)S(1)}, u32[]{:S(2)}, u32[]{:S(2)}) %collective-permute-start.5) | collective-permute-done | bytes 196640 | tf_op jit(solution)/shard_map/ppermute | solution.py:73
  28.8 0.7 collective-permute-start.9
  29.5 3.2 %collective-permute-start.12 = (bf16[512,512]{1,0:T(8,128)(2,1)S(1)}, bf16[512,512]{1,0:T(8,128)(2,1)S(1)}, u32[]{:S(2)}, u32[]{:S(2)}) collective-permute-start(bf16[512,512]{1,0:T(8,128)(2,1)S(1)} %collective-permute-done.3.odd_k), channel_id=1, source_target_pairs={{0,4},{4,8},{8,12},{12,16},{16,20},{20,24},{24,28},{1,5},{5,9},{9,... | collective-permute-start | bytes 1572872 | tf_op jit(solution)/shard_map/ppermute | solution.py:93
  32.7 1.6 %collective-permute-done.6 = bf16[3,64,512]{2,1,0:T(8,128)(2,1)S(1)} collective-permute-done((bf16[3,64,512]{2,1,0:T(8,128)(2,1)S(1)}, bf16[3,64,512]{2,1,0:T(8,128)(2,1)S(1)}, u32[]{:S(2)}, u32[]{:S(2)}) %collective-permute-start.6) | collective-permute-done | bytes 196640 | tf_op jit(solution)/shard_map/ppermute | solution.py:73
  34.4 1.3 %collective-permute-start.7 = (bf16[3,64,512]{2,1,0:T(8,128)(2,1)S(1)}, bf16[3,64,512]{2,1,0:T(8,128)(2,1)S(1)}, u32[]{:S(2)}, u32[]{:S(2)}) collective-permute-start(bf16[3,64,512]{2,1,0:T(8,128)(2,1)S(1)} %add_convert_fusion), channel_id=1, source_target_pairs={{0,2},{1,3},{2,0},{3,1},{4,6},{5,7},{6,4},{7,5},{8,10},{9,11},{10,... | collective-permute-start | bytes 589832 | tf_op jit(solution)/shard_map/ppermute | solution.py:73
  35.7 3.6 %collective-permute-done.7 = bf16[3,64,512]{2,1,0:T(8,128)(2,1)S(1)} collective-permute-done((bf16[3,64,512]{2,1,0:T(8,128)(2,1)S(1)}, bf16[3,64,512]{2,1,0:T(8,128)(2,1)S(1)}, u32[]{:S(2)}, u32[]{:S(2)}) %collective-permute-start.7) | collective-permute-done | bytes 196640 | tf_op jit(solution)/shard_map/ppermute | solution.py:73
  39.3 3.3 %collective-permute-start.8 = (bf16[3,64,512]{2,1,0:T(8,128)(2,1)S(1)}, bf16[3,64,512]{2,1,0:T(8,128)(2,1)}, u32[]{:S(2)}, u32[]{:S(2)}) collective-permute-start(bf16[3,64,512]{2,1,0:T(8,128)(2,1)S(1)} %pad_maximum_fusion.2), channel_id=1, source_target_pairs={{0,4},{1,9},{2,6},{3,11},{4,0},{5,13},{6,2},{7,15},{8,12},{9,1},{1... | collective-permute-start | bytes 589832 | tf_op jit(solution)/shard_map/ppermute | solution.py:73
  42.7 0.1 collective-permute-start.11
  42.8 3.2 %collective-permute-done.8 = bf16[3,64,512]{2,1,0:T(8,128)(2,1)} collective-permute-done((bf16[3,64,512]{2,1,0:T(8,128)(2,1)S(1)}, bf16[3,64,512]{2,1,0:T(8,128)(2,1)}, u32[]{:S(2)}, u32[]{:S(2)}) %collective-permute-start.8) | collective-permute-done | bytes 196640 | tf_op jit(solution)/shard_map/ppermute | solution.py:73
  46.0 5.2 %collective-permute-start.14 = (bf16[512,512]{1,0:T(8,128)(2,1)S(1)}, bf16[512,512]{1,0:T(8,128)(2,1)S(1)}, u32[]{:S(2)}, u32[]{:S(2)}) collective-permute-start(bf16[512,512]{1,0:T(8,128)(2,1)S(1)} %broadcast_select_fusion), channel_id=1, source_target_pairs={{0,2},{4,6},{8,10},{12,14},{16,18},{20,22},{24,26},{28,30},{2,0},{... | collective-permute-start | bytes 1572872 | tf_op jit(solution)/shard_map/ppermute | solution.py:84
  51.3 2.8 %collective-permute-start.13 = (bf16[3,128,512]{2,1,0:T(8,128)(2,1)S(1)}, bf16[3,128,512]{2,1,0:T(8,128)(2,1)S(1)}, u32[]{:S(2)}, u32[]{:S(2)}) collective-permute-start(bf16[3,128,512]{2,1,0:T(8,128)(2,1)S(1)} %pad_maximum_fusion.1.refs_2_), channel_id=1, source_target_pairs={{0,8},{1,5},{2,10},{3,7},{4,12},{5,1},{6,14},{7,3},{8,0},{9,13},{1... | collective-permute-start | bytes 1179656 | tf_op jit(solution)/shard_map/ppermute | solution.py:73
  54.1 1.0 %pad_maximum_fusion.refs_0_ = bf16[3,128,512]{2,1,0:T(8,128)(2,1)S(1)} fusion(bf16[3,64,512]{2,1,0:T(8,128)(2,1)} %collective-permute-done.8, bf16[3,32,512]{2,1,0:T(8,128)(2,1)S(1)} %get-tuple-element.57, bf16[3,32,512]{2,1,0:T(8,128)(2,1)S(1)} %get-tuple-element.55), kind=kLoop, calls=%fused_computation.1 | loop fusion | flops 1179648 | bytes 786432 | tf_op jit(solution)/shard_map/concatenate | solution.py:361
  55.1 2.9 %collective-permute-done.14.prev_v = bf16[512,512]{1,0:T(8,128)(2,1)S(1)} collective-permute-done((bf16[512,512]{1,0:T(8,128)(2,1)S(1)}, bf16[512,512]{1,0:T(8,128)(2,1)S(1)}, u32[]{:S(2)}, u32[]{:S(2)}) %collective-permute-start.14) | collective-permute-done | bytes 524320 | tf_op jit(solution)/shard_map/ppermute | solution.py:84
  58.1 5.3 %window_attention.1 = (f32[768,512]{1,0:T(8,128)S(1)}, f32[3,8,512]{2,1,0:T(8,128)S(1)}) custom-call(bf16[768,512]{1,0:T(8,128)(2,1)S(1)} %copy-done, bf16[768,512]{1,0:T(8,128)(2,1)S(1)} %copy-done.6, bf16[768,512]{1,0:T(8,128)(2,1)S(1)} %copy-done.7, bf16[512,512]{1,0:T(8,128)(2,1)S(1)} %collective-permute-done.3.odd_k, ...), custom_call_target="tpu_custom_call" | custom-call | flops 1207959552 | bytes 3145728 | tf_op jit(solution)/shard_map/window_attention/pallas_call | solution.py:364
  63.4 2.3 %collective-permute-done.10.refs_1_ = bf16[3,128,512]{2,1,0:T(8,128)(2,1)S(1)} collective-permute-done((bf16[3,128,512]{2,1,0:T(8,128)(2,1)S(1)}, bf16[3,128,512]{2,1,0:T(8,128)(2,1)S(1)}, u32[]{:S(2)}, u32[]{:S(2)}) %collective-permute-start.10) | collective-permute-done | bytes 393248 | tf_op jit(solution)/shard_map/ppermute | solution.py:73
  65.7 2.7 %apply.1 = (f32[768,512]{1,0:T(8,128)S(1)}, f32[8,768]{1,0:T(8,128)S(1)}, bf16[32,512]{1,0:T(8,128)(2,1)}, bf16[32,512]{1,0:T(8,128)(2,1)}, bf16[32,512]{1,0:T(8,128)(2,1)}) custom-call(bf16[3,128,512]{2,1,0:T(8,128)(2,1)S(1)} %pad_maximum_fusion.refs_0_, bf16[3,128,512]{2,1,0:T(8,128)(2,1)S(1)} %collective-permute-done.10.refs_1_, ...), custom_call_target="tpu_custom_call" | custom-call | flops 1207959552 | bytes 4718592 | tf_op jit(solution)/shard_map/apply/pallas_call | solution.py:386
  68.5 6.0 %collective-permute-start.15 = (f32[8,768]{1,0:T(8,128)S(1)}, f32[8,768]{1,0:T(8,128)S(1)}, u32[]{:S(2)}, u32[]{:S(2)}) collective-permute-start(f32[8,768]{1,0:T(8,128)S(1)} %get-tuple-element.50.sums_ref), channel_id=1, source_target_pairs={{0,1},{1,0},{2,3},{3,2},{4,5},{5,4},{6,7},{7,6},{8,9},{9,8},{10,11... | collective-permute-start | bytes 73736 | tf_op jit(solution)/shard_map/ppermute | solution.py:410
  74.4 0.8 %collective-permute-done.15.more_ref = f32[8,768]{1,0:T(8,128)S(1)} collective-permute-done((f32[8,768]{1,0:T(8,128)S(1)}, f32[8,768]{1,0:T(8,128)S(1)}, u32[]{:S(2)}, u32[]{:S(2)}) %collective-permute-start.15) | collective-permute-done | bytes 24608 | tf_op jit(solution)/shard_map/ppermute | solution.py:410
  75.3 1.2 %norm.1 = bf16[768,512]{1,0:T(8,128)(2,1)} custom-call(f32[768,512]{1,0:T(8,128)S(1)} %get-tuple-element.49.combined_ref, f32[8,768]{1,0:T(8,128)S(1)} %get-tuple-element.50.sums_ref, f32[8,768]{1,0:T(8,128)S(1)} %collective-permute-done.15.more_ref, f32[1,512]{1,0:T(1,128)S(1)} %bitcast.2), custom_call_target="tpu_custom_call" | custom-call | flops 1572864 | bytes 2359296 | tf_op jit(solution)/shard_map/norm/pallas_call | solution.py:418
  (36 shorter events, 0.6 us)
Async XLA Ops:
  7.6 11.4 %copy-start.4 = (f32[3,128,512]{2,1,0:T(8,128)S(1)}, f32[3,128,512]{2,1,0:T(8,128)}, u32[]{:S(2)}) copy-start(f32[3,128,512]{2,1,0:T(8,128)} %get-tuple-element.32.refs_0_) | copy-start | bytes 2359300
  7.6 7.2 %collective-permute-start = (bf16[3,128,512]{2,1,0:T(8,128)(2,1)}, bf16[3,128,512]{2,1,0:T(8,128)(2,1)S(1)}, u32[]{:S(2)}, u32[]{:S(2)}) collective-permute-start(bf16[3,128,512]{2,1,0:T(8,128)(2,1)} %get-tuple-element.30), channel_id=1, source_target_pairs={{0,8},{1,5},{2,10},{3,7},{4,12},{5,1},{6,14},{7,3},{8,0},{9,13},{1... | collective-permute-start | bytes 1179656 | tf_op jit(solution)/shard_map/ppermute | solution.py:73
  8.9 10.1 %collective-permute-start.1 = (bf16[3,128,512]{2,1,0:T(8,128)(2,1)}, bf16[3,128,512]{2,1,0:T(8,128)(2,1)S(1)}, u32[]{:S(2)}, u32[]{:S(2)}) collective-permute-start(bf16[3,128,512]{2,1,0:T(8,128)(2,1)} %get-tuple-element.33), channel_id=1, source_target_pairs={{0,8},{1,5},{2,10},{3,7},{4,12},{5,1},{6,14},{7,3},{8,0},{9,13},{1... | collective-permute-start | bytes 1179656 | tf_op jit(solution)/shard_map/ppermute | solution.py:73
  9.1 12.4 %collective-permute-start.3 = (bf16[512,512]{1,0:T(8,128)(2,1)}, bf16[512,512]{1,0:T(8,128)(2,1)S(1)}, u32[]{:S(2)}, u32[]{:S(2)}) collective-permute-start(bf16[512,512]{1,0:T(8,128)(2,1)} %get-tuple-element.36), channel_id=1, source_target_pairs={{0,2},{2,0},{4,6},{6,4},{8,10},{10,8},{12,14},{14,12},{16,18},{18,... | collective-permute-start | bytes 1572872 | tf_op jit(solution)/shard_map/ppermute | solution.py:89
  14.8 1.1 %copy-start.5 = (f32[3,128,512]{2,1,0:T(8,128)S(1)}, f32[3,128,512]{2,1,0:T(8,128)}, u32[]{:S(2)}) copy-start(f32[3,128,512]{2,1,0:T(8,128)} %get-tuple-element.29.refs_0_) | copy-start | bytes 2359300
  16.0 6.3 %collective-permute-start.2 = (bf16[3,64,512]{2,1,0:T(8,128)(2,1)S(1)}, bf16[3,64,512]{2,1,0:T(8,128)(2,1)S(1)}, u32[]{:S(2)}, u32[]{:S(2)}) collective-permute-start(bf16[3,64,512]{2,1,0:T(8,128)(2,1)S(1)} %get-tuple-element.35), channel_id=1, source_target_pairs={{0,4},{1,9},{2,6},{3,11},{4,0},{5,13},{6,2},{7,15},{8,12},{9,1},{1... | collective-permute-start | bytes 589832 | tf_op jit(solution)/shard_map/ppermute | solution.py:73
  19.0 9.8 %copy-start.9 = (bf16[512,512]{1,0:T(8,128)(2,1)S(1)}, bf16[512,512]{1,0:T(8,128)(2,1)}, u32[]{:S(2)}) copy-start(bf16[512,512]{1,0:T(8,128)(2,1)} %get-tuple-element.41) | copy-start | bytes 1572868
  19.1 5.0 %collective-permute-start.4 = (bf16[3,64,512]{2,1,0:T(8,128)(2,1)S(1)}, bf16[3,64,512]{2,1,0:T(8,128)(2,1)S(1)}, u32[]{:S(2)}, u32[]{:S(2)}) collective-permute-start(bf16[3,64,512]{2,1,0:T(8,128)(2,1)S(1)} %get-tuple-element.38), channel_id=1, source_target_pairs={{0,4},{1,9},{2,6},{3,11},{4,0},{5,13},{6,2},{7,15},{8,12},{9,1},{1... | collective-permute-start | bytes 589832 | tf_op jit(solution)/shard_map/ppermute | solution.py:73
  24.1 4.6 %collective-permute-start.5 = (bf16[3,64,512]{2,1,0:T(8,128)(2,1)S(1)}, bf16[3,64,512]{2,1,0:T(8,128)(2,1)S(1)}, u32[]{:S(2)}, u32[]{:S(2)}) collective-permute-start(bf16[3,64,512]{2,1,0:T(8,128)(2,1)S(1)} %get-tuple-element.40), channel_id=1, source_target_pairs={{0,2},{1,3},{2,0},{3,1},{4,6},{5,7},{6,4},{7,5},{8,10},{9,11},{10,... | collective-permute-start | bytes 589832 | tf_op jit(solution)/shard_map/ppermute | solution.py:73
  28.7 5.6 %collective-permute-start.6 = (bf16[3,64,512]{2,1,0:T(8,128)(2,1)S(1)}, bf16[3,64,512]{2,1,0:T(8,128)(2,1)S(1)}, u32[]{:S(2)}, u32[]{:S(2)}) collective-permute-start(bf16[3,64,512]{2,1,0:T(8,128)(2,1)S(1)} %add_convert_fusion.1), channel_id=1, source_target_pairs={{0,16},{1,17},{2,18},{3,19},{4,20},{5,21},{6,22},{7,23},{8,24},{9,... | collective-permute-start | bytes 589832 | tf_op jit(solution)/shard_map/ppermute | solution.py:73
  28.8 13.9 %collective-permute-start.9 = (bf16[512,512]{1,0:T(8,128)(2,1)S(1)}, bf16[512,512]{1,0:T(8,128)(2,1)S(1)}, u32[]{:S(2)}, u32[]{:S(2)}) collective-permute-start(bf16[512,512]{1,0:T(8,128)(2,1)S(1)} %copy-done.9), channel_id=1, source_target_pairs={{2,6},{6,10},{10,14},{14,18},{18,22},{22,26},{26,30},{3,7},{7,11},... | collective-permute-start | bytes 1572872 | tf_op jit(solution)/shard_map/ppermute | solution.py:77
  29.5 21.7 %collective-permute-start.12 = (bf16[512,512]{1,0:T(8,128)(2,1)S(1)}, bf16[512,512]{1,0:T(8,128)(2,1)S(1)}, u32[]{:S(2)}, u32[]{:S(2)}) collective-permute-start(bf16[512,512]{1,0:T(8,128)(2,1)S(1)} %collective-permute-done.3.odd_k), channel_id=1, source_target_pairs={{0,4},{4,8},{8,12},{12,16},{16,20},{20,24},{24,28},{1,5},{5,9},{9,... | collective-permute-start | bytes 1572872 | tf_op jit(solution)/shard_map/ppermute | solution.py:93
  34.4 4.9 %collective-permute-start.7 = (bf16[3,64,512]{2,1,0:T(8,128)(2,1)S(1)}, bf16[3,64,512]{2,1,0:T(8,128)(2,1)S(1)}, u32[]{:S(2)}, u32[]{:S(2)}) collective-permute-start(bf16[3,64,512]{2,1,0:T(8,128)(2,1)S(1)} %add_convert_fusion), channel_id=1, source_target_pairs={{0,2},{1,3},{2,0},{3,1},{4,6},{5,7},{6,4},{7,5},{8,10},{9,11},{10,... | collective-permute-start | bytes 589832 | tf_op jit(solution)/shard_map/ppermute | solution.py:73
  39.3 18.8 %copy-start.7 = (bf16[768,512]{1,0:T(8,128)(2,1)S(1)}, bf16[768,512]{1,0:T(8,128)(2,1)}, u32[]{:S(2)}) copy-start(bf16[768,512]{1,0:T(8,128)(2,1)} %v_ref.1) | copy-start | bytes 2359300
  39.3 6.6 %collective-permute-start.8 = (bf16[3,64,512]{2,1,0:T(8,128)(2,1)S(1)}, bf16[3,64,512]{2,1,0:T(8,128)(2,1)}, u32[]{:S(2)}, u32[]{:S(2)}) collective-permute-start(bf16[3,64,512]{2,1,0:T(8,128)(2,1)S(1)} %pad_maximum_fusion.2), channel_id=1, source_target_pairs={{0,4},{1,9},{2,6},{3,11},{4,0},{5,13},{6,2},{7,15},{8,12},{9,1},{1... | collective-permute-start | bytes 589832 | tf_op jit(solution)/shard_map/ppermute | solution.py:73
  42.6 15.5 %copy-start = (bf16[768,512]{1,0:T(8,128)(2,1)S(1)}, bf16[768,512]{1,0:T(8,128)(2,1)}, u32[]{:S(2)}) copy-start(bf16[768,512]{1,0:T(8,128)(2,1)} %refs_4_.3) | copy-start | bytes 2359300
  42.6 15.5 %copy-start.1 = (bf16[512,512]{1,0:T(8,128)(2,1)S(1)}, bf16[512,512]{1,0:T(8,128)(2,1)}, u32[]{:S(2)}) copy-start(bf16[512,512]{1,0:T(8,128)(2,1)} %refs_5_.1) | copy-start | bytes 1572868
  42.6 15.5 %copy-start.2 = (bf16[512,512]{1,0:T(8,128)(2,1)S(1)}, bf16[512,512]{1,0:T(8,128)(2,1)}, u32[]{:S(2)}) copy-start(bf16[512,512]{1,0:T(8,128)(2,1)} %refs_6_.1) | copy-start | bytes 1572868
  42.6 15.5 %copy-start.3 = (bf16[512,512]{1,0:T(8,128)(2,1)S(1)}, bf16[512,512]{1,0:T(8,128)(2,1)}, u32[]{:S(2)}) copy-start(bf16[512,512]{1,0:T(8,128)(2,1)} %refs_7_.1) | copy-start | bytes 1572868
  42.6 15.5 %copy-start.6 = (bf16[768,512]{1,0:T(8,128)(2,1)S(1)}, bf16[768,512]{1,0:T(8,128)(2,1)}, u32[]{:S(2)}) copy-start(bf16[768,512]{1,0:T(8,128)(2,1)} %k_ref.1) | copy-start | bytes 2359300
  42.7 8.6 %collective-permute-start.11 = (bf16[3,64,512]{2,1,0:T(8,128)(2,1)S(1)}, bf16[3,64,512]{2,1,0:T(8,128)(2,1)S(1)}, u32[]{:S(2)}, u32[]{:S(2)}) collective-permute-start(bf16[3,64,512]{2,1,0:T(8,128)(2,1)S(1)} %pad_maximum_fusion.3), channel_id=1, source_target_pairs={{0,4},{1,9},{2,6},{3,11},{4,0},{5,13},{6,2},{7,15},{8,12},{9,1},{1... | collective-permute-start | bytes 589832 | tf_op jit(solution)/shard_map/ppermute | solution.py:73
  46.0 12.1 %collective-permute-start.14 = (bf16[512,512]{1,0:T(8,128)(2,1)S(1)}, bf16[512,512]{1,0:T(8,128)(2,1)S(1)}, u32[]{:S(2)}, u32[]{:S(2)}) collective-permute-start(bf16[512,512]{1,0:T(8,128)(2,1)S(1)} %broadcast_select_fusion), channel_id=1, source_target_pairs={{0,2},{4,6},{8,10},{12,14},{16,18},{20,22},{24,26},{28,30},{2,0},{... | collective-permute-start | bytes 1572872 | tf_op jit(solution)/shard_map/ppermute | solution.py:84
  51.3 12.2 %collective-permute-start.13 = (bf16[3,128,512]{2,1,0:T(8,128)(2,1)S(1)}, bf16[3,128,512]{2,1,0:T(8,128)(2,1)S(1)}, u32[]{:S(2)}, u32[]{:S(2)}) collective-permute-start(bf16[3,128,512]{2,1,0:T(8,128)(2,1)S(1)} %pad_maximum_fusion.1.refs_2_), channel_id=1, source_target_pairs={{0,8},{1,5},{2,10},{3,7},{4,12},{5,1},{6,14},{7,3},{8,0},{9,13},{1... | collective-permute-start | bytes 1179656 | tf_op jit(solution)/shard_map/ppermute | solution.py:73
  55.1 10.7 %collective-permute-start.10 = (bf16[3,128,512]{2,1,0:T(8,128)(2,1)S(1)}, bf16[3,128,512]{2,1,0:T(8,128)(2,1)S(1)}, u32[]{:S(2)}, u32[]{:S(2)}) collective-permute-start(bf16[3,128,512]{2,1,0:T(8,128)(2,1)S(1)} %pad_maximum_fusion.refs_0_), channel_id=1, source_target_pairs={{0,8},{1,5},{2,10},{3,7},{4,12},{5,1},{6,14},{7,3},{8,0},{9,13},{1... | collective-permute-start | bytes 1179656 | tf_op jit(solution)/shard_map/ppermute | solution.py:73
  65.7 9.6 %copy-start.8 = (f32[512]{0:T(512)S(1)}, f32[512]{0:T(512)}, u32[]{:S(2)}) copy-start(f32[512]{0:T(512)} %param.15) | copy-start | bytes 6148
  68.5 6.8 %collective-permute-start.15 = (f32[8,768]{1,0:T(8,128)S(1)}, f32[8,768]{1,0:T(8,128)S(1)}, u32[]{:S(2)}, u32[]{:S(2)}) collective-permute-start(f32[8,768]{1,0:T(8,128)S(1)} %get-tuple-element.50.sums_ref), channel_id=1, source_target_pairs={{0,1},{1,0},{2,3},{3,2},{4,5},{5,4},{6,7},{7,6},{8,9},{9,8},{10,11... | collective-permute-start | bytes 73736 | tf_op jit(solution)/shard_map/ppermute | solution.py:410

commit v8 on v7

--- a/solution.py
+++ b/solution.py
@@ -121,13 +121,18 @@
     for at, place in enumerate(places):
         order_ref[:, place] = k_ref[:, at * half : (at + 1) * half]
     rate_col = jnp.transpose(jnp.broadcast_to(rate_ref[...], (8, rows)))[:, :1]
-    for copy in copies[1:]:
-        copy.wait()
-    tails[1].start()
     for start in range(0, rows, BLOCK):
         here = slice(start, start + BLOCK)
+        if start == 0:
+            copies[1].wait()
         gate_pre = dot(k_ref[here], gate_ref[...])
+        if start == 0:
+            copies[2].wait()
         up_pre = dot(k_ref[here], up_ref[...])
+        if start == 0:
+            copies[3].wait()
+            copies[4].wait()
+            tails[1].start()
         target = (rate_col[here] * v_ref[here].astype(F32)).astype(BF16)
         target_ref[here] = target
         backward = outer_cols(target, down_ref[...])
@@ -283,10 +288,20 @@
         sums_ref[:, here] = outer_cols(ones, high) + outer_cols(ones, low)
 
 
-def norm_kernel(width, combined_ref, sums_ref, more_ref, gain_ref, out_ref):
-    sums = sums_ref[...] if more_ref is None else sums_ref[...] + more_ref[...]
+def norm_kernel(width, combined_ref, *refs):
+    *sums_refs, gain_ref, out_hbm, held_ref, sems = refs
+    sums = sums_refs[0][...]
+    for ref in sums_refs[1:]:
+        sums = sums + ref[...]
     scale = jnp.transpose(lax.rsqrt(sums / width + EPSILON))[:, :1]
-    out_ref[...] = (combined_ref[...] * scale * gain_ref[...]).astype(BF16)
+    copies = []
+    for at, start in enumerate(range(0, held_ref.shape[0], BLOCK // 2)):
+        here = slice(start, start + BLOCK // 2)
+        held_ref[here] = (combined_ref[here] * scale[here] * gain_ref[...]).astype(BF16)
+        copies.append(pltpu.make_async_copy(held_ref.at[here], out_hbm.at[here], sems.at[at]))
+        copies[-1].start()
+    for copy in copies:
+        copy.wait()
 
 
 def body(queries, keys, values, rates, w_gate, w_up, w_down, out_gain):
@@ -353,11 +368,9 @@
         here = slice(c * rows, (c + 1) * rows)
         piece = jnp.concatenate([total[:, here], more[:, here]], axis=1)
         came = swap(piece, steps[1])
-        if c == 0:
-            came, passed = lax.optimization_barrier((came, passed))
+        if c == 1:
+            came, passed, before_k = lax.optimization_barrier((came, passed, before_k))
             prev_v = shift_passed(value_tail, passed)
-        if c == 1:
-            came, before_k = lax.optimization_barrier((came, before_k))
         piece = jnp.concatenate([piece, came], axis=1)
         pieces += [piece, swap(piece, steps[0])]
 
@@ -407,21 +420,25 @@
 
     width = fw_dim * head_count
     if head_count == 2:
-        more = [lax.ppermute(sums, "head", [(0, 1), (1, 0)])]
-        norm = functools.partial(norm_kernel, width)
+        sums = [sums, lax.ppermute(sums, "head", [(0, 1), (1, 0)])]
     else:
-        sums, more = lax.psum(sums, "head"), []
-
-        def norm(combined_ref, sums_ref, gain_ref, out_ref):
-            norm_kernel(width, combined_ref, sums_ref, None, gain_ref, out_ref)
-
-    output = kernel_call(
-        norm,
-        "norm",
-        jax.ShapeDtypeStruct((tok_rows, fw_dim), BF16),
-        4 * tok_rows * fw_dim,
-        6 * tok_rows * fw_dim,
-    )(combined, sums, *more, out_gain.reshape(1, fw_dim))
+        sums = [lax.psum(sums, "head")]
+    output = pl.pallas_call(
+        functools.partial(norm_kernel, width),
+        out_shape=jax.ShapeDtypeStruct((tok_rows, fw_dim), BF16),
+        out_specs=hbm,
+        name="norm",
+        scratch_shapes=[
+            pltpu.VMEM((tok_rows, fw_dim), BF16),
+            pltpu.SemaphoreType.DMA((2 * tok_rows // BLOCK,)),
+        ],
+        compiler_params=pltpu.CompilerParams(vmem_limit_bytes=VMEM_LIMIT),
+        cost_estimate=pl.CostEstimate(
+            flops=4 * tok_rows * fw_dim,
+            bytes_accessed=6 * tok_rows * fw_dim,
+            transcendentals=0,
+        ),
+    )(combined, *sums, out_gain.reshape(1, fw_dim))
     return (output, *parts)
 
 

time: 77.5 us -> 77.4 us (level)
  starting transfers between devices: 29.4 us -> 25.5 us
  waiting for transfers between devices: 27.5 us -> 31.4 us
    ppermute x1, waiting for transfers between devices: 0.01 us -> 7.13 us  [pass_on(): lax.ppermute(x, 'seq', [(i, i + 2) for i in range(0, lax.axis_size('seq')...]
    ppermute x1, starting transfers between devices: 5.23 us -> 1.27 us  [shift_passed(): return lax.ppermute(jnp.where(odd, passed, x), 'seq', pairs)]
    ppermute x11, waiting for transfers between devices: 22.6 us -> 19.2 us  [swap(): return lax.ppermute(x, ('seq', 'head'), pairs)]
where the time goes in v8:
time: 77.4 us; the launch traced here: 76.4 us
  waiting for transfers between devices  31.4 us (41%)
  starting transfers between devices  25.5 us (33%)
  Pallas kernels  16.1 us (21%)
  local copies, waits for them, and re-layouts  1.21 us (2%)
  other arithmetic  1.15 us (1%)
  between operations  1 us (1%)
    ppermute x11, waiting for transfers between devices, swap(): return lax.ppermute(x, ('seq', 'head'), pairs)  19.2 us
    ppermute x11, starting transfers between devices, swap(): return lax.ppermute(x, ('seq', 'head'), pairs)  13.2 us
    ppermute x1, waiting for transfers between devices, pass_on(): lax.ppermute(x, 'seq', [(i, i + 2) for i in range(0, lax.axis_size('seq')...  7.13 us
    pallas_call x1, Pallas kernels, body(): pl.pallas_call(functools.partial(grads_kernel, steps[0]), out_shape=[jax....  6.75 us
    ppermute x1, starting transfers between devices, body(): sums = [sums, lax.ppermute(sums, 'head', [(0, 1), (1, 0)])]  5.97 us
    pallas_call x1, Pallas kernels, body(): pl.pallas_call(attend_kernel, out_shape=(jax.ShapeDtypeStruct((tok_rows,...  5.29 us
    ppermute x1, waiting for transfers between devices, shift_passed(): return lax.ppermute(jnp.where(odd, passed, x), 'seq', pairs)  3.2 us
    ppermute x1, starting transfers between devices, pass_on(): lax.ppermute(x, 'seq', [(i, i + 2) for i in range(0, lax.axis_size('seq')...  3.17 us
  transfers between devices with their start and end apart: 16, of which 12 were waited for; matrix products, arithmetic and copies ran while one was open for 1% of the time, Pallas kernels for 7%

profile of v8, /device:TPU:17, one launch (start us, length us, event | category | flops | bytes accessed | tf_op | source)
XLA Modules:
  0.0 76.4 jit_solution(2697226763931406726)
XLA Ops:
  0.6 6.7 %gradients.1 = (bf16[512,512]{1,0:T(8,128)(2,1)}, bf16[512,512]{1,0:T(8,128)(2,1)}, bf16[3,128,512]{2,1,0:T(8,128)(2,1)}, bf16[3,128,512]{2,1,0:T(8,128)(2,1)}, ...) custom-call(bf16[768,512]{1,0:T(8,128)(2,1)} %k_ref.1, bf16[768,512]{1,0:T(8,128)(2,1)} %v_ref.1, ...), custom_call_target="tpu_custom_call" | custom-call | flops 2415919104 | bytes 6291456 | tf_op jit(solution)/shard_map/gradients/pallas_call | solution.py:318
  7.4 1.3 %collective-permute-start = (bf16[3,128,512]{2,1,0:T(8,128)(2,1)}, bf16[3,128,512]{2,1,0:T(8,128)(2,1)S(1)}, u32[]{:S(2)}, u32[]{:S(2)}) collective-permute-start(bf16[3,128,512]{2,1,0:T(8,128)(2,1)} %get-tuple-element.29), channel_id=1, source_target_pairs={{0,8},{1,5},{2,10},{3,7},{4,12},{5,1},{6,14},{7,3},{8,0},{9,13},{1... | collective-permute-start | bytes 1179656 | tf_op jit(solution)/shard_map/ppermute | solution.py:73
  8.7 0.2 collective-permute-start.1
  8.9 1.2 %collective-permute-start.3 = (bf16[512,512]{1,0:T(8,128)(2,1)}, bf16[512,512]{1,0:T(8,128)(2,1)S(1)}, u32[]{:S(2)}, u32[]{:S(2)}) collective-permute-start(bf16[512,512]{1,0:T(8,128)(2,1)} %get-tuple-element.35), channel_id=1, source_target_pairs={{0,2},{2,0},{4,6},{6,4},{8,10},{10,8},{12,14},{14,12},{16,18},{18,... | collective-permute-start | bytes 1572872 | tf_op jit(solution)/shard_map/ppermute | solution.py:89
  10.1 4.5 %collective-permute-done.refs_1_ = bf16[3,128,512]{2,1,0:T(8,128)(2,1)S(1)} collective-permute-done((bf16[3,128,512]{2,1,0:T(8,128)(2,1)}, bf16[3,128,512]{2,1,0:T(8,128)(2,1)S(1)}, u32[]{:S(2)}, u32[]{:S(2)}) %collective-permute-start) | collective-permute-done | bytes 393248 | tf_op jit(solution)/shard_map/ppermute | solution.py:73
  14.6 1.1 %copy-done.5 = f32[3,128,512]{2,1,0:T(8,128)S(1)} copy-done((f32[3,128,512]{2,1,0:T(8,128)S(1)}, f32[3,128,512]{2,1,0:T(8,128)}, u32[]{:S(2)}) %copy-start.5) | copy-done | bytes 786456
  15.8 1.4 %collective-permute-start.2 = (bf16[3,64,512]{2,1,0:T(8,128)(2,1)S(1)}, bf16[3,64,512]{2,1,0:T(8,128)(2,1)S(1)}, u32[]{:S(2)}, u32[]{:S(2)}) collective-permute-start(bf16[3,64,512]{2,1,0:T(8,128)(2,1)S(1)} %get-tuple-element.34), channel_id=1, source_target_pairs={{0,4},{1,9},{2,6},{3,11},{4,0},{5,13},{6,2},{7,15},{8,12},{9,1},{1... | collective-permute-start | bytes 589832 | tf_op jit(solution)/shard_map/ppermute | solution.py:73
  17.2 1.6 %collective-permute-done.1.refs_1_ = bf16[3,128,512]{2,1,0:T(8,128)(2,1)S(1)} collective-permute-done((bf16[3,128,512]{2,1,0:T(8,128)(2,1)}, bf16[3,128,512]{2,1,0:T(8,128)(2,1)S(1)}, u32[]{:S(2)}, u32[]{:S(2)}) %collective-permute-start.1) | collective-permute-done | bytes 393248 | tf_op jit(solution)/shard_map/ppermute | solution.py:73
  18.9 1.4 %collective-permute-start.4 = (bf16[3,64,512]{2,1,0:T(8,128)(2,1)S(1)}, bf16[3,64,512]{2,1,0:T(8,128)(2,1)S(1)}, u32[]{:S(2)}, u32[]{:S(2)}) collective-permute-start(bf16[3,64,512]{2,1,0:T(8,128)(2,1)S(1)} %get-tuple-element.37), channel_id=1, source_target_pairs={{0,4},{1,9},{2,6},{3,11},{4,0},{5,13},{6,2},{7,15},{8,12},{9,1},{1... | collective-permute-start | bytes 589832 | tf_op jit(solution)/shard_map/ppermute | solution.py:73
  20.2 1.1 %collective-permute-done.3.odd_k = bf16[512,512]{1,0:T(8,128)(2,1)S(1)} collective-permute-done((bf16[512,512]{1,0:T(8,128)(2,1)}, bf16[512,512]{1,0:T(8,128)(2,1)S(1)}, u32[]{:S(2)}, u32[]{:S(2)}) %collective-permute-start.3) | collective-permute-done | bytes 524320 | tf_op jit(solution)/shard_map/ppermute | solution.py:89
  21.3 0.7 collective-permute-done.2.refs_2_
  22.0 1.8 %collective-permute-done.4.refs_3_ = bf16[3,64,512]{2,1,0:T(8,128)(2,1)S(1)} collective-permute-done((bf16[3,64,512]{2,1,0:T(8,128)(2,1)S(1)}, bf16[3,64,512]{2,1,0:T(8,128)(2,1)S(1)}, u32[]{:S(2)}, u32[]{:S(2)}) %collective-permute-start.4) | collective-permute-done | bytes 196640 | tf_op jit(solution)/shard_map/ppermute | solution.py:73
  23.9 1.3 %collective-permute-start.5 = (bf16[3,64,512]{2,1,0:T(8,128)(2,1)S(1)}, bf16[3,64,512]{2,1,0:T(8,128)(2,1)S(1)}, u32[]{:S(2)}, u32[]{:S(2)}) collective-permute-start(bf16[3,64,512]{2,1,0:T(8,128)(2,1)S(1)} %get-tuple-element.39), channel_id=1, source_target_pairs={{0,2},{1,3},{2,0},{3,1},{4,6},{5,7},{6,4},{7,5},{8,10},{9,11},{10,... | collective-permute-start | bytes 589832 | tf_op jit(solution)/shard_map/ppermute | solution.py:73
  25.2 3.3 %collective-permute-done.5 = bf16[3,64,512]{2,1,0:T(8,128)(2,1)S(1)} collective-permute-done((bf16[3,64,512]{2,1,0:T(8,128)(2,1)S(1)}, bf16[3,64,512]{2,1,0:T(8,128)(2,1)S(1)}, u32[]{:S(2)}, u32[]{:S(2)}) %collective-permute-start.5) | collective-permute-done | bytes 196640 | tf_op jit(solution)/shard_map/ppermute | solution.py:73
  28.6 0.7 collective-permute-start.11
  29.3 3.2 %collective-permute-start.12 = (bf16[512,512]{1,0:T(8,128)(2,1)S(1)}, bf16[512,512]{1,0:T(8,128)(2,1)S(1)}, u32[]{:S(2)}, u32[]{:S(2)}) collective-permute-start(bf16[512,512]{1,0:T(8,128)(2,1)S(1)} %collective-permute-done.3.odd_k), channel_id=1, source_target_pairs={{0,4},{4,8},{8,12},{12,16},{16,20},{20,24},{24,28},{1,5},{5,9},{9,... | collective-permute-start | bytes 1572872 | tf_op jit(solution)/shard_map/ppermute | solution.py:93
  32.5 1.6 %collective-permute-done.6 = bf16[3,64,512]{2,1,0:T(8,128)(2,1)S(1)} collective-permute-done((bf16[3,64,512]{2,1,0:T(8,128)(2,1)S(1)}, bf16[3,64,512]{2,1,0:T(8,128)(2,1)S(1)}, u32[]{:S(2)}, u32[]{:S(2)}) %collective-permute-start.6) | collective-permute-done | bytes 196640 | tf_op jit(solution)/shard_map/ppermute | solution.py:73
  34.2 1.3 %collective-permute-start.7 = (bf16[3,64,512]{2,1,0:T(8,128)(2,1)S(1)}, bf16[3,64,512]{2,1,0:T(8,128)(2,1)S(1)}, u32[]{:S(2)}, u32[]{:S(2)}) collective-permute-start(bf16[3,64,512]{2,1,0:T(8,128)(2,1)S(1)} %add_convert_fusion), channel_id=1, source_target_pairs={{0,2},{1,3},{2,0},{3,1},{4,6},{5,7},{6,4},{7,5},{8,10},{9,11},{10,... | collective-permute-start | bytes 589832 | tf_op jit(solution)/shard_map/ppermute | solution.py:73
  35.5 3.6 %collective-permute-done.7 = bf16[3,64,512]{2,1,0:T(8,128)(2,1)S(1)} collective-permute-done((bf16[3,64,512]{2,1,0:T(8,128)(2,1)S(1)}, bf16[3,64,512]{2,1,0:T(8,128)(2,1)S(1)}, u32[]{:S(2)}, u32[]{:S(2)}) %collective-permute-start.7) | collective-permute-done | bytes 196640 | tf_op jit(solution)/shard_map/ppermute | solution.py:73
  39.1 3.3 %collective-permute-start.10 = (bf16[3,64,512]{2,1,0:T(8,128)(2,1)S(1)}, bf16[3,64,512]{2,1,0:T(8,128)(2,1)}, u32[]{:S(2)}, u32[]{:S(2)}) collective-permute-start(bf16[3,64,512]{2,1,0:T(8,128)(2,1)S(1)} %pad_maximum_fusion.3), channel_id=1, source_target_pairs={{0,4},{1,9},{2,6},{3,11},{4,0},{5,13},{6,2},{7,15},{8,12},{9,1},{1... | collective-permute-start | bytes 589832 | tf_op jit(solution)/shard_map/ppermute | solution.py:73
  42.5 0.1 collective-permute-start.8
  42.6 7.1 %collective-permute-done.12.even_k = bf16[512,512]{1,0:T(8,128)(2,1)S(1)} collective-permute-done((bf16[512,512]{1,0:T(8,128)(2,1)S(1)}, bf16[512,512]{1,0:T(8,128)(2,1)S(1)}, u32[]{:S(2)}, u32[]{:S(2)}) %collective-permute-start.12) | collective-permute-done | bytes 524320 | tf_op jit(solution)/shard_map/ppermute | solution.py:93
  49.8 1.3 %collective-permute-start.14 = (bf16[512,512]{1,0:T(8,128)(2,1)S(1)}, bf16[512,512]{1,0:T(8,128)(2,1)S(1)}, u32[]{:S(2)}, u32[]{:S(2)}) collective-permute-start(bf16[512,512]{1,0:T(8,128)(2,1)S(1)} %broadcast_select_fusion), channel_id=1, source_target_pairs={{0,2},{4,6},{8,10},{12,14},{16,18},{20,22},{24,26},{28,30},{2,0},{... | collective-permute-start | bytes 1572872 | tf_op jit(solution)/shard_map/ppermute | solution.py:84
  51.1 2.8 %collective-permute-start.9 = (bf16[3,128,512]{2,1,0:T(8,128)(2,1)S(1)}, bf16[3,128,512]{2,1,0:T(8,128)(2,1)S(1)}, u32[]{:S(2)}, u32[]{:S(2)}) collective-permute-start(bf16[3,128,512]{2,1,0:T(8,128)(2,1)S(1)} %pad_maximum_fusion.refs_0_), channel_id=1, source_target_pairs={{0,8},{1,5},{2,10},{3,7},{4,12},{5,1},{6,14},{7,3},{8,0},{9,13},{1... | collective-permute-start | bytes 1179656 | tf_op jit(solution)/shard_map/ppermute | solution.py:73
  53.9 1.0 %pad_maximum_fusion.1.refs_2_ = bf16[3,128,512]{2,1,0:T(8,128)(2,1)S(1)} fusion(bf16[3,64,512]{2,1,0:T(8,128)(2,1)} %collective-permute-done.10, bf16[3,32,512]{2,1,0:T(8,128)(2,1)S(1)} %get-tuple-element.54, bf16[3,32,512]{2,1,0:T(8,128)(2,1)S(1)} %get-tuple-element.52), kind=kLoop, calls=%fused_computation.2 | loop fusion | flops 1179648 | bytes 786432 | tf_op jit(solution)/shard_map/concatenate | solution.py:374
  54.9 3.2 %collective-permute-done.14.prev_v = bf16[512,512]{1,0:T(8,128)(2,1)S(1)} collective-permute-done((bf16[512,512]{1,0:T(8,128)(2,1)S(1)}, bf16[512,512]{1,0:T(8,128)(2,1)S(1)}, u32[]{:S(2)}, u32[]{:S(2)}) %collective-permute-start.14) | collective-permute-done | bytes 524320 | tf_op jit(solution)/shard_map/ppermute | solution.py:84
  58.2 5.3 %window_attention.1 = (f32[768,512]{1,0:T(8,128)S(1)}, f32[3,8,512]{2,1,0:T(8,128)S(1)}) custom-call(bf16[768,512]{1,0:T(8,128)(2,1)S(1)} %copy-done, bf16[768,512]{1,0:T(8,128)(2,1)S(1)} %copy-done.6, bf16[768,512]{1,0:T(8,128)(2,1)S(1)} %copy-done.7, bf16[512,512]{1,0:T(8,128)(2,1)S(1)} %collective-permute-done.3.odd_k, ...), custom_call_target="tpu_custom_call" | custom-call | flops 1207959552 | bytes 3145728 | tf_op jit(solution)/shard_map/window_attention/pallas_call | solution.py:377
  63.5 2.0 %collective-permute-done.13.refs_3_ = bf16[3,128,512]{2,1,0:T(8,128)(2,1)S(1)} collective-permute-done((bf16[3,128,512]{2,1,0:T(8,128)(2,1)S(1)}, bf16[3,128,512]{2,1,0:T(8,128)(2,1)S(1)}, u32[]{:S(2)}, u32[]{:S(2)}) %collective-permute-start.13) | collective-permute-done | bytes 393248 | tf_op jit(solution)/shard_map/ppermute | solution.py:73
  65.5 2.7 %apply.1 = (f32[768,512]{1,0:T(8,128)S(1)}, f32[8,768]{1,0:T(8,128)S(1)}, bf16[32,512]{1,0:T(8,128)(2,1)}, bf16[32,512]{1,0:T(8,128)(2,1)}, bf16[32,512]{1,0:T(8,128)(2,1)}) custom-call(bf16[3,128,512]{2,1,0:T(8,128)(2,1)S(1)} %pad_maximum_fusion.refs_0_, bf16[3,128,512]{2,1,0:T(8,128)(2,1)S(1)} %collective-permute-done.9.refs_1_, ...), custom_call_target="tpu_custom_call" | custom-call | flops 1207959552 | bytes 4718592 | tf_op jit(solution)/shard_map/apply/pallas_call | solution.py:399
  68.3 6.0 %collective-permute-start.15 = (f32[8,768]{1,0:T(8,128)S(1)}, f32[8,768]{1,0:T(8,128)S(1)}, u32[]{:S(2)}, u32[]{:S(2)}) collective-permute-start(f32[8,768]{1,0:T(8,128)S(1)} %get-tuple-element.48.refs_0_), channel_id=1, source_target_pairs={{0,1},{1,0},{2,3},{3,2},{4,5},{5,4},{6,7},{7,6},{8,9},{9,8},{10,11... | collective-permute-start | bytes 73736 | tf_op jit(solution)/shard_map/ppermute | solution.py:423
  74.2 0.8 %collective-permute-done.15.refs_1_ = f32[8,768]{1,0:T(8,128)S(1)} collective-permute-done((f32[8,768]{1,0:T(8,128)S(1)}, f32[8,768]{1,0:T(8,128)S(1)}, u32[]{:S(2)}, u32[]{:S(2)}) %collective-permute-start.15) | collective-permute-done | bytes 24608 | tf_op jit(solution)/shard_map/ppermute | solution.py:423
  75.1 1.2 %norm.1 = bf16[768,512]{1,0:T(8,128)(2,1)} custom-call(f32[768,512]{1,0:T(8,128)S(1)} %get-tuple-element.47.combined_ref, f32[8,768]{1,0:T(8,128)S(1)} %get-tuple-element.48.refs_0_, f32[8,768]{1,0:T(8,128)S(1)} %collective-permute-done.15.refs_1_, f32[1,512]{1,0:T(1,128)S(1)} %bitcast.2), custom_call_target="tpu_custom_call" | custom-call | flops 1572864 | bytes 2359296 | tf_op jit(solution)/shard_map/norm/pallas_call | solution.py:426
  (36 shorter events, 0.6 us)
Async XLA Ops:
  7.4 11.4 %copy-start.4 = (f32[3,128,512]{2,1,0:T(8,128)S(1)}, f32[3,128,512]{2,1,0:T(8,128)}, u32[]{:S(2)}) copy-start(f32[3,128,512]{2,1,0:T(8,128)} %get-tuple-element.31.refs_0_) | copy-start | bytes 2359300
  7.4 7.2 %collective-permute-start = (bf16[3,128,512]{2,1,0:T(8,128)(2,1)}, bf16[3,128,512]{2,1,0:T(8,128)(2,1)S(1)}, u32[]{:S(2)}, u32[]{:S(2)}) collective-permute-start(bf16[3,128,512]{2,1,0:T(8,128)(2,1)} %get-tuple-element.29), channel_id=1, source_target_pairs={{0,8},{1,5},{2,10},{3,7},{4,12},{5,1},{6,14},{7,3},{8,0},{9,13},{1... | collective-permute-start | bytes 1179656 | tf_op jit(solution)/shard_map/ppermute | solution.py:73
  8.7 10.1 %collective-permute-start.1 = (bf16[3,128,512]{2,1,0:T(8,128)(2,1)}, bf16[3,128,512]{2,1,0:T(8,128)(2,1)S(1)}, u32[]{:S(2)}, u32[]{:S(2)}) collective-permute-start(bf16[3,128,512]{2,1,0:T(8,128)(2,1)} %get-tuple-element.32), channel_id=1, source_target_pairs={{0,8},{1,5},{2,10},{3,7},{4,12},{5,1},{6,14},{7,3},{8,0},{9,13},{1... | collective-permute-start | bytes 1179656 | tf_op jit(solution)/shard_map/ppermute | solution.py:73
  8.9 12.4 %collective-permute-start.3 = (bf16[512,512]{1,0:T(8,128)(2,1)}, bf16[512,512]{1,0:T(8,128)(2,1)S(1)}, u32[]{:S(2)}, u32[]{:S(2)}) collective-permute-start(bf16[512,512]{1,0:T(8,128)(2,1)} %get-tuple-element.35), channel_id=1, source_target_pairs={{0,2},{2,0},{4,6},{6,4},{8,10},{10,8},{12,14},{14,12},{16,18},{18,... | collective-permute-start | bytes 1572872 | tf_op jit(solution)/shard_map/ppermute | solution.py:89
  14.6 1.1 %copy-start.5 = (f32[3,128,512]{2,1,0:T(8,128)S(1)}, f32[3,128,512]{2,1,0:T(8,128)}, u32[]{:S(2)}) copy-start(f32[3,128,512]{2,1,0:T(8,128)} %get-tuple-element.28.refs_0_) | copy-start | bytes 2359300
  15.8 6.3 %collective-permute-start.2 = (bf16[3,64,512]{2,1,0:T(8,128)(2,1)S(1)}, bf16[3,64,512]{2,1,0:T(8,128)(2,1)S(1)}, u32[]{:S(2)}, u32[]{:S(2)}) collective-permute-start(bf16[3,64,512]{2,1,0:T(8,128)(2,1)S(1)} %get-tuple-element.34), channel_id=1, source_target_pairs={{0,4},{1,9},{2,6},{3,11},{4,0},{5,13},{6,2},{7,15},{8,12},{9,1},{1... | collective-permute-start | bytes 589832 | tf_op jit(solution)/shard_map/ppermute | solution.py:73
  18.8 9.8 %copy-start.9 = (bf16[512,512]{1,0:T(8,128)(2,1)S(1)}, bf16[512,512]{1,0:T(8,128)(2,1)}, u32[]{:S(2)}) copy-start(bf16[512,512]{1,0:T(8,128)(2,1)} %get-tuple-element.40) | copy-start | bytes 1572868
  18.9 5.0 %collective-permute-start.4 = (bf16[3,64,512]{2,1,0:T(8,128)(2,1)S(1)}, bf16[3,64,512]{2,1,0:T(8,128)(2,1)S(1)}, u32[]{:S(2)}, u32[]{:S(2)}) collective-permute-start(bf16[3,64,512]{2,1,0:T(8,128)(2,1)S(1)} %get-tuple-element.37), channel_id=1, source_target_pairs={{0,4},{1,9},{2,6},{3,11},{4,0},{5,13},{6,2},{7,15},{8,12},{9,1},{1... | collective-permute-start | bytes 589832 | tf_op jit(solution)/shard_map/ppermute | solution.py:73
  23.9 4.6 %collective-permute-start.5 = (bf16[3,64,512]{2,1,0:T(8,128)(2,1)S(1)}, bf16[3,64,512]{2,1,0:T(8,128)(2,1)S(1)}, u32[]{:S(2)}, u32[]{:S(2)}) collective-permute-start(bf16[3,64,512]{2,1,0:T(8,128)(2,1)S(1)} %get-tuple-element.39), channel_id=1, source_target_pairs={{0,2},{1,3},{2,0},{3,1},{4,6},{5,7},{6,4},{7,5},{8,10},{9,11},{10,... | collective-permute-start | bytes 589832 | tf_op jit(solution)/shard_map/ppermute | solution.py:73
  28.6 5.6 %collective-permute-start.6 = (bf16[3,64,512]{2,1,0:T(8,128)(2,1)S(1)}, bf16[3,64,512]{2,1,0:T(8,128)(2,1)S(1)}, u32[]{:S(2)}, u32[]{:S(2)}) collective-permute-start(bf16[3,64,512]{2,1,0:T(8,128)(2,1)S(1)} %add_convert_fusion.1), channel_id=1, source_target_pairs={{0,16},{1,17},{2,18},{3,19},{4,20},{5,21},{6,22},{7,23},{8,24},{9,... | collective-permute-start | bytes 589832 | tf_op jit(solution)/shard_map/ppermute | solution.py:73
  28.6 13.9 %collective-permute-start.11 = (bf16[512,512]{1,0:T(8,128)(2,1)S(1)}, bf16[512,512]{1,0:T(8,128)(2,1)S(1)}, u32[]{:S(2)}, u32[]{:S(2)}) collective-permute-start(bf16[512,512]{1,0:T(8,128)(2,1)S(1)} %copy-done.9), channel_id=1, source_target_pairs={{2,6},{6,10},{10,14},{14,18},{18,22},{22,26},{26,30},{3,7},{7,11},... | collective-permute-start | bytes 1572872 | tf_op jit(solution)/shard_map/ppermute | solution.py:77
  29.3 20.3 %collective-permute-start.12 = (bf16[512,512]{1,0:T(8,128)(2,1)S(1)}, bf16[512,512]{1,0:T(8,128)(2,1)S(1)}, u32[]{:S(2)}, u32[]{:S(2)}) collective-permute-start(bf16[512,512]{1,0:T(8,128)(2,1)S(1)} %collective-permute-done.3.odd_k), channel_id=1, source_target_pairs={{0,4},{4,8},{8,12},{12,16},{16,20},{20,24},{24,28},{1,5},{5,9},{9,... | collective-permute-start | bytes 1572872 | tf_op jit(solution)/shard_map/ppermute | solution.py:93
  34.2 4.9 %collective-permute-start.7 = (bf16[3,64,512]{2,1,0:T(8,128)(2,1)S(1)}, bf16[3,64,512]{2,1,0:T(8,128)(2,1)S(1)}, u32[]{:S(2)}, u32[]{:S(2)}) collective-permute-start(bf16[3,64,512]{2,1,0:T(8,128)(2,1)S(1)} %add_convert_fusion), channel_id=1, source_target_pairs={{0,2},{1,3},{2,0},{3,1},{4,6},{5,7},{6,4},{7,5},{8,10},{9,11},{10,... | collective-permute-start | bytes 589832 | tf_op jit(solution)/shard_map/ppermute | solution.py:73
  39.1 19.1 %copy-start.7 = (bf16[768,512]{1,0:T(8,128)(2,1)S(1)}, bf16[768,512]{1,0:T(8,128)(2,1)}, u32[]{:S(2)}) copy-start(bf16[768,512]{1,0:T(8,128)(2,1)} %v_ref.1) | copy-start | bytes 2359300
  39.1 10.6 %collective-permute-start.10 = (bf16[3,64,512]{2,1,0:T(8,128)(2,1)S(1)}, bf16[3,64,512]{2,1,0:T(8,128)(2,1)}, u32[]{:S(2)}, u32[]{:S(2)}) collective-permute-start(bf16[3,64,512]{2,1,0:T(8,128)(2,1)S(1)} %pad_maximum_fusion.3), channel_id=1, source_target_pairs={{0,4},{1,9},{2,6},{3,11},{4,0},{5,13},{6,2},{7,15},{8,12},{9,1},{1... | collective-permute-start | bytes 589832 | tf_op jit(solution)/shard_map/ppermute | solution.py:73
  42.4 15.8 %copy-start = (bf16[768,512]{1,0:T(8,128)(2,1)S(1)}, bf16[768,512]{1,0:T(8,128)(2,1)}, u32[]{:S(2)}) copy-start(bf16[768,512]{1,0:T(8,128)(2,1)} %refs_4_.3) | copy-start | bytes 2359300
  42.4 15.7 %copy-start.1 = (bf16[512,512]{1,0:T(8,128)(2,1)S(1)}, bf16[512,512]{1,0:T(8,128)(2,1)}, u32[]{:S(2)}) copy-start(bf16[512,512]{1,0:T(8,128)(2,1)} %refs_5_.1) | copy-start | bytes 1572868
  42.4 15.7 %copy-start.2 = (bf16[512,512]{1,0:T(8,128)(2,1)S(1)}, bf16[512,512]{1,0:T(8,128)(2,1)}, u32[]{:S(2)}) copy-start(bf16[512,512]{1,0:T(8,128)(2,1)} %refs_6_.1) | copy-start | bytes 1572868
  42.4 15.7 %copy-start.3 = (bf16[512,512]{1,0:T(8,128)(2,1)S(1)}, bf16[512,512]{1,0:T(8,128)(2,1)}, u32[]{:S(2)}) copy-start(bf16[512,512]{1,0:T(8,128)(2,1)} %refs_7_.1) | copy-start | bytes 1572868
  42.4 15.7 %copy-start.6 = (bf16[768,512]{1,0:T(8,128)(2,1)S(1)}, bf16[768,512]{1,0:T(8,128)(2,1)}, u32[]{:S(2)}) copy-start(bf16[768,512]{1,0:T(8,128)(2,1)} %k_ref.1) | copy-start | bytes 2359300
  42.5 8.6 %collective-permute-start.8 = (bf16[3,64,512]{2,1,0:T(8,128)(2,1)S(1)}, bf16[3,64,512]{2,1,0:T(8,128)(2,1)S(1)}, u32[]{:S(2)}, u32[]{:S(2)}) collective-permute-start(bf16[3,64,512]{2,1,0:T(8,128)(2,1)S(1)} %pad_maximum_fusion.2), channel_id=1, source_target_pairs={{0,4},{1,9},{2,6},{3,11},{4,0},{5,13},{6,2},{7,15},{8,12},{9,1},{1... | collective-permute-start | bytes 589832 | tf_op jit(solution)/shard_map/ppermute | solution.py:73
  49.8 8.4 %collective-permute-start.14 = (bf16[512,512]{1,0:T(8,128)(2,1)S(1)}, bf16[512,512]{1,0:T(8,128)(2,1)S(1)}, u32[]{:S(2)}, u32[]{:S(2)}) collective-permute-start(bf16[512,512]{1,0:T(8,128)(2,1)S(1)} %broadcast_select_fusion), channel_id=1, source_target_pairs={{0,2},{4,6},{8,10},{12,14},{16,18},{20,22},{24,26},{28,30},{2,0},{... | collective-permute-start | bytes 1572872 | tf_op jit(solution)/shard_map/ppermute | solution.py:84
  51.1 12.4 %collective-permute-start.9 = (bf16[3,128,512]{2,1,0:T(8,128)(2,1)S(1)}, bf16[3,128,512]{2,1,0:T(8,128)(2,1)S(1)}, u32[]{:S(2)}, u32[]{:S(2)}) collective-permute-start(bf16[3,128,512]{2,1,0:T(8,128)(2,1)S(1)} %pad_maximum_fusion.refs_0_), channel_id=1, source_target_pairs={{0,8},{1,5},{2,10},{3,7},{4,12},{5,1},{6,14},{7,3},{8,0},{9,13},{1... | collective-permute-start | bytes 1179656 | tf_op jit(solution)/shard_map/ppermute | solution.py:73
  54.9 10.7 %collective-permute-start.13 = (bf16[3,128,512]{2,1,0:T(8,128)(2,1)S(1)}, bf16[3,128,512]{2,1,0:T(8,128)(2,1)S(1)}, u32[]{:S(2)}, u32[]{:S(2)}) collective-permute-start(bf16[3,128,512]{2,1,0:T(8,128)(2,1)S(1)} %pad_maximum_fusion.1.refs_2_), channel_id=1, source_target_pairs={{0,8},{1,5},{2,10},{3,7},{4,12},{5,1},{6,14},{7,3},{8,0},{9,13},{1... | collective-permute-start | bytes 1179656 | tf_op jit(solution)/shard_map/ppermute | solution.py:73
  65.5 9.6 %copy-start.8 = (f32[512]{0:T(512)S(1)}, f32[512]{0:T(512)}, u32[]{:S(2)}) copy-start(f32[512]{0:T(512)} %param.15) | copy-start | bytes 6148
  68.3 6.8 %collective-permute-start.15 = (f32[8,768]{1,0:T(8,128)S(1)}, f32[8,768]{1,0:T(8,128)S(1)}, u32[]{:S(2)}, u32[]{:S(2)}) collective-permute-start(f32[8,768]{1,0:T(8,128)S(1)} %get-tuple-element.48.refs_0_), channel_id=1, source_target_pairs={{0,1},{1,0},{2,3},{3,2},{4,5},{5,4},{6,7},{7,6},{8,9},{9,8},{10,11... | collective-permute-start | bytes 73736 | tf_op jit(solution)/shard_map/ppermute | solution.py:423

commit v9 on v8

--- a/solution.py
+++ b/solution.py
@@ -368,9 +368,11 @@
         here = slice(c * rows, (c + 1) * rows)
         piece = jnp.concatenate([total[:, here], more[:, here]], axis=1)
         came = swap(piece, steps[1])
+        if c == 0:
+            came, passed = lax.optimization_barrier((came, passed))
+            prev_v = shift_passed(value_tail, passed)
         if c == 1:
-            came, passed, before_k = lax.optimization_barrier((came, passed, before_k))
-            prev_v = shift_passed(value_tail, passed)
+            came, before_k = lax.optimization_barrier((came, before_k))
         piece = jnp.concatenate([piece, came], axis=1)
         pieces += [piece, swap(piece, steps[0])]
 

time: 77.4 us -> 77.4 us (level)
  starting transfers between devices: 25.5 us -> 29.5 us
  waiting for transfers between devices: 31.4 us -> 27.5 us
    ppermute x1, waiting for transfers between devices: 7.13 us -> 0.01 us  [pass_on(): lax.ppermute(x, 'seq', [(i, i + 2) for i in range(0, lax.axis_size('seq')...]
    ppermute x1, starting transfers between devices: 1.27 us -> 5.23 us  [shift_passed(): return lax.ppermute(jnp.where(odd, passed, x), 'seq', pairs)]
    ppermute x11, waiting for transfers between devices: 19.2 us -> 22.6 us  [swap(): return lax.ppermute(x, ('seq', 'head'), pairs)]
where the time goes in v9:
time: 77.4 us; the launch traced here: 76.4 us
  starting transfers between devices  29.5 us (38%)
  waiting for transfers between devices  27.5 us (36%)
  Pallas kernels  16.1 us (21%)
  local copies, waits for them, and re-layouts  1.21 us (2%)
  other arithmetic  1.15 us (1%)
  between operations  1 us (1%)
    ppermute x11, waiting for transfers between devices, swap(): return lax.ppermute(x, ('seq', 'head'), pairs)  22.6 us
    ppermute x11, starting transfers between devices, swap(): return lax.ppermute(x, ('seq', 'head'), pairs)  13.2 us
    pallas_call x1, Pallas kernels, body(): pl.pallas_call(functools.partial(grads_kernel, steps[0]), out_shape=[jax....  6.75 us
    ppermute x1, starting transfers between devices, body(): sums = [sums, lax.ppermute(sums, 'head', [(0, 1), (1, 0)])]  5.97 us
    pallas_call x1, Pallas kernels, body(): pl.pallas_call(attend_kernel, out_shape=(jax.ShapeDtypeStruct((tok_rows,...  5.3 us
    ppermute x1, starting transfers between devices, shift_passed(): return lax.ppermute(jnp.where(odd, passed, x), 'seq', pairs)  5.23 us
    ppermute x1, starting transfers between devices, pass_on(): lax.ppermute(x, 'seq', [(i, i + 2) for i in range(0, lax.axis_size('seq')...  3.17 us
    ppermute x1, waiting for transfers between devices, shift_passed(): return lax.ppermute(jnp.where(odd, passed, x), 'seq', pairs)  2.95 us
  transfers between devices with their start and end apart: 16, of which 12 were waited for; matrix products, arithmetic and copies ran while one was open for 1% of the time, Pallas kernels for 7%

profile of v9, /device:TPU:17, one launch (start us, length us, event | category | flops | bytes accessed | tf_op | source)
XLA Modules:
  0.0 76.4 jit_solution(8658700417982872238)
XLA Ops:
  0.6 6.7 %gradients.1 = (bf16[512,512]{1,0:T(8,128)(2,1)}, bf16[512,512]{1,0:T(8,128)(2,1)}, bf16[3,128,512]{2,1,0:T(8,128)(2,1)}, bf16[3,128,512]{2,1,0:T(8,128)(2,1)}, ...) custom-call(bf16[768,512]{1,0:T(8,128)(2,1)} %k_ref.1, bf16[768,512]{1,0:T(8,128)(2,1)} %v_ref.1, ...), custom_call_target="tpu_custom_call" | custom-call | flops 2415919104 | bytes 6291456 | tf_op jit(solution)/shard_map/gradients/pallas_call | solution.py:318
  7.4 1.3 %collective-permute-start = (bf16[3,128,512]{2,1,0:T(8,128)(2,1)}, bf16[3,128,512]{2,1,0:T(8,128)(2,1)S(1)}, u32[]{:S(2)}, u32[]{:S(2)}) collective-permute-start(bf16[3,128,512]{2,1,0:T(8,128)(2,1)} %get-tuple-element.30), channel_id=1, source_target_pairs={{0,8},{1,5},{2,10},{3,7},{4,12},{5,1},{6,14},{7,3},{8,0},{9,13},{1... | collective-permute-start | bytes 1179656 | tf_op jit(solution)/shard_map/ppermute | solution.py:73
  8.7 0.2 collective-permute-start.1
  8.9 1.2 %collective-permute-start.3 = (bf16[512,512]{1,0:T(8,128)(2,1)}, bf16[512,512]{1,0:T(8,128)(2,1)S(1)}, u32[]{:S(2)}, u32[]{:S(2)}) collective-permute-start(bf16[512,512]{1,0:T(8,128)(2,1)} %get-tuple-element.36), channel_id=1, source_target_pairs={{0,2},{2,0},{4,6},{6,4},{8,10},{10,8},{12,14},{14,12},{16,18},{18,... | collective-permute-start | bytes 1572872 | tf_op jit(solution)/shard_map/ppermute | solution.py:89
  10.1 4.5 %collective-permute-done.refs_1_ = bf16[3,128,512]{2,1,0:T(8,128)(2,1)S(1)} collective-permute-done((bf16[3,128,512]{2,1,0:T(8,128)(2,1)}, bf16[3,128,512]{2,1,0:T(8,128)(2,1)S(1)}, u32[]{:S(2)}, u32[]{:S(2)}) %collective-permute-start) | collective-permute-done | bytes 393248 | tf_op jit(solution)/shard_map/ppermute | solution.py:73
  14.6 1.1 %copy-done.5 = f32[3,128,512]{2,1,0:T(8,128)S(1)} copy-done((f32[3,128,512]{2,1,0:T(8,128)S(1)}, f32[3,128,512]{2,1,0:T(8,128)}, u32[]{:S(2)}) %copy-start.5) | copy-done | bytes 786456
  15.8 1.4 %collective-permute-start.2 = (bf16[3,64,512]{2,1,0:T(8,128)(2,1)S(1)}, bf16[3,64,512]{2,1,0:T(8,128)(2,1)S(1)}, u32[]{:S(2)}, u32[]{:S(2)}) collective-permute-start(bf16[3,64,512]{2,1,0:T(8,128)(2,1)S(1)} %get-tuple-element.35), channel_id=1, source_target_pairs={{0,4},{1,9},{2,6},{3,11},{4,0},{5,13},{6,2},{7,15},{8,12},{9,1},{1... | collective-permute-start | bytes 589832 | tf_op jit(solution)/shard_map/ppermute | solution.py:73
  17.2 1.6 %collective-permute-done.1.refs_1_ = bf16[3,128,512]{2,1,0:T(8,128)(2,1)S(1)} collective-permute-done((bf16[3,128,512]{2,1,0:T(8,128)(2,1)}, bf16[3,128,512]{2,1,0:T(8,128)(2,1)S(1)}, u32[]{:S(2)}, u32[]{:S(2)}) %collective-permute-start.1) | collective-permute-done | bytes 393248 | tf_op jit(solution)/shard_map/ppermute | solution.py:73
  18.9 1.4 %collective-permute-start.4 = (bf16[3,64,512]{2,1,0:T(8,128)(2,1)S(1)}, bf16[3,64,512]{2,1,0:T(8,128)(2,1)S(1)}, u32[]{:S(2)}, u32[]{:S(2)}) collective-permute-start(bf16[3,64,512]{2,1,0:T(8,128)(2,1)S(1)} %get-tuple-element.38), channel_id=1, source_target_pairs={{0,4},{1,9},{2,6},{3,11},{4,0},{5,13},{6,2},{7,15},{8,12},{9,1},{1... | collective-permute-start | bytes 589832 | tf_op jit(solution)/shard_map/ppermute | solution.py:73
  20.2 1.1 %collective-permute-done.3.odd_k = bf16[512,512]{1,0:T(8,128)(2,1)S(1)} collective-permute-done((bf16[512,512]{1,0:T(8,128)(2,1)}, bf16[512,512]{1,0:T(8,128)(2,1)S(1)}, u32[]{:S(2)}, u32[]{:S(2)}) %collective-permute-start.3) | collective-permute-done | bytes 524320 | tf_op jit(solution)/shard_map/ppermute | solution.py:89
  21.3 0.7 collective-permute-done.2.refs_2_
  22.0 1.8 %collective-permute-done.4.refs_3_ = bf16[3,64,512]{2,1,0:T(8,128)(2,1)S(1)} collective-permute-done((bf16[3,64,512]{2,1,0:T(8,128)(2,1)S(1)}, bf16[3,64,512]{2,1,0:T(8,128)(2,1)S(1)}, u32[]{:S(2)}, u32[]{:S(2)}) %collective-permute-start.4) | collective-permute-done | bytes 196640 | tf_op jit(solution)/shard_map/ppermute | solution.py:73
  23.9 1.3 %collective-permute-start.5 = (bf16[3,64,512]{2,1,0:T(8,128)(2,1)S(1)}, bf16[3,64,512]{2,1,0:T(8,128)(2,1)S(1)}, u32[]{:S(2)}, u32[]{:S(2)}) collective-permute-start(bf16[3,64,512]{2,1,0:T(8,128)(2,1)S(1)} %get-tuple-element.40), channel_id=1, source_target_pairs={{0,2},{1,3},{2,0},{3,1},{4,6},{5,7},{6,4},{7,5},{8,10},{9,11},{10,... | collective-permute-start | bytes 589832 | tf_op jit(solution)/shard_map/ppermute | solution.py:73
  25.2 3.3 %collective-permute-done.5 = bf16[3,64,512]{2,1,0:T(8,128)(2,1)S(1)} collective-permute-done((bf16[3,64,512]{2,1,0:T(8,128)(2,1)S(1)}, bf16[3,64,512]{2,1,0:T(8,128)(2,1)S(1)}, u32[]{:S(2)}, u32[]{:S(2)}) %collective-permute-start.5) | collective-permute-done | bytes 196640 | tf_op jit(solution)/shard_map/ppermute | solution.py:73
  28.6 0.7 collective-permute-start.9
  29.3 3.2 %collective-permute-start.12 = (bf16[512,512]{1,0:T(8,128)(2,1)S(1)}, bf16[512,512]{1,0:T(8,128)(2,1)S(1)}, u32[]{:S(2)}, u32[]{:S(2)}) collective-permute-start(bf16[512,512]{1,0:T(8,128)(2,1)S(1)} %collective-permute-done.3.odd_k), channel_id=1, source_target_pairs={{0,4},{4,8},{8,12},{12,16},{16,20},{20,24},{24,28},{1,5},{5,9},{9,... | collective-permute-start | bytes 1572872 | tf_op jit(solution)/shard_map/ppermute | solution.py:93
  32.5 1.6 %collective-permute-done.6 = bf16[3,64,512]{2,1,0:T(8,128)(2,1)S(1)} collective-permute-done((bf16[3,64,512]{2,1,0:T(8,128)(2,1)S(1)}, bf16[3,64,512]{2,1,0:T(8,128)(2,1)S(1)}, u32[]{:S(2)}, u32[]{:S(2)}) %collective-permute-start.6) | collective-permute-done | bytes 196640 | tf_op jit(solution)/shard_map/ppermute | solution.py:73
  34.2 1.3 %collective-permute-start.7 = (bf16[3,64,512]{2,1,0:T(8,128)(2,1)S(1)}, bf16[3,64,512]{2,1,0:T(8,128)(2,1)S(1)}, u32[]{:S(2)}, u32[]{:S(2)}) collective-permute-start(bf16[3,64,512]{2,1,0:T(8,128)(2,1)S(1)} %add_convert_fusion), channel_id=1, source_target_pairs={{0,2},{1,3},{2,0},{3,1},{4,6},{5,7},{6,4},{7,5},{8,10},{9,11},{10,... | collective-permute-start | bytes 589832 | tf_op jit(solution)/shard_map/ppermute | solution.py:73
  35.5 3.6 %collective-permute-done.7 = bf16[3,64,512]{2,1,0:T(8,128)(2,1)S(1)} collective-permute-done((bf16[3,64,512]{2,1,0:T(8,128)(2,1)S(1)}, bf16[3,64,512]{2,1,0:T(8,128)(2,1)S(1)}, u32[]{:S(2)}, u32[]{:S(2)}) %collective-permute-start.7) | collective-permute-done | bytes 196640 | tf_op jit(solution)/shard_map/ppermute | solution.py:73
  39.1 3.3 %collective-permute-start.8 = (bf16[3,64,512]{2,1,0:T(8,128)(2,1)S(1)}, bf16[3,64,512]{2,1,0:T(8,128)(2,1)}, u32[]{:S(2)}, u32[]{:S(2)}) collective-permute-start(bf16[3,64,512]{2,1,0:T(8,128)(2,1)S(1)} %pad_maximum_fusion.2), channel_id=1, source_target_pairs={{0,4},{1,9},{2,6},{3,11},{4,0},{5,13},{6,2},{7,15},{8,12},{9,1},{1... | collective-permute-start | bytes 589832 | tf_op jit(solution)/shard_map/ppermute | solution.py:73
  42.5 0.1 collective-permute-start.11
  42.6 3.2 %collective-permute-done.8 = bf16[3,64,512]{2,1,0:T(8,128)(2,1)} collective-permute-done((bf16[3,64,512]{2,1,0:T(8,128)(2,1)S(1)}, bf16[3,64,512]{2,1,0:T(8,128)(2,1)}, u32[]{:S(2)}, u32[]{:S(2)}) %collective-permute-start.8) | collective-permute-done | bytes 196640 | tf_op jit(solution)/shard_map/ppermute | solution.py:73
  45.8 5.2 %collective-permute-start.14 = (bf16[512,512]{1,0:T(8,128)(2,1)S(1)}, bf16[512,512]{1,0:T(8,128)(2,1)S(1)}, u32[]{:S(2)}, u32[]{:S(2)}) collective-permute-start(bf16[512,512]{1,0:T(8,128)(2,1)S(1)} %broadcast_select_fusion), channel_id=1, source_target_pairs={{0,2},{4,6},{8,10},{12,14},{16,18},{20,22},{24,26},{28,30},{2,0},{... | collective-permute-start | bytes 1572872 | tf_op jit(solution)/shard_map/ppermute | solution.py:84
  51.1 2.8 %collective-permute-start.13 = (bf16[3,128,512]{2,1,0:T(8,128)(2,1)S(1)}, bf16[3,128,512]{2,1,0:T(8,128)(2,1)S(1)}, u32[]{:S(2)}, u32[]{:S(2)}) collective-permute-start(bf16[3,128,512]{2,1,0:T(8,128)(2,1)S(1)} %pad_maximum_fusion.1.refs_2_), channel_id=1, source_target_pairs={{0,8},{1,5},{2,10},{3,7},{4,12},{5,1},{6,14},{7,3},{8,0},{9,13},{1... | collective-permute-start | bytes 1179656 | tf_op jit(solution)/shard_map/ppermute | solution.py:73
  53.9 1.0 %pad_maximum_fusion.refs_0_ = bf16[3,128,512]{2,1,0:T(8,128)(2,1)S(1)} fusion(bf16[3,64,512]{2,1,0:T(8,128)(2,1)} %collective-permute-done.8, bf16[3,32,512]{2,1,0:T(8,128)(2,1)S(1)} %get-tuple-element.57, bf16[3,32,512]{2,1,0:T(8,128)(2,1)S(1)} %get-tuple-element.55), kind=kLoop, calls=%fused_computation.1 | loop fusion | flops 1179648 | bytes 786432 | tf_op jit(solution)/shard_map/concatenate | solution.py:376
  54.9 2.9 %collective-permute-done.14.prev_v = bf16[512,512]{1,0:T(8,128)(2,1)S(1)} collective-permute-done((bf16[512,512]{1,0:T(8,128)(2,1)S(1)}, bf16[512,512]{1,0:T(8,128)(2,1)S(1)}, u32[]{:S(2)}, u32[]{:S(2)}) %collective-permute-start.14) | collective-permute-done | bytes 524320 | tf_op jit(solution)/shard_map/ppermute | solution.py:84
  57.9 5.3 %window_attention.1 = (f32[768,512]{1,0:T(8,128)S(1)}, f32[3,8,512]{2,1,0:T(8,128)S(1)}) custom-call(bf16[768,512]{1,0:T(8,128)(2,1)S(1)} %copy-done, bf16[768,512]{1,0:T(8,128)(2,1)S(1)} %copy-done.6, bf16[768,512]{1,0:T(8,128)(2,1)S(1)} %copy-done.7, bf16[512,512]{1,0:T(8,128)(2,1)S(1)} %collective-permute-done.3.odd_k, ...), custom_call_target="tpu_custom_call" | custom-call | flops 1207959552 | bytes 3145728 | tf_op jit(solution)/shard_map/window_attention/pallas_call | solution.py:379
  63.2 2.3 %collective-permute-done.10.refs_1_ = bf16[3,128,512]{2,1,0:T(8,128)(2,1)S(1)} collective-permute-done((bf16[3,128,512]{2,1,0:T(8,128)(2,1)S(1)}, bf16[3,128,512]{2,1,0:T(8,128)(2,1)S(1)}, u32[]{:S(2)}, u32[]{:S(2)}) %collective-permute-start.10) | collective-permute-done | bytes 393248 | tf_op jit(solution)/shard_map/ppermute | solution.py:73
  65.5 2.7 %apply.1 = (f32[768,512]{1,0:T(8,128)S(1)}, f32[8,768]{1,0:T(8,128)S(1)}, bf16[32,512]{1,0:T(8,128)(2,1)}, bf16[32,512]{1,0:T(8,128)(2,1)}, bf16[32,512]{1,0:T(8,128)(2,1)}) custom-call(bf16[3,128,512]{2,1,0:T(8,128)(2,1)S(1)} %pad_maximum_fusion.refs_0_, bf16[3,128,512]{2,1,0:T(8,128)(2,1)S(1)} %collective-permute-done.10.refs_1_, ...), custom_call_target="tpu_custom_call" | custom-call | flops 1207959552 | bytes 4718592 | tf_op jit(solution)/shard_map/apply/pallas_call | solution.py:401
  68.3 6.0 %collective-permute-start.15 = (f32[8,768]{1,0:T(8,128)S(1)}, f32[8,768]{1,0:T(8,128)S(1)}, u32[]{:S(2)}, u32[]{:S(2)}) collective-permute-start(f32[8,768]{1,0:T(8,128)S(1)} %get-tuple-element.50.refs_0_), channel_id=1, source_target_pairs={{0,1},{1,0},{2,3},{3,2},{4,5},{5,4},{6,7},{7,6},{8,9},{9,8},{10,11... | collective-permute-start | bytes 73736 | tf_op jit(solution)/shard_map/ppermute | solution.py:425
  74.2 0.8 %collective-permute-done.15.refs_1_ = f32[8,768]{1,0:T(8,128)S(1)} collective-permute-done((f32[8,768]{1,0:T(8,128)S(1)}, f32[8,768]{1,0:T(8,128)S(1)}, u32[]{:S(2)}, u32[]{:S(2)}) %collective-permute-start.15) | collective-permute-done | bytes 24608 | tf_op jit(solution)/shard_map/ppermute | solution.py:425
  75.1 1.2 %norm.1 = bf16[768,512]{1,0:T(8,128)(2,1)} custom-call(f32[768,512]{1,0:T(8,128)S(1)} %get-tuple-element.49.combined_ref, f32[8,768]{1,0:T(8,128)S(1)} %get-tuple-element.50.refs_0_, f32[8,768]{1,0:T(8,128)S(1)} %collective-permute-done.15.refs_1_, f32[1,512]{1,0:T(1,128)S(1)} %bitcast.2), custom_call_target="tpu_custom_call" | custom-call | flops 1572864 | bytes 2359296 | tf_op jit(solution)/shard_map/norm/pallas_call | solution.py:428
  (36 shorter events, 0.6 us)
Async XLA Ops:
  7.4 11.4 %copy-start.4 = (f32[3,128,512]{2,1,0:T(8,128)S(1)}, f32[3,128,512]{2,1,0:T(8,128)}, u32[]{:S(2)}) copy-start(f32[3,128,512]{2,1,0:T(8,128)} %get-tuple-element.32.refs_0_) | copy-start | bytes 2359300
  7.4 7.2 %collective-permute-start = (bf16[3,128,512]{2,1,0:T(8,128)(2,1)}, bf16[3,128,512]{2,1,0:T(8,128)(2,1)S(1)}, u32[]{:S(2)}, u32[]{:S(2)}) collective-permute-start(bf16[3,128,512]{2,1,0:T(8,128)(2,1)} %get-tuple-element.30), channel_id=1, source_target_pairs={{0,8},{1,5},{2,10},{3,7},{4,12},{5,1},{6,14},{7,3},{8,0},{9,13},{1... | collective-permute-start | bytes 1179656 | tf_op jit(solution)/shard_map/ppermute | solution.py:73
  8.7 10.1 %collective-permute-start.1 = (bf16[3,128,512]{2,1,0:T(8,128)(2,1)}, bf16[3,128,512]{2,1,0:T(8,128)(2,1)S(1)}, u32[]{:S(2)}, u32[]{:S(2)}) collective-permute-start(bf16[3,128,512]{2,1,0:T(8,128)(2,1)} %get-tuple-element.33), channel_id=1, source_target_pairs={{0,8},{1,5},{2,10},{3,7},{4,12},{5,1},{6,14},{7,3},{8,0},{9,13},{1... | collective-permute-start | bytes 1179656 | tf_op jit(solution)/shard_map/ppermute | solution.py:73
  8.9 12.4 %collective-permute-start.3 = (bf16[512,512]{1,0:T(8,128)(2,1)}, bf16[512,512]{1,0:T(8,128)(2,1)S(1)}, u32[]{:S(2)}, u32[]{:S(2)}) collective-permute-start(bf16[512,512]{1,0:T(8,128)(2,1)} %get-tuple-element.36), channel_id=1, source_target_pairs={{0,2},{2,0},{4,6},{6,4},{8,10},{10,8},{12,14},{14,12},{16,18},{18,... | collective-permute-start | bytes 1572872 | tf_op jit(solution)/shard_map/ppermute | solution.py:89
  14.6 1.1 %copy-start.5 = (f32[3,128,512]{2,1,0:T(8,128)S(1)}, f32[3,128,512]{2,1,0:T(8,128)}, u32[]{:S(2)}) copy-start(f32[3,128,512]{2,1,0:T(8,128)} %get-tuple-element.29.refs_0_) | copy-start | bytes 2359300
  15.8 6.3 %collective-permute-start.2 = (bf16[3,64,512]{2,1,0:T(8,128)(2,1)S(1)}, bf16[3,64,512]{2,1,0:T(8,128)(2,1)S(1)}, u32[]{:S(2)}, u32[]{:S(2)}) collective-permute-start(bf16[3,64,512]{2,1,0:T(8,128)(2,1)S(1)} %get-tuple-element.35), channel_id=1, source_target_pairs={{0,4},{1,9},{2,6},{3,11},{4,0},{5,13},{6,2},{7,15},{8,12},{9,1},{1... | collective-permute-start | bytes 589832 | tf_op jit(solution)/shard_map/ppermute | solution.py:73
  18.8 9.8 %copy-start.9 = (bf16[512,512]{1,0:T(8,128)(2,1)S(1)}, bf16[512,512]{1,0:T(8,128)(2,1)}, u32[]{:S(2)}) copy-start(bf16[512,512]{1,0:T(8,128)(2,1)} %get-tuple-element.41) | copy-start | bytes 1572868
  18.9 5.0 %collective-permute-start.4 = (bf16[3,64,512]{2,1,0:T(8,128)(2,1)S(1)}, bf16[3,64,512]{2,1,0:T(8,128)(2,1)S(1)}, u32[]{:S(2)}, u32[]{:S(2)}) collective-permute-start(bf16[3,64,512]{2,1,0:T(8,128)(2,1)S(1)} %get-tuple-element.38), channel_id=1, source_target_pairs={{0,4},{1,9},{2,6},{3,11},{4,0},{5,13},{6,2},{7,15},{8,12},{9,1},{1... | collective-permute-start | bytes 589832 | tf_op jit(solution)/shard_map/ppermute | solution.py:73
  23.9 4.6 %collective-permute-start.5 = (bf16[3,64,512]{2,1,0:T(8,128)(2,1)S(1)}, bf16[3,64,512]{2,1,0:T(8,128)(2,1)S(1)}, u32[]{:S(2)}, u32[]{:S(2)}) collective-permute-start(bf16[3,64,512]{2,1,0:T(8,128)(2,1)S(1)} %get-tuple-element.40), channel_id=1, source_target_pairs={{0,2},{1,3},{2,0},{3,1},{4,6},{5,7},{6,4},{7,5},{8,10},{9,11},{10,... | collective-permute-start | bytes 589832 | tf_op jit(solution)/shard_map/ppermute | solution.py:73
  28.6 5.6 %collective-permute-start.6 = (bf16[3,64,512]{2,1,0:T(8,128)(2,1)S(1)}, bf16[3,64,512]{2,1,0:T(8,128)(2,1)S(1)}, u32[]{:S(2)}, u32[]{:S(2)}) collective-permute-start(bf16[3,64,512]{2,1,0:T(8,128)(2,1)S(1)} %add_convert_fusion.1), channel_id=1, source_target_pairs={{0,16},{1,17},{2,18},{3,19},{4,20},{5,21},{6,22},{7,23},{8,24},{9,... | collective-permute-start | bytes 589832 | tf_op jit(solution)/shard_map/ppermute | solution.py:73
  28.6 13.9 %collective-permute-start.9 = (bf16[512,512]{1,0:T(8,128)(2,1)S(1)}, bf16[512,512]{1,0:T(8,128)(2,1)S(1)}, u32[]{:S(2)}, u32[]{:S(2)}) collective-permute-start(bf16[512,512]{1,0:T(8,128)(2,1)S(1)} %copy-done.9), channel_id=1, source_target_pairs={{2,6},{6,10},{10,14},{14,18},{18,22},{22,26},{26,30},{3,7},{7,11},... | collective-permute-start | bytes 1572872 | tf_op jit(solution)/shard_map/ppermute | solution.py:77
  29.3 21.7 %collective-permute-start.12 = (bf16[512,512]{1,0:T(8,128)(2,1)S(1)}, bf16[512,512]{1,0:T(8,128)(2,1)S(1)}, u32[]{:S(2)}, u32[]{:S(2)}) collective-permute-start(bf16[512,512]{1,0:T(8,128)(2,1)S(1)} %collective-permute-done.3.odd_k), channel_id=1, source_target_pairs={{0,4},{4,8},{8,12},{12,16},{16,20},{20,24},{24,28},{1,5},{5,9},{9,... | collective-permute-start | bytes 1572872 | tf_op jit(solution)/shard_map/ppermute | solution.py:93
  34.2 4.9 %collective-permute-start.7 = (bf16[3,64,512]{2,1,0:T(8,128)(2,1)S(1)}, bf16[3,64,512]{2,1,0:T(8,128)(2,1)S(1)}, u32[]{:S(2)}, u32[]{:S(2)}) collective-permute-start(bf16[3,64,512]{2,1,0:T(8,128)(2,1)S(1)} %add_convert_fusion), channel_id=1, source_target_pairs={{0,2},{1,3},{2,0},{3,1},{4,6},{5,7},{6,4},{7,5},{8,10},{9,11},{10,... | collective-permute-start | bytes 589832 | tf_op jit(solution)/shard_map/ppermute | solution.py:73
  39.1 18.8 %copy-start.7 = (bf16[768,512]{1,0:T(8,128)(2,1)S(1)}, bf16[768,512]{1,0:T(8,128)(2,1)}, u32[]{:S(2)}) copy-start(bf16[768,512]{1,0:T(8,128)(2,1)} %v_ref.1) | copy-start | bytes 2359300
  39.1 6.6 %collective-permute-start.8 = (bf16[3,64,512]{2,1,0:T(8,128)(2,1)S(1)}, bf16[3,64,512]{2,1,0:T(8,128)(2,1)}, u32[]{:S(2)}, u32[]{:S(2)}) collective-permute-start(bf16[3,64,512]{2,1,0:T(8,128)(2,1)S(1)} %pad_maximum_fusion.2), channel_id=1, source_target_pairs={{0,4},{1,9},{2,6},{3,11},{4,0},{5,13},{6,2},{7,15},{8,12},{9,1},{1... | collective-permute-start | bytes 589832 | tf_op jit(solution)/shard_map/ppermute | solution.py:73
  42.4 15.5 %copy-start = (bf16[768,512]{1,0:T(8,128)(2,1)S(1)}, bf16[768,512]{1,0:T(8,128)(2,1)}, u32[]{:S(2)}) copy-start(bf16[768,512]{1,0:T(8,128)(2,1)} %refs_4_.3) | copy-start | bytes 2359300
  42.4 15.5 %copy-start.1 = (bf16[512,512]{1,0:T(8,128)(2,1)S(1)}, bf16[512,512]{1,0:T(8,128)(2,1)}, u32[]{:S(2)}) copy-start(bf16[512,512]{1,0:T(8,128)(2,1)} %refs_5_.1) | copy-start | bytes 1572868
  42.4 15.5 %copy-start.2 = (bf16[512,512]{1,0:T(8,128)(2,1)S(1)}, bf16[512,512]{1,0:T(8,128)(2,1)}, u32[]{:S(2)}) copy-start(bf16[512,512]{1,0:T(8,128)(2,1)} %refs_6_.1) | copy-start | bytes 1572868
  42.4 15.5 %copy-start.3 = (bf16[512,512]{1,0:T(8,128)(2,1)S(1)}, bf16[512,512]{1,0:T(8,128)(2,1)}, u32[]{:S(2)}) copy-start(bf16[512,512]{1,0:T(8,128)(2,1)} %refs_7_.1) | copy-start | bytes 1572868
  42.4 15.5 %copy-start.6 = (bf16[768,512]{1,0:T(8,128)(2,1)S(1)}, bf16[768,512]{1,0:T(8,128)(2,1)}, u32[]{:S(2)}) copy-start(bf16[768,512]{1,0:T(8,128)(2,1)} %k_ref.1) | copy-start | bytes 2359300
  42.5 8.6 %collective-permute-start.11 = (bf16[3,64,512]{2,1,0:T(8,128)(2,1)S(1)}, bf16[3,64,512]{2,1,0:T(8,128)(2,1)S(1)}, u32[]{:S(2)}, u32[]{:S(2)}) collective-permute-start(bf16[3,64,512]{2,1,0:T(8,128)(2,1)S(1)} %pad_maximum_fusion.3), channel_id=1, source_target_pairs={{0,4},{1,9},{2,6},{3,11},{4,0},{5,13},{6,2},{7,15},{8,12},{9,1},{1... | collective-permute-start | bytes 589832 | tf_op jit(solution)/shard_map/ppermute | solution.py:73
  45.8 12.1 %collective-permute-start.14 = (bf16[512,512]{1,0:T(8,128)(2,1)S(1)}, bf16[512,512]{1,0:T(8,128)(2,1)S(1)}, u32[]{:S(2)}, u32[]{:S(2)}) collective-permute-start(bf16[512,512]{1,0:T(8,128)(2,1)S(1)} %broadcast_select_fusion), channel_id=1, source_target_pairs={{0,2},{4,6},{8,10},{12,14},{16,18},{20,22},{24,26},{28,30},{2,0},{... | collective-permute-start | bytes 1572872 | tf_op jit(solution)/shard_map/ppermute | solution.py:84
  51.1 12.2 %collective-permute-start.13 = (bf16[3,128,512]{2,1,0:T(8,128)(2,1)S(1)}, bf16[3,128,512]{2,1,0:T(8,128)(2,1)S(1)}, u32[]{:S(2)}, u32[]{:S(2)}) collective-permute-start(bf16[3,128,512]{2,1,0:T(8,128)(2,1)S(1)} %pad_maximum_fusion.1.refs_2_), channel_id=1, source_target_pairs={{0,8},{1,5},{2,10},{3,7},{4,12},{5,1},{6,14},{7,3},{8,0},{9,13},{1... | collective-permute-start | bytes 1179656 | tf_op jit(solution)/shard_map/ppermute | solution.py:73
  54.9 10.7 %collective-permute-start.10 = (bf16[3,128,512]{2,1,0:T(8,128)(2,1)S(1)}, bf16[3,128,512]{2,1,0:T(8,128)(2,1)S(1)}, u32[]{:S(2)}, u32[]{:S(2)}) collective-permute-start(bf16[3,128,512]{2,1,0:T(8,128)(2,1)S(1)} %pad_maximum_fusion.refs_0_), channel_id=1, source_target_pairs={{0,8},{1,5},{2,10},{3,7},{4,12},{5,1},{6,14},{7,3},{8,0},{9,13},{1... | collective-permute-start | bytes 1179656 | tf_op jit(solution)/shard_map/ppermute | solution.py:73
  65.5 9.6 %copy-start.8 = (f32[512]{0:T(512)S(1)}, f32[512]{0:T(512)}, u32[]{:S(2)}) copy-start(f32[512]{0:T(512)} %param.15) | copy-start | bytes 6148
  68.3 6.8 %collective-permute-start.15 = (f32[8,768]{1,0:T(8,128)S(1)}, f32[8,768]{1,0:T(8,128)S(1)}, u32[]{:S(2)}, u32[]{:S(2)}) collective-permute-start(f32[8,768]{1,0:T(8,128)S(1)} %get-tuple-element.50.refs_0_), channel_id=1, source_target_pairs={{0,1},{1,0},{2,3},{3,2},{4,5},{5,4},{6,7},{7,6},{8,9},{9,8},{10,11... | collective-permute-start | bytes 73736 | tf_op jit(solution)/shard_map/ppermute | solution.py:425
